TPU v7x, 32 devices: a whole 2x2x4 slice. The times are simulated.
32 devices in a mesh: seq: 8 (over z, y), tensor: 2 (over core), dp: 2 (over x).
Axes of the slice: x: 2, y: 2, z: 4, core: 2. Of those that a mesh axis runs over, the one named last changes fastest.
Arguments:
- inputs: bfloat16 [2, 6144, 1536], P('dp', 'seq', 'tensor'), may hold values from -6 to 6
- lengths: int32 [2], P('dp'), may hold values from 1536 to 6144, as said below
- cotangent: bfloat16 [2, 6144, 1536], P('dp', 'seq', 'tensor'), may hold values from -6 to 6
- w_value: bfloat16 [1536, 1536], P(None, 'tensor'), may hold values from -0.15625 to 0.15625
- w_gate: bfloat16 [1536, 1536], P(None, 'tensor'), may hold values from -0.15625 to 0.15625
- kernel: bfloat16 [31, 1536], P(None, 'tensor'), may hold values from -1 to 1
- w_out: bfloat16 [1536, 1536], P('tensor'), may hold values from -0.15625 to 0.15625
Outputs:
- output: bfloat16 [2, 6144, 1536], P('dp', 'seq', 'tensor')
- input_gradient: bfloat16 [2, 6144, 1536], P('dp', 'seq', 'tensor')
- value_grad: float32 [1536, 1536], P(('seq', 'dp'), 'tensor')
- gate_grad: float32 [1536, 1536], P(('seq', 'dp'), 'tensor')
- kernel_grad: float32 [31, 1536], P(None, 'tensor')
- out_grad: float32 [1536, 1536], P('tensor', ('seq', 'dp'))
Inputs may be any that keep to these rules, and one draw needn't show every extreme that they name: `lengths`: in every draw some utterance has all 6144 frames valid.
All inputs are finite; a program needn't handle non-finite values.
Results may differ from a plain program's by a relative error of at most 0.009.
Values may be sent and summed in bfloat16 or wider, within the bound.
No kernel may reach another device: no remote copies, remote signals or barrier semaphores. Data moves between devices by JAX's collectives and lax.ppermute only.
A program may use at most 128 MiB of HBM per device.

v0:
```python
import jax
import jax.numpy as jnp
from jax import lax
from jax.sharding import PartitionSpec as P

epsilon = 1e-05


def padded_2(shard, sides, width):
    for axis, dim in sides:
        peers, length = (lax.axis_size(axis), shard.shape[dim])
        up = [(i, (i + 1) % peers) for i in range(peers - 1)]
        down = [(j, i) for i, j in up]
        last = lax.slice_in_dim(shard, length - width, length, axis=dim)
        leading = lax.slice_in_dim(shard, 0, width, axis=dim)
        before = lax.ppermute(last, axis, up)
        after = lax.ppermute(leading, axis, down)
        shard = jnp.concatenate([before, shard, after], axis=dim)
    return shard


def layer_normalizer(values):
    center = values - jnp.mean(values, axis=-1, keepdims=True)
    inverse = lax.rsqrt(jnp.mean(center * center, axis=-1, keepdims=True) + epsilon)
    return (center * inverse, inverse)


def shards(inputs, lengths, cotangent, w_value, w_gate, kernel, w_out):
    frame_total = inputs[0]
    count = frame_total.shape[0]
    channel_total = frame_total.shape[1]
    channel_width = channel_total * lax.axis_size("tensor")
    taps_count = kernel.shape[0]
    half = (taps_count - 1) // 2
    tensor_position = lax.axis_index("tensor")
    first_frame = lax.axis_index("seq") * count
    positions = first_frame + jnp.arange(count, dtype=jnp.int32)
    valid = (positions < lengths[0]).astype(jnp.float32)[:, None]
    taps = kernel.astype(jnp.float32)
    complete_rows = lax.all_gather(frame_total, "tensor", axis=1, tiled=True)
    centered_scaled, inverse_deviation_one = layer_normalizer(complete_rows.astype(jnp.float32))
    normalized_rows = centered_scaled.astype(jnp.bfloat16)
    values = jnp.dot(normalized_rows, w_value, preferred_element_type=jnp.float32)
    gates = jnp.dot(normalized_rows, w_gate, preferred_element_type=jnp.float32)
    sigma = jax.nn.sigmoid(gates)
    hidden = (values * sigma * valid).astype(jnp.bfloat16)
    padded = padded_2(hidden, (("seq", 0),), half).astype(jnp.float32)
    conv = jnp.zeros((count, channel_total), jnp.float32)
    for offset in range(taps_count):
        conv = conv + padded[offset : offset + count] * taps[offset]
    conv_sum, conv_square = lax.psum(
        (jnp.sum(conv, axis=-1), jnp.sum(conv * conv, axis=-1)), "tensor"
    )
    conv_mean = (conv_sum / channel_width)[:, None]
    conv_var = (conv_square / channel_width)[:, None] - conv_mean * conv_mean
    rstd_two = lax.rsqrt(conv_var + epsilon)
    zhat = (conv - conv_mean) * rstd_two
    swish_gate = jax.nn.sigmoid(zhat)
    swished = (zhat * swish_gate).astype(jnp.bfloat16)
    partial_out = jnp.dot(swished, w_out, preferred_element_type=jnp.float32)
    summed = lax.psum_scatter(
        partial_out.astype(jnp.bfloat16), "tensor", scatter_dimension=1, tiled=True
    ).astype(jnp.float32)
    output = (frame_total.astype(jnp.float32) + summed).astype(jnp.bfloat16)
    upstream = cotangent[0]
    upstream_whole = lax.all_gather(upstream, "tensor", axis=1, tiled=True)
    out_term = jnp.dot(swished.T, upstream_whole, preferred_element_type=jnp.float32)
    dswish = jnp.dot(upstream_whole, w_out.T, preferred_element_type=jnp.float32)
    dswish = dswish * (swish_gate + zhat * swish_gate * (1.0 - swish_gate))
    slope_sum, slope_cross = lax.psum(
        (jnp.sum(dswish, axis=-1), jnp.sum(dswish * zhat, axis=-1)), "tensor"
    )
    dconv = rstd_two * (
        dswish
        - (slope_sum / channel_width)[:, None]
        - zhat * (slope_cross / channel_width)[:, None]
    )
    dconv = dconv.astype(jnp.bfloat16)
    slope = dconv.astype(jnp.float32)
    kernel_term = jnp.stack(
        [jnp.sum(padded[offset : offset + count] * slope, axis=0) for offset in range(taps_count)]
    )
    slope_pad = padded_2(dconv, (("seq", 0),), half).astype(jnp.float32)
    dhidden = jnp.zeros((count, channel_total), jnp.float32)
    for offset in range(taps_count):
        dhidden = dhidden + slope_pad[2 * half - offset : 2 * half - offset + count] * taps[offset]
    dhidden = dhidden * valid
    dvalues = (dhidden * sigma).astype(jnp.bfloat16)
    dgates = (dhidden * values * sigma * (1.0 - sigma)).astype(jnp.bfloat16)
    value_term = jnp.dot(normalized_rows.T, dvalues, preferred_element_type=jnp.float32)
    gate_term = jnp.dot(normalized_rows.T, dgates, preferred_element_type=jnp.float32)
    kernel_grad = lax.psum(kernel_term, ("seq", "dp"))
    dnormed_part = jnp.dot(dvalues, w_value.T, preferred_element_type=jnp.float32) + jnp.dot(
        dgates, w_gate.T, preferred_element_type=jnp.float32
    )
    normalized_grad = lax.psum_scatter(
        dnormed_part.astype(jnp.bfloat16), "tensor", scatter_dimension=1, tiled=True
    ).astype(jnp.float32)
    local_centered_scaled = lax.dynamic_slice_in_dim(
        centered_scaled, tensor_position * channel_total, channel_total, 1
    )
    input_total_sum, input_cross_term = lax.psum(
        (
            jnp.sum(normalized_grad, axis=-1),
            jnp.sum(normalized_grad * local_centered_scaled, axis=-1),
        ),
        "tensor",
    )
    input_gradient = upstream.astype(jnp.float32) + inverse_deviation_one * (
        normalized_grad
        - (input_total_sum / channel_width)[:, None]
        - local_centered_scaled * (input_cross_term / channel_width)[:, None]
    )
    input_gradient = input_gradient.astype(jnp.bfloat16)
    value_grad, gate_grad, out_grad = (
        lax.psum_scatter(value_term, ("seq", "dp"), scatter_dimension=0, tiled=True),
        lax.psum_scatter(gate_term, ("seq", "dp"), scatter_dimension=0, tiled=True),
        lax.psum_scatter(out_term, ("seq", "dp"), scatter_dimension=1, tiled=True),
    )
    return (output[None], input_gradient[None], value_grad, gate_grad, kernel_grad, out_grad)


def solution(mesh):
    return jax.shard_map(
        shards,
        mesh=mesh,
        in_specs=(
            P("dp", "seq", "tensor"),
            P("dp"),
            P("dp", "seq", "tensor"),
            P(None, "tensor"),
            P(None, "tensor"),
            P(None, "tensor"),
            P("tensor", None),
        ),
        out_specs=(
            P("dp", "seq", "tensor"),
            P("dp", "seq", "tensor"),
            P(("seq", "dp"), "tensor"),
            P(("seq", "dp"), "tensor"),
            P(None, "tensor"),
            P("tensor", ("seq", "dp")),
        ),
        check_vma=False,
    )
```

profile of v0, /device:TPU:0, one launch (start us, length us, event | category | flops | bytes accessed | tf_op | source)
XLA Modules:
  0.0 680.9 jit_solution(15295582354793908402)
XLA Ops:
  9.7 13.5 %all-gather.5.cloned.1.call-done = bf16[1,768,1536]{2,1,0:T(8,128)(2,1)} async-done(((bf16[1,768,768]{2,1,0:T(8,128)(2,1)}), bf16[1,768,1536]{2,1,0:T(8,128)(2,1)}) %all-gather.5.cloned.1.call-update) | async-done | bytes 2359312 | tf_op jit(solution)/shard_map/all_gather | solution.py:40
  28.8 3.5 multiply_convert_fusion.3
  32.3 3.6 collective-permute-start
  37.5 4.2 collective-permute-done.1
  42.1 10.7 %fusion.94 = (f32[768]{0:T(1024)S(1)}, f32[768]{0:T(1024)S(1)}, f32[768,768]{1,0:T(8,128)}) fusion(f32[768]{0:T(1024)S(1)} %get-tuple-element.44, f32[798,768]{1,0:T(8,128)S(1)} %maximum_convert_fusion, f32[768]{0:T(1024)S(1)} %get-tuple-element.45, f32[768]{0:T(1024)S(1)} %get-tuple-element.46, f32[768]{0:T(1024)S(1)} %get-tuple-element.47, ...), kind=kLoop, calls=%fused_computation.209 | loop fusion | flops 37747200 | bytes 75598848 | tf_op jit(solution)/shard_map/reduce_sum | solution.py:52
  55.5 7.0 %fusion.93 = (f32[768]{0:T(1024)S(1)}, f32[768]{0:T(1024)S(1)}, f32[768,768]{1,0:T(8,128)}) fusion(f32[768]{0:T(1024)S(1)} %get-tuple-element.89, f32[768,768]{1,0:T(8,128)} %get-tuple-element.83, f32[768]{0:T(1024)S(1)} %get-tuple-element.88, bf16[768,1536]{1,0:T(8,128)(2,1)} %param.13, bf16[1,768,1536]{2,1,0:T(8,128)(2,1)} %all-gather.7.cloned.1.call-done), kind=kOutput, calls=%fused_computation.208 | convolution fusion | flops 1819605504 | bytes 9449472 | tf_op jit(solution)/shard_map/dot_general | solution.py:68
  65.0 27.0 %fusion.39 = (f32[768]{0:T(1024)}, f32[768]{0:T(1024)}, f32[768]{0:T(1024)}, f32[768]{0:T(1024)}, f32[768]{0:T(1024)}, /*index=5*/f32[768]{0:T(1024)}, f32[768]{...) fusion(f32[798,768]{1,0:T(8,128)} %copy-done.1, ...), kind=kLoop, calls=%fused_computation.77 | loop fusion | flops 25938432 | bytes 48433152 | tf_op jit(solution)/shard_map/reduce_sum | solution.py:81
  92.7 4.9 collective-permute-start.2
  98.9 3.9 convolution_convert_fusion
  104.9 10.9 %multiply_convert_fusion = (bf16[768,768]{1,0:T(8,128)(2,1)S(1)}, f32[768,768]{1,0:T(8,128)S(1)}) fusion(f32[768,768]{1,0:T(8,128)S(1)} %copy-done.5, f32[768,768]{1,0:T(8,128)} %get-tuple-element.91, f32[768]{0:T(1024)S(1)} %copy-done.72, f32[768]{0:T(1024)S(1)} %get-tuple-element.44, f32[798,768]{1,0:T(8,128)S(1)} %maximum_convert_fusion.1, ...), kind=kLoop, calls=%fused_computation.146 | loop fusion | flops 39518208 | bytes 81494016 | tf_op jit(solution)/shard_map/convert_element_type | solution.py:89
  118.4 3.5 add_convert_fusion
  122.4 15.4 %fusion.38 = (f32[768]{0:T(1024)S(1)}, f32[768]{0:T(1024)S(1)}, f32[768]{0:T(1024)S(1)}, f32[768]{0:T(1024)S(1)}, f32[768]{0:T(1024)S(1)}, /*index=5*/f32[768]{0...) fusion(bf16[768,768]{1,0:T(8,128)(2,1)S(1)} %get-tuple-element., ...), kind=kLoop, calls=%fused_computation.76 | loop fusion | flops 15915264 | bytes 31890432 | tf_op jit(solution)/shard_map/reduce_sum | solution.py:81
  138.4 2.6 stack.127
  141.1 6.8 %fusion.72 = f32[768,1536]{0,1:T(8,128)} fusion(bf16[1,768,1536]{2,1,0:T(8,128)(2,1)} %all-gather.7.cloned.1.call-done, f32[768,768]{1,0:T(8,128)} %get-tuple-element.83, f32[768]{0:T(1024)} %copy-done.93, f32[768]{0:T(1024)} %copy-done.91), kind=kOutput, calls=%fused_computation.142 | convolution fusion | flops 1816068096 | bytes 9443328 | tf_op jit(solution)/shard_map/dot_general | solution.py:67
  149.2 6.1 fusion.88
  156.5 6.1 fusion.86
  162.7 4.5 fusion.1
  169.7 2.6 convert_reduce_fusion.1
  172.3 3.1 all-reduce
  176.1 3.6 fusion.81
  179.8 65.0 %all-reduce.5.cloned.1.call-done = f32[31,768]{1,0:T(8,128)} async-done(((f32[31,768]{1,0:T(8,128)}), f32[31,768]{1,0:T(8,128)}) %all-reduce.5.cloned.1.call-update) | async-done | bytes 95248 | tf_op jit(solution)/shard_map/psum | solution.py:92
  244.8 142.9 %reduce-scatter.14.cloned.1.call-done = f32[768,96]{0,1:T(8,128)} async-done(((f32[768,1536]{0,1:T(8,128)}), f32[768,96]{0,1:T(8,128)}) %reduce-scatter.14.cloned.1.call-update) | async-done | bytes 294928 | tf_op jit(solution)/shard_map/reduce_scatter | solution.py:118
  387.7 142.8 %reduce-scatter.10.cloned.1.call-done = f32[96,768]{1,0:T(8,128)} async-done(((f32[1536,768]{1,0:T(8,128)}), f32[96,768]{1,0:T(8,128)}) %reduce-scatter.10.cloned.1.call-update) | async-done | bytes 294928 | tf_op jit(solution)/shard_map/reduce_scatter | solution.py:116
  530.5 142.0 %reduce-scatter.12.cloned.1.call-done = f32[96,768]{1,0:T(8,128)} async-done(((f32[1536,768]{1,0:T(8,128)}), f32[96,768]{1,0:T(8,128)}) %reduce-scatter.12.cloned.1.call-update) | async-done | bytes 294928 | tf_op jit(solution)/shard_map/reduce_scatter | solution.py:117
  (274 shorter events, 27.9 us)
Async XLA Ops:
  7.2 16.1 %all-gather.5.cloned.1.call-start = ((), (), s32[]{:S(2)}) async-start(), calls=%async_computation.11 | async-start | bytes 3538944 | tf_op jit(solution)/shard_map/all_gather | solution.py:40
  7.9 47.6 %all-gather.7.cloned.1.call-start = ((), (), s32[]{:S(2)}) async-start(), calls=%async_computation.12 | async-start | bytes 3538944 | tf_op jit(solution)/shard_map/all_gather | solution.py:66
  8.7 158.5 %reduce-scatter.6.cloned.1.call-start = ((), (), s32[]{:S(2)}) async-start(), calls=%async_computation.5 | async-start | bytes 3538944 | tf_op jit(solution)/shard_map/reduce_scatter | solution.py:61
  9.6 32.4 %copy-start.13 = (f32[768]{0:T(1024)}, f32[768]{0:T(1024)S(1)}, u32[]{:S(2)}) copy-start(f32[768]{0:T(1024)S(1)} %get-tuple-element.47) | copy-start | bytes 9220
  9.6 32.4 %copy-start.15 = (f32[768]{0:T(1024)}, f32[768]{0:T(1024)S(1)}, u32[]{:S(2)}) copy-start(f32[768]{0:T(1024)S(1)} %get-tuple-element.48) | copy-start | bytes 9220
  9.6 32.4 %copy-start.17 = (f32[768]{0:T(1024)}, f32[768]{0:T(1024)S(1)}, u32[]{:S(2)}) copy-start(f32[768]{0:T(1024)S(1)} %get-tuple-element.49) | copy-start | bytes 9220
  9.6 32.4 %copy-start.19 = (f32[768]{0:T(1024)}, f32[768]{0:T(1024)S(1)}, u32[]{:S(2)}) copy-start(f32[768]{0:T(1024)S(1)} %get-tuple-element.50) | copy-start | bytes 9220
  9.6 32.4 %copy-start.21 = (f32[768]{0:T(1024)}, f32[768]{0:T(1024)S(1)}, u32[]{:S(2)}) copy-start(f32[768]{0:T(1024)S(1)} %get-tuple-element.51) | copy-start | bytes 9220
  9.6 32.4 %copy-start.23 = (f32[768]{0:T(1024)}, f32[768]{0:T(1024)S(1)}, u32[]{:S(2)}) copy-start(f32[768]{0:T(1024)S(1)} %get-tuple-element.52) | copy-start | bytes 9220
  9.6 32.4 %copy-start.25 = (f32[768]{0:T(1024)}, f32[768]{0:T(1024)S(1)}, u32[]{:S(2)}) copy-start(f32[768]{0:T(1024)S(1)} %get-tuple-element.53) | copy-start | bytes 9220
  9.6 32.4 %copy-start.27 = (f32[768]{0:T(1024)}, f32[768]{0:T(1024)S(1)}, u32[]{:S(2)}) copy-start(f32[768]{0:T(1024)S(1)} %get-tuple-element.54) | copy-start | bytes 9220
  32.3 5.2 collective-permute-start
  36.0 5.7 collective-permute-start.1
  65.0 33.8 %copy-start.3 = (f32[768,768]{1,0:T(8,128)S(1)}, f32[768,768]{1,0:T(8,128)}, u32[]{:S(2)}) copy-start(f32[768,768]{1,0:T(8,128)} %get-tuple-element.83) | copy-start | bytes 7077892
  65.0 33.8 %copy-start.92 = (f32[768]{0:T(1024)S(1)}, f32[768]{0:T(1024)}, u32[]{:S(2)}) copy-start(f32[768]{0:T(1024)} %copy-done.91) | copy-start | bytes 9220
  65.0 33.8 %copy-start.94 = (f32[768]{0:T(1024)S(1)}, f32[768]{0:T(1024)}, u32[]{:S(2)}) copy-start(f32[768]{0:T(1024)} %copy-done.93) | copy-start | bytes 9220
  65.0 33.8 %copy-start.95 = (bf16[768,1536]{1,0:T(8,128)(2,1)S(1)}, bf16[768,1536]{1,0:T(8,128)(2,1)}, u32[]{:S(2)}) copy-start(bf16[768,1536]{1,0:T(8,128)(2,1)} %param.13) | copy-start | bytes 7077892
  92.7 10.4 %collective-permute-start.2 = (bf16[15,768]{1,0:T(8,128)(2,1)}, bf16[15,768]{1,0:T(8,128)(2,1)}, u32[]{:S(2)}, u32[]{:S(2)}) collective-permute-start(bf16[15,768]{1,0:T(8,128)(2,1)} %get-tuple-element.84), channel_id=1, source_target_pairs={{0,4},{4,8},{8,12},{12,16},{16,20},{20,24},{24,28},{1,5},{5,9},{9,... | collective-permute-start | bytes 69128 | tf_op jit(solution)/shard_map/ppermute | solution.py:16
  97.5 6.0 collective-permute-start.3
  102.8 67.0 %reduce-scatter.8.cloned.1.call-start = ((), (), s32[]{:S(2)}) async-start(), calls=%async_computation.6 | async-start | bytes 3538944 | tf_op jit(solution)/shard_map/reduce_scatter | solution.py:96
  122.0 122.8 %all-reduce.5.cloned.1.call-start = ((), (), s32[]{:S(2)}) async-start(), calls=%async_computation.9 | async-start | bytes 196608 | tf_op jit(solution)/shard_map/psum | solution.py:92
  141.0 246.7 %reduce-scatter.14.cloned.1.call-start = ((), (), s32[]{:S(2)}) async-start(), calls=%async_computation.10 | async-start | bytes 5013504 | tf_op jit(solution)/shard_map/reduce_scatter | solution.py:118
  147.9 382.6 %reduce-scatter.10.cloned.1.call-start = ((), (), s32[]{:S(2)}) async-start(), calls=%async_computation.7 | async-start | bytes 5013504 | tf_op jit(solution)/shard_map/reduce_scatter | solution.py:116
  155.3 517.2 %reduce-scatter.12.cloned.1.call-start = ((), (), s32[]{:S(2)}) async-start(), calls=%async_computation.8 | async-start | bytes 5013504 | tf_op jit(solution)/shard_map/reduce_scatter | solution.py:117
  (86 other events, 857.1 us)
Sparse Core Ops, SparseCore 0:
  9.6 13.6 all-gather.4
  24.8 12.1 all-gather.6
  102.9 10.4 reduce-scatter.5
  122.1 10.3 reduce-scatter.7
  141.1 103.5 all-reduce.4
  250.4 137.2 reduce-scatter.13
  394.3 136.2 reduce-scatter.9
  536.2 136.2 reduce-scatter.11
where the time goes:
time: 681 us
  waiting for transfers between devices  512 us (75%)
  other arithmetic  82.8 us (12%)
  matrix products  41.3 us (6%)
  between operations  16.6 us (2%)
  starting transfers between devices  11.6 us (2%)
  local copies, waits for them, and re-layouts  8.19 us (1%)
  blocking collectives  8.05 us (1%)
    reduce_scatter x1, waiting for transfers between devices, shards(): lax.psum_scatter(out_term, ('seq', 'dp'), scatter_dimension=1, tiled=True)  143 us
    reduce_scatter x1, waiting for transfers between devices, shards(): lax.psum_scatter(value_term, ('seq', 'dp'), scatter_dimension=0, tiled=True)  143 us
    reduce_scatter x1, waiting for transfers between devices, shards(): lax.psum_scatter(gate_term, ('seq', 'dp'), scatter_dimension=0, tiled=True)  142 us
    psum x1, waiting for transfers between devices, shards(): kernel_grad = lax.psum(kernel_term, ('seq', 'dp'))  65 us
    reduce_sum x2, other arithmetic, shards(): jnp.sum(padded[offset:offset + count] * slope, axis=0)  42.5 us
  transfers between devices with their start and end apart: 12, of which 7 were waited for; matrix products, arithmetic and copies ran while one was open for 14% of the time, Pallas kernels for 0%

commit v1 on v0

v1 whole, which is shorter than its diff:
```python
import jax
import jax.numpy as jnp
from jax import lax
from jax.sharding import PartitionSpec as P

epsilon = 1e-05


def swap(value, axis, bit=0):
    size = lax.axis_size(axis)
    return lax.ppermute(value, axis, [(i, i ^ (1 << bit)) for i in range(size)])


def bits_of(axis):
    return [(axis, b) for b in range(lax.axis_size(axis).bit_length() - 1)]


def pair_sum(value):
    return value + swap(value, "tensor")


def both_halves(own, other, dim):
    first = lax.axis_index("tensor") == 0
    return jnp.where(
        first,
        jnp.concatenate([own, other], axis=dim),
        jnp.concatenate([other, own], axis=dim),
    )


def padded_2(shard, width):
    peers, length = (lax.axis_size("seq"), shard.shape[0])
    up = [(i, (i + 1) % peers) for i in range(peers - 1)]
    down = [(j, i) for i, j in up]
    before = lax.ppermute(shard[length - width :], "seq", up)
    after = lax.ppermute(shard[:width], "seq", down)
    return jnp.concatenate([before, shard, after], axis=0)


def layer_normalizer(values):
    center = values - jnp.mean(values, axis=-1, keepdims=True)
    inverse = lax.rsqrt(jnp.mean(center * center, axis=-1, keepdims=True) + epsilon)
    return (center * inverse, inverse)


class Halver:
    def __init__(self, terms):
        self.bits = bits_of("seq")[::-1] + bits_of("dp")[::-1]
        blocks = 1 << len(self.bits)
        rows = terms.shape[0] // blocks
        self.value = terms.reshape((2,) * len(self.bits) + (rows, terms.shape[1]))

    def step(self, bit):
        dim = self.bits.index(bit)
        mine = (lax.axis_index(bit[0]) >> bit[1]) & 1
        send = lax.dynamic_index_in_dim(self.value, 1 - mine, dim, keepdims=False)
        keep = lax.dynamic_index_in_dim(self.value, mine, dim, keepdims=False)
        shape = send.shape
        got = swap(send.reshape(-1, shape[-1]), *bit).reshape(shape)
        self.value = keep.astype(jnp.float32) + got.astype(jnp.float32)
        self.bits = self.bits[:dim] + self.bits[dim + 1 :]
        if self.bits:
            self.value = self.value.astype(jnp.bfloat16)


def scatter_sum(terms):
    thirds = [Halver(t) for t in jnp.split(terms, 3, axis=1)]
    every = bits_of("dp") + bits_of("seq")
    turning, rest = every[:3], every[3:]
    for phase in range(len(turning)):
        for i, third in enumerate(thirds):
            third.step(turning[(i + phase) % len(turning)])
    merged = thirds[0]
    merged.value = jnp.concatenate([t.value for t in thirds], axis=-1)
    for bit in rest:
        merged.step(bit)
    return merged.value


def shards(inputs, lengths, cotangent, w_value, w_gate, kernel, w_out):
    frame_total = inputs[0]
    count = frame_total.shape[0]
    channel_total = frame_total.shape[1]
    channel_width = channel_total * lax.axis_size("tensor")
    taps_count = kernel.shape[0]
    half = (taps_count - 1) // 2
    tensor_position = lax.axis_index("tensor")
    first_frame = lax.axis_index("seq") * count
    positions = first_frame + jnp.arange(count, dtype=jnp.int32)
    valid = (positions < lengths[0]).astype(jnp.float32)[:, None]
    taps = kernel.astype(jnp.float32)
    upstream = cotangent[0]
    complete_rows = both_halves(frame_total, swap(frame_total, "tensor"), 1)
    upstream_whole = both_halves(upstream, swap(upstream, "tensor"), 1)
    centered_scaled, inverse_deviation_one = layer_normalizer(complete_rows.astype(jnp.float32))
    normalized_rows = centered_scaled.astype(jnp.bfloat16)
    values = jnp.dot(normalized_rows, w_value, preferred_element_type=jnp.float32)
    gates = jnp.dot(normalized_rows, w_gate, preferred_element_type=jnp.float32)
    sigma = jax.nn.sigmoid(gates)
    hidden = (values * sigma * valid).astype(jnp.bfloat16)
    padded = padded_2(hidden, half).astype(jnp.float32)
    conv = jnp.zeros((count, channel_total), jnp.float32)
    for offset in range(taps_count):
        conv = conv + padded[offset : offset + count] * taps[offset]
    conv_sums = pair_sum(jnp.stack([jnp.sum(conv, axis=-1), jnp.sum(conv * conv, axis=-1)]))
    conv_mean = (conv_sums[0] / channel_width)[:, None]
    conv_var = (conv_sums[1] / channel_width)[:, None] - conv_mean * conv_mean
    rstd_two = lax.rsqrt(conv_var + epsilon)
    zhat = (conv - conv_mean) * rstd_two
    swish_gate = jax.nn.sigmoid(zhat)
    swished = (zhat * swish_gate).astype(jnp.bfloat16)
    out_term = jnp.dot(upstream_whole.T, swished, preferred_element_type=jnp.float32)
    out_grad = scatter_sum(out_term.astype(jnp.bfloat16)).T
    partial_out = jnp.dot(swished, w_out, preferred_element_type=jnp.float32).astype(jnp.bfloat16)

    def pair_scatter(partial):
        mine = lax.dynamic_slice_in_dim(
            partial, tensor_position * channel_total, channel_total, 1
        )
        theirs = lax.dynamic_slice_in_dim(
            partial, (1 - tensor_position) * channel_total, channel_total, 1
        )
        return mine.astype(jnp.float32) + swap(theirs, "tensor").astype(jnp.float32)

    output = (frame_total.astype(jnp.float32) + pair_scatter(partial_out)).astype(jnp.bfloat16)
    dswish = jnp.dot(upstream_whole, w_out.T, preferred_element_type=jnp.float32)
    dswish = dswish * (swish_gate + zhat * swish_gate * (1.0 - swish_gate))
    slopes = pair_sum(jnp.stack([jnp.sum(dswish, axis=-1), jnp.sum(dswish * zhat, axis=-1)]))
    dconv = rstd_two * (
        dswish
        - (slopes[0] / channel_width)[:, None]
        - zhat * (slopes[1] / channel_width)[:, None]
    )
    dconv = dconv.astype(jnp.bfloat16)
    slope = dconv.astype(jnp.float32)
    slope_pad = padded_2(dconv, half).astype(jnp.float32)
    dhidden = jnp.zeros((count, channel_total), jnp.float32)
    for offset in range(taps_count):
        dhidden = dhidden + slope_pad[2 * half - offset : 2 * half - offset + count] * taps[offset]
    dhidden = dhidden * valid
    dvalues = (dhidden * sigma).astype(jnp.bfloat16)
    dgates = (dhidden * values * sigma * (1.0 - sigma)).astype(jnp.bfloat16)
    value_term = jnp.dot(normalized_rows.T, dvalues, preferred_element_type=jnp.float32)
    gate_term = jnp.dot(normalized_rows.T, dgates, preferred_element_type=jnp.float32)
    grads = scatter_sum(
        jnp.concatenate(
            [
                t[:, c : c + channel_total // 3]
                for c in range(0, channel_total, channel_total // 3)
                for t in (value_term.astype(jnp.bfloat16), gate_term.astype(jnp.bfloat16))
            ],
            axis=1,
        )
    )
    width = channel_total // 3
    value_grad = jnp.concatenate([grads[:, i * width : (i + 1) * width] for i in (0, 2, 4)], axis=1)
    gate_grad = jnp.concatenate([grads[:, i * width : (i + 1) * width] for i in (1, 3, 5)], axis=1)
    kernel_grad = jnp.stack(
        [jnp.sum(padded[offset : offset + count] * slope, axis=0) for offset in range(taps_count)]
    )
    for bit in bits_of("dp") + bits_of("seq"):
        kernel_grad = kernel_grad + swap(kernel_grad, *bit)
    dnormed_part = jnp.dot(dvalues, w_value.T, preferred_element_type=jnp.float32) + jnp.dot(
        dgates, w_gate.T, preferred_element_type=jnp.float32
    )
    normalized_grad = pair_scatter(dnormed_part.astype(jnp.bfloat16))
    local_centered_scaled = lax.dynamic_slice_in_dim(
        centered_scaled, tensor_position * channel_total, channel_total, 1
    )
    input_sums = pair_sum(
        jnp.stack(
            [
                jnp.sum(normalized_grad, axis=-1),
                jnp.sum(normalized_grad * local_centered_scaled, axis=-1),
            ]
        )
    )
    input_gradient = upstream.astype(jnp.float32) + inverse_deviation_one * (
        normalized_grad
        - (input_sums[0] / channel_width)[:, None]
        - local_centered_scaled * (input_sums[1] / channel_width)[:, None]
    )
    input_gradient = input_gradient.astype(jnp.bfloat16)
    return (output[None], input_gradient[None], value_grad, gate_grad, kernel_grad, out_grad)


def solution(mesh):
    return jax.shard_map(
        shards,
        mesh=mesh,
        in_specs=(
            P("dp", "seq", "tensor"),
            P("dp"),
            P("dp", "seq", "tensor"),
            P(None, "tensor"),
            P(None, "tensor"),
            P(None, "tensor"),
            P("tensor", None),
        ),
        out_specs=(
            P("dp", "seq", "tensor"),
            P("dp", "seq", "tensor"),
            P(("seq", "dp"), "tensor"),
            P(("seq", "dp"), "tensor"),
            P(None, "tensor"),
            P("tensor", ("seq", "dp")),
        ),
        check_vma=False,
    )
```

time: 681 us -> 274 us (0.40)
  waiting for transfers between devices: 512 us -> 73.4 us
  local copies, waits for them, and re-layouts: 8.19 us -> 46 us
  starting transfers between devices: 11.6 us -> 47.2 us
  other arithmetic: 82.8 us -> 66.3 us
  between operations: 16.6 us -> 3.36 us
  matrix products: 41.3 us -> 32.7 us
  blocking collectives: 8.05 us -> 0 us
    reduce_scatter x5 -> x0, waiting for transfers between devices: 428 us -> none  [the longest x1 143 us: shards(): lax.psum_scatter(out_term, ('seq', 'dp'), scatter_dimension=1, tiled=True)]
    ppermute x4 -> x35, waiting for transfers between devices: 4.62 us -> 73.4 us  [the longest x31 70.7 us: swap(): return lax.ppermute(value, axis, [(i, i ^ 1 << bit) for i in range(size)])]
    psum x1 -> x0, waiting for transfers between devices: 65 us -> none  [shards(): kernel_grad = lax.psum(kernel_term, ('seq', 'dp'))]
    ppermute x4 -> x35, starting transfers between devices: 11.1 us -> 47.2 us  [the longest x31 36.7 us: swap(): return lax.ppermute(value, axis, [(i, i ^ 1 << bit) for i in range(size)])]
    reduce_sum x2, other arithmetic: 42.5 us -> 10.6 us  [shards(): jnp.sum(padded[offset:offset + count] * slope, axis=0)]
    another operation x32, local copies, waits for them, and re-layouts: 2.72 us -> 23.6 us  [shards(): jnp.stack([jnp.sum(padded[offset:offset + count] * slope, axis=0) for off...]
    all_gather x2 -> x0, waiting for transfers between devices: 13.5 us -> none  [the longest x1 13.5 us: shards(): complete_rows = lax.all_gather(frame_total, 'tensor', axis=1, tiled=True)]
    convert_element_type x2 -> x21, other arithmetic: 1.32 us -> 10.9 us  [the longest x18 4.8 us: step(): self.value = self.value.astype(jnp.bfloat16)]
  transfers between devices with their start and end apart: 12 -> 35, of which waited for: 7 -> 17; matrix products, arithmetic and copies ran while one was open for 14% -> 49% of each run, Pallas kernels for 0% -> 0%
where the time goes in v1:
time: 274 us; the launch traced here: 269 us
  waiting for transfers between devices  73.4 us (27%)
  other arithmetic  66.3 us (24%)
  starting transfers between devices  47.2 us (17%)
  local copies, waits for them, and re-layouts  46 us (17%)
  matrix products  32.7 us (12%)
  between operations  3.36 us (1%)
    ppermute x31, waiting for transfers between devices, swap(): return lax.ppermute(value, axis, [(i, i ^ 1 << bit) for i in range(size)])  70.7 us
    ppermute x31, starting transfers between devices, swap(): return lax.ppermute(value, axis, [(i, i ^ 1 << bit) for i in range(size)])  36.7 us
    another operation x32, local copies, waits for them, and re-layouts, shards(): jnp.stack([jnp.sum(padded[offset:offset + count] * slope, axis=0) for off...  23.6 us
    convert_element_type x1, other arithmetic, shards(): dgates = (dhidden * values * sigma * (1.0 - sigma)).astype(jnp.bfloat16)  10.9 us
    reduce_sum x1, other arithmetic, shards(): jnp.sum(conv, axis=-1)  10.7 us
    reduce_sum x2, other arithmetic, shards(): jnp.sum(padded[offset:offset + count] * slope, axis=0)  10.6 us
    concatenate x3, local copies, waits for them, and re-layouts, shards(): jnp.concatenate([t[:, c:c + channel_total // 3] for c in range(0, channel...  8.02 us
    ppermute x2, starting transfers between devices, padded_2(): before = lax.ppermute(shard[length - width:], 'seq', up)  7.35 us
  transfers between devices with their start and end apart: 35, of which 17 were waited for; matrix products, arithmetic and copies ran while one was open for 49% of the time, Pallas kernels for 0%

profile of v1, /device:TPU:0, one launch (start us, length us, event | category | flops | bytes accessed | tf_op | source)
XLA Modules:
  0.0 269.1 jit_solution(10524592836402750067)
XLA Ops:
  4.9 3.0 %convert_reduce_fusion = f32[768]{0:T(1024)S(1)} fusion(bf16[768,768]{1,0:T(8,128)(2,1)} %bitcast.163, bf16[768,768]{1,0:T(8,128)(2,1)} %collective-permute-done, pred[]{:T(512)S(6)} %eq.4), kind=kLoop, calls=%fused_computation.32 | loop fusion | flops 12975360 | bytes 2362369 | tf_op jit(solution)/shard_map/reduce_sum | solution.py:41
  8.0 2.9 %fusion.2 = f32[768]{0:T(1024)S(1)} fusion(f32[768]{0:T(1024)S(1)} %broadcast_multiply_fusion, bf16[768,768]{1,0:T(8,128)(2,1)S(1)} %bitcast.164, bf16[768,768]{1,0:T(8,128)(2,1)} %collective-permute-done, pred[]{:T(512)S(6)} %eq.4), kind=kLoop, calls=%fused_computation.35 | loop fusion | flops 15334656 | bytes 2365441 | tf_op jit(solution)/shard_map/reduce_sum | solution.py:42
  11.0 4.3 %fusion.106 = (bf16[768,1536]{1,0:T(8,128)(2,1)S(1)}, f32[768,1536]{1,0:T(8,128)}) fusion(f32[768]{0:T(1024)S(1)} %add_rsqrt_fusion.1, f32[768]{0:T(1024)S(1)} %broadcast_multiply_fusion, bf16[768,768]{1,0:T(8,128)(2,1)S(1)} %bitcast.165, bf16[768,768]{1,0:T(8,128)(2,1)} %collective-permute-done, pred[]{:T(512)S(6)} %eq.4), kind=kLoop, calls=%fused_computation.292 | loop fusion | flops 15335424 | bytes 9443329 | tf_op jit(solution)/shard_map/convert_element_type | solution.py:96
  17.5 3.4 %multiply_convert_fusion.3 = (bf16[768,768]{1,0:T(8,128)(2,1)S(1)}, f32[768,768]{1,0:T(8,128)}) fusion(f32[768,768]{1,0:T(8,128)S(1)} %add_divide_fusion.1, f32[768]{0:T(1024)S(1)} %fusion.89, bf16[768,1536]{1,0:T(8,128)(2,1)S(1)} %get-tuple-element.84, bf16[1536,768]{1,0:T(8,128)(2,1)S(1)} %copy-done), kind=kOutput, calls=%fused_computation.149 | convolution fusion | flops 1813708800 | bytes 10619904 | tf_op jit(solution)/shard_map/dot_general | solution.py:97
  21.0 4.8 %collective-permute-start.1 = (bf16[15,768]{1,0:T(8,128)(2,1)S(1)}, bf16[15,768]{1,0:T(8,128)(2,1)S(1)}, u32[]{:S(2)}, u32[]{:S(2)}) collective-permute-start(bf16[15,768]{1,0:T(8,128)(2,1)S(1)} %get-tuple-element.101), channel_id=1, source_target_pairs={{0,4},{4,8},{8,12},{12,16},{16,20},{20,24},{24,28},{1,5},{5,9},{9,... | collective-permute-start | bytes 69128 | tf_op jit(solution)/shard_map/ppermute | solution.py:35
  31.9 10.7 %fusion.104 = (f32[768]{0:T(1024)S(1)}, f32[768]{0:T(1024)S(1)}, f32[768,768]{1,0:T(8,128)}) fusion(f32[768]{0:T(1024)S(1)} %get-tuple-element.44, f32[798,768]{1,0:T(8,128)S(1)} %maximum_convert_fusion, f32[768]{0:T(1024)S(1)} %get-tuple-element.45, f32[768]{0:T(1024)S(1)} %get-tuple-element.46, f32[768]{0:T(1024)S(1)} %get-tuple-element.47, ...), kind=kLoop, calls=%fused_computation.291 | loop fusion | flops 37747200 | bytes 75598848 | tf_op jit(solution)/shard_map/reduce_sum | solution.py:105
  46.3 5.6 %convolution_convert_fusion = bf16[1536,768]{1,0:T(8,128)(2,1)S(1)} fusion(bf16[768,768]{1,0:T(8,128)(2,1)} %collective-permute-done.5, bf16[768,768]{1,0:T(8,128)(2,1)} %bitcast.175, pred[]{:T(512)S(6)} %eq.4, f32[768,768]{1,0:T(8,128)} %get-tuple-element.83, f32[768]{0:T(1024)S(1)} %add_rsqrt_fusion, f32[768]{0:T(1024)S(1)} %get-tuple-element.78), kind=kOutput, calls=%fused_computation.37 | convolution fusion | flops 1827864576 | bytes 7084033 | tf_op jit(solution)/shard_map/dot_general | solution.py:112
  63.5 5.2 %fusion.103 = (f32[768]{0:T(1024)S(1)}, f32[768]{0:T(1024)S(1)}, f32[768,768]{1,0:T(8,128)S(1)}) fusion(f32[768]{0:T(1024)S(1)} %add_rsqrt_fusion, f32[768,768]{1,0:T(8,128)S(1)} %copy-done.5, f32[768]{0:T(1024)S(1)} %get-tuple-element.78, bf16[768,1536]{1,0:T(8,128)(2,1)S(1)} %copy-done.83, bf16[768,768]{1,0:T(8,128)(2,1)} %collective-permute-done.5, ...), kind=kOutput, calls=%fused_computation.290 | convolution fusion | flops 1830222336 | bytes 9449473 | tf_op jit(solution)/shard_map/dot_general | solution.py:126
  70.1 6.7 %fusion.33 = (f32[768]{0:T(1024)S(1)}, f32[768]{0:T(1024)S(1)}, f32[768]{0:T(1024)S(1)}, f32[768]{0:T(1024)S(1)}, f32[768]{0:T(1024)S(1)}, /*index=5*/f32[768]{0...) fusion(f32[798,768]{1,0:T(8,128)S(1)} %copy-done.2, ...), kind=kLoop, calls=%fused_computation.71 | loop fusion | flops 25938432 | bytes 48433152 | tf_op jit(solution)/shard_map/reduce_sum | solution.py:159
  81.5 3.9 %fusion.32 = (f32[768]{0:T(1024)S(1)}, f32[768]{0:T(1024)S(1)}, f32[768]{0:T(1024)S(1)}, f32[768]{0:T(1024)S(1)}, f32[768]{0:T(1024)S(1)}, /*index=5*/f32[768]{0...) fusion(bf16[768,768]{1,0:T(8,128)(2,1)S(1)} %get-tuple-element., ...), kind=kLoop, calls=%fused_computation.70 | loop fusion | flops 15915264 | bytes 31890432 | tf_op jit(solution)/shard_map/reduce_sum | solution.py:159
  103.6 5.4 %stack.163 = f32[31,768]{1,0:T(8,128)} concatenate(f32[1,768]{1,0:T(1,128)} %stack.132, f32[1,768]{1,0:T(1,128)} %stack.133, f32[1,768]{1,0:T(1,128)} %stack.134, f32[1,768]{1,0:T(1,128)} %stack.135, f32[1,768]{1,0:T(1,128)} %stack.136, f32[1,768]{1,0:T(1,128)} %stack.137, f32[1,768]{1,0:T(1,128)} %stack.138, f32[1,768]{1,0:T(1,128)} %stack.139, f32[1,768]{1,0:T(1,128)} %stack.140, ...), dimensions={0} | concatenate | bytes 190464 | tf_op jit(solution)/shard_map/stack | solution.py:158
  111.9 10.9 %multiply_convert_fusion = (bf16[768,768]{1,0:T(8,128)(2,1)S(1)}, f32[768,768]{1,0:T(8,128)S(1)}) fusion(f32[768,768]{1,0:T(8,128)S(1)} %copy-done.7, f32[768,768]{1,0:T(8,128)} %get-tuple-element.114, f32[768]{0:T(1024)S(1)} %copy-done.82, f32[768]{0:T(1024)S(1)} %get-tuple-element.44, f32[798,768]{1,0:T(8,128)S(1)} %maximum_convert_fusion.1, ...), kind=kLoop, calls=%fused_computation.139 | loop fusion | flops 39518208 | bytes 81494016 | tf_op jit(solution)/shard_map/convert_element_type | solution.py:142
  127.0 4.2 %fusion.114 = f32[768,1536]{1,0:T(8,128)} fusion(bf16[768,768]{1,0:T(8,128)(2,1)S(1)} %multiply_convert_fusion.1, bf16[1536,768]{1,0:T(8,128)(2,1)S(1)} %copy-done), kind=kOutput, calls=%fused_computation.299 | convolution fusion | flops 1811939328 | bytes 8257536 | tf_op jit(solution)/shard_map/dot_general | solution.py:163
  147.9 5.5 %add_convert_fusion = bf16[768,1536]{1,0:T(8,128)(2,1)S(1)} fusion(f32[768,1536]{1,0:T(8,128)} %fusion.114, bf16[768,768]{1,0:T(8,128)(2,1)} %copy-done.21, bf16[1536,768]{1,0:T(8,128)(2,1)} %param.11), kind=kOutput, calls=%fused_computation.36 | convolution fusion | flops 1814298624 | bytes 10616832 | tf_op jit(solution)/shard_map/dot_general | solution.py:163
  158.0 3.0 %collective-permute-done.22 = f32[31,768]{1,0:T(8,128)S(1)} collective-permute-done((f32[31,768]{1,0:T(8,128)S(1)}, f32[31,768]{1,0:T(8,128)S(1)}, u32[]{:S(2)}, u32[]{:S(2)}) %collective-permute-start.22) | collective-permute-done | bytes 95264 | tf_op jit(solution)/shard_map/ppermute | solution.py:11
  181.6 13.3 %collective-permute-done.26 = bf16[384,256]{1,0:T(8,128)(2,1)S(1)} collective-permute-done((bf16[384,256]{1,0:T(8,128)(2,1)S(1)}, bf16[384,256]{1,0:T(8,128)(2,1)S(1)}, u32[]{:S(2)}, u32[]{:S(2)}) %collective-permute-start.26) | collective-permute-done | bytes 196640 | tf_op jit(solution)/shard_map/ppermute | solution.py:11
  196.8 3.9 %collective-permute-done.29 = bf16[384,256]{1,0:T(8,128)(2,1)S(1)} collective-permute-done((bf16[384,256]{1,0:T(8,128)(2,1)S(1)}, bf16[384,256]{1,0:T(8,128)(2,1)S(1)}, u32[]{:S(2)}, u32[]{:S(2)}) %collective-permute-start.29) | collective-permute-done | bytes 196640 | tf_op jit(solution)/shard_map/ppermute | solution.py:11
  201.3 5.0 %collective-permute-done.32 = bf16[384,256]{1,0:T(8,128)(2,1)S(1)} collective-permute-done((bf16[384,256]{1,0:T(8,128)(2,1)S(1)}, bf16[384,256]{1,0:T(8,128)(2,1)S(1)}, u32[]{:S(2)}, u32[]{:S(2)}) %collective-permute-start.32) | collective-permute-done | bytes 196640 | tf_op jit(solution)/shard_map/ppermute | solution.py:11
  211.5 4.1 %collective-permute-done.30 = bf16[192,256]{1,0:T(8,128)(2,1)S(1)} collective-permute-done((bf16[192,256]{1,0:T(8,128)(2,1)S(1)}, bf16[192,256]{1,0:T(8,128)(2,1)S(1)}, u32[]{:S(2)}, u32[]{:S(2)}) %collective-permute-start.30) | collective-permute-done | bytes 98336 | tf_op jit(solution)/shard_map/ppermute | solution.py:11
  226.8 4.1 %collective-permute-done.34 = bf16[96,768]{1,0:T(8,128)(2,1)S(1)} collective-permute-done((bf16[96,768]{1,0:T(8,128)(2,1)S(1)}, bf16[96,768]{1,0:T(8,128)(2,1)S(1)}, u32[]{:S(2)}, u32[]{:S(2)}) %collective-permute-start.34) | collective-permute-done | bytes 147488 | tf_op jit(solution)/shard_map/ppermute | solution.py:11
  232.2 3.2 %fusion.71 = bf16[1,768,768]{2,1,0:T(8,128)(2,1)} fusion(bf16[768,768]{1,0:T(8,128)(2,1)} %collective-permute-done.4, bf16[768,1536]{1,0:T(8,128)(2,1)S(1)} %copy-done.14, s32[]{:T(128)S(6)} %select_n.93, bf16[1,768,768]{2,1,0:T(8,128)(2,1)S(1)} %copy-done.3), kind=kLoop, calls=%fused_computation.165 | loop fusion | flops 3538944 | bytes 4718596 | tf_op jit(solution)/shard_map/broadcast_in_dim | solution.py:184
  238.0 4.9 %collective-permute-done.18 = bf16[384,512]{1,0:T(8,128)(2,1)S(1)} collective-permute-done((bf16[384,512]{1,0:T(8,128)(2,1)S(1)}, bf16[384,512]{1,0:T(8,128)(2,1)S(1)}, u32[]{:S(2)}, u32[]{:S(2)}) %collective-permute-start.18) | collective-permute-done | bytes 393248 | tf_op jit(solution)/shard_map/ppermute | solution.py:11
  245.9 5.2 %collective-permute-done.19 = bf16[192,512]{1,0:T(8,128)(2,1)S(1)} collective-permute-done((bf16[192,512]{1,0:T(8,128)(2,1)S(1)}, bf16[192,512]{1,0:T(8,128)(2,1)S(1)}, u32[]{:S(2)}, u32[]{:S(2)}) %collective-permute-start.19) | collective-permute-done | bytes 196640 | tf_op jit(solution)/shard_map/ppermute | solution.py:11
  253.2 14.0 %collective-permute-done.20 = bf16[96,1536]{1,0:T(8,128)(2,1)S(1)} collective-permute-done((bf16[96,1536]{1,0:T(8,128)(2,1)S(1)}, bf16[96,1536]{1,0:T(8,128)(2,1)S(1)}, u32[]{:S(2)}, u32[]{:S(2)}) %collective-permute-start.20) | collective-permute-done | bytes 294944 | tf_op jit(solution)/shard_map/ppermute | solution.py:11
  (362 shorter events, 128.3 us)
Async XLA Ops:
  1.2 45.1 %collective-permute-start.5 = (bf16[768,768]{1,0:T(8,128)(2,1)}, bf16[768,768]{1,0:T(8,128)(2,1)}, u32[]{:S(2)}, u32[]{:S(2)}) collective-permute-start(bf16[768,768]{1,0:T(8,128)(2,1)} %bitcast.174), channel_id=1, source_target_pairs={{0,2},{2,0},{1,3},{3,1},{4,6},{6,4},{5,7},{7,5},{8,10},{10,8},{9,1... | collective-permute-start | bytes 3538952 | tf_op jit(solution)/shard_map/ppermute | solution.py:11
  21.0 7.9 %collective-permute-start.1 = (bf16[15,768]{1,0:T(8,128)(2,1)S(1)}, bf16[15,768]{1,0:T(8,128)(2,1)S(1)}, u32[]{:S(2)}, u32[]{:S(2)}) collective-permute-start(bf16[15,768]{1,0:T(8,128)(2,1)S(1)} %get-tuple-element.101), channel_id=1, source_target_pairs={{0,4},{4,8},{8,12},{12,16},{16,20},{20,24},{24,28},{1,5},{5,9},{9,... | collective-permute-start | bytes 69128 | tf_op jit(solution)/shard_map/ppermute | solution.py:35
  25.8 5.7 %collective-permute-start.2 = (bf16[15,768]{1,0:T(8,128)(2,1)S(1)}, bf16[15,768]{1,0:T(8,128)(2,1)S(1)}, u32[]{:S(2)}, u32[]{:S(2)}) collective-permute-start(bf16[15,768]{1,0:T(8,128)(2,1)S(1)} %get-tuple-element.102), channel_id=1, source_target_pairs={{4,0},{8,4},{12,8},{16,12},{20,16},{24,20},{28,24},{5,1},{9,5},{13... | collective-permute-start | bytes 69128 | tf_op jit(solution)/shard_map/ppermute | solution.py:36
  53.7 120.3 %collective-permute-start.25 = (bf16[768,256]{1,0:T(8,128)(2,1)}, bf16[768,256]{1,0:T(8,128)(2,1)}, u32[]{:S(2)}, u32[]{:S(2)}) collective-permute-start(bf16[768,256]{1,0:T(8,128)(2,1)} %bitcast.39), channel_id=1, source_target_pairs={{0,1},{1,0},{2,3},{3,2},{4,5},{5,4},{6,7},{7,6},{8,9},{9,8},{10,11... | collective-permute-start | bytes 1179656 | tf_op jit(solution)/shard_map/ppermute | solution.py:11
  56.1 121.3 %collective-permute-start.28 = (bf16[768,256]{1,0:T(8,128)(2,1)}, bf16[768,256]{1,0:T(8,128)(2,1)}, u32[]{:S(2)}, u32[]{:S(2)}) collective-permute-start(bf16[768,256]{1,0:T(8,128)(2,1)} %bitcast.49), channel_id=1, source_target_pairs={{0,4},{4,0},{8,12},{12,8},{16,20},{20,16},{24,28},{28,24},{1,5},{5... | collective-permute-start | bytes 1179656 | tf_op jit(solution)/shard_map/ppermute | solution.py:11
  59.5 119.2 %collective-permute-start.31 = (bf16[768,256]{1,0:T(8,128)(2,1)}, bf16[768,256]{1,0:T(8,128)(2,1)}, u32[]{:S(2)}, u32[]{:S(2)}) collective-permute-start(bf16[768,256]{1,0:T(8,128)(2,1)} %bitcast.59), channel_id=1, source_target_pairs={{0,8},{4,12},{8,0},{12,4},{16,24},{20,28},{24,16},{28,20},{1,9},{5... | collective-permute-start | bytes 1179656 | tf_op jit(solution)/shard_map/ppermute | solution.py:11
  77.5 31.7 %collective-permute-start.7 = (bf16[15,768]{1,0:T(8,128)(2,1)}, bf16[15,768]{1,0:T(8,128)(2,1)}, u32[]{:S(2)}, u32[]{:S(2)}) collective-permute-start(bf16[15,768]{1,0:T(8,128)(2,1)} %get-tuple-element.99), channel_id=1, source_target_pairs={{0,4},{4,8},{8,12},{12,16},{16,20},{20,24},{24,28},{1,5},{5,9},{9,... | collective-permute-start | bytes 69128 | tf_op jit(solution)/shard_map/ppermute | solution.py:35
  80.0 29.5 %collective-permute-start.8 = (bf16[15,768]{1,0:T(8,128)(2,1)}, bf16[15,768]{1,0:T(8,128)(2,1)}, u32[]{:S(2)}, u32[]{:S(2)}) collective-permute-start(bf16[15,768]{1,0:T(8,128)(2,1)} %get-tuple-element.100), channel_id=1, source_target_pairs={{4,0},{8,4},{12,8},{16,12},{20,16},{24,20},{28,24},{5,1},{9,5},{13... | collective-permute-start | bytes 69128 | tf_op jit(solution)/shard_map/ppermute | solution.py:36
  109.3 122.9 %collective-permute-start.4 = (bf16[768,768]{1,0:T(8,128)(2,1)}, bf16[768,768]{1,0:T(8,128)(2,1)}, u32[]{:S(2)}, u32[]{:S(2)}) collective-permute-start(bf16[768,768]{1,0:T(8,128)(2,1)} %constant_dynamic-slice_fusion.23), channel_id=1, source_target_pairs={{0,2},{2,0},{1,3},{3,1},{4,6},{6,4},{5,7},{7,5},{8,10},{10,8},{9,1... | collective-permute-start | bytes 3538952 | tf_op jit(solution)/shard_map/ppermute | solution.py:11
  109.5 44.1 %collective-permute-start.21 = (f32[31,768]{1,0:T(8,128)}, f32[31,768]{1,0:T(8,128)}, u32[]{:S(2)}, u32[]{:S(2)}) collective-permute-start(f32[31,768]{1,0:T(8,128)} %stack.163), channel_id=1, source_target_pairs={{0,1},{1,0},{2,3},{3,2},{4,5},{5,4},{6,7},{7,6},{8,9},{9,8},{10,11... | collective-permute-start | bytes 285704 | tf_op jit(solution)/shard_map/ppermute | solution.py:11
  155.3 5.8 %collective-permute-start.22 = (f32[31,768]{1,0:T(8,128)S(1)}, f32[31,768]{1,0:T(8,128)S(1)}, u32[]{:S(2)}, u32[]{:S(2)}) collective-permute-start(f32[31,768]{1,0:T(8,128)S(1)} %add.489), channel_id=1, source_target_pairs={{0,4},{4,0},{8,12},{12,8},{16,20},{20,16},{24,28},{28,24},{1,5},{5... | collective-permute-start | bytes 285704 | tf_op jit(solution)/shard_map/ppermute | solution.py:11
  171.8 48.4 %collective-permute-start.11 = (bf16[768,512]{1,0:T(8,128)(2,1)S(1)}, bf16[768,512]{1,0:T(8,128)(2,1)S(1)}, u32[]{:S(2)}, u32[]{:S(2)}) collective-permute-start(bf16[768,512]{1,0:T(8,128)(2,1)S(1)} %bitcast.178), channel_id=1, source_target_pairs={{0,1},{1,0},{2,3},{3,2},{4,5},{5,4},{6,7},{7,6},{8,9},{9,8},{10,11... | collective-permute-start | bytes 2359304 | tf_op jit(solution)/shard_map/ppermute | solution.py:11
  174.0 49.4 %collective-permute-start.14 = (bf16[768,512]{1,0:T(8,128)(2,1)S(1)}, bf16[768,512]{1,0:T(8,128)(2,1)S(1)}, u32[]{:S(2)}, u32[]{:S(2)}) collective-permute-start(bf16[768,512]{1,0:T(8,128)(2,1)S(1)} %bitcast.180), channel_id=1, source_target_pairs={{0,4},{4,0},{8,12},{12,8},{16,20},{20,16},{24,28},{28,24},{1,5},{5... | collective-permute-start | bytes 2359304 | tf_op jit(solution)/shard_map/ppermute | solution.py:11
  177.4 47.0 %collective-permute-start.17 = (bf16[768,512]{1,0:T(8,128)(2,1)S(1)}, bf16[768,512]{1,0:T(8,128)(2,1)S(1)}, u32[]{:S(2)}, u32[]{:S(2)}) collective-permute-start(bf16[768,512]{1,0:T(8,128)(2,1)S(1)} %bitcast.179), channel_id=1, source_target_pairs={{0,8},{4,12},{8,0},{12,4},{16,24},{20,28},{24,16},{28,20},{1,9},{5... | collective-permute-start | bytes 2359304 | tf_op jit(solution)/shard_map/ppermute | solution.py:11
  178.7 16.2 %collective-permute-start.26 = (bf16[384,256]{1,0:T(8,128)(2,1)S(1)}, bf16[384,256]{1,0:T(8,128)(2,1)S(1)}, u32[]{:S(2)}, u32[]{:S(2)}) collective-permute-start(bf16[384,256]{1,0:T(8,128)(2,1)S(1)} %bitcast.192), channel_id=1, source_target_pairs={{0,4},{4,0},{8,12},{12,8},{16,20},{20,16},{24,28},{28,24},{1,5},{5... | collective-permute-start | bytes 589832 | tf_op jit(solution)/shard_map/ppermute | solution.py:11
  220.1 22.9 %collective-permute-start.9 = (bf16[768,768]{1,0:T(8,128)(2,1)S(1)}, bf16[768,768]{1,0:T(8,128)(2,1)S(1)}, u32[]{:S(2)}, u32[]{:S(2)}) collective-permute-start(bf16[768,768]{1,0:T(8,128)(2,1)S(1)} %constant_dynamic-slice_fusion.22), channel_id=1, source_target_pairs={{0,2},{2,0},{1,3},{3,1},{4,6},{6,4},{5,7},{7,5},{8,10},{10,8},{9,1... | collective-permute-start | bytes 3538952 | tf_op jit(solution)/shard_map/ppermute | solution.py:11
  220.2 10.7 %collective-permute-start.34 = (bf16[96,768]{1,0:T(8,128)(2,1)S(1)}, bf16[96,768]{1,0:T(8,128)(2,1)S(1)}, u32[]{:S(2)}, u32[]{:S(2)}) collective-permute-start(bf16[96,768]{1,0:T(8,128)(2,1)S(1)} %dynamic-slice_bitcast_fusion.1), channel_id=1, source_target_pairs={{0,16},{4,20},{8,24},{12,28},{16,0},{20,4},{24,8},{28,12},{1,17},{... | collective-permute-start | bytes 442376 | tf_op jit(solution)/shard_map/ppermute | solution.py:11
  223.4 12.0 %collective-permute-start.12 = (bf16[384,512]{1,0:T(8,128)(2,1)S(1)}, bf16[384,512]{1,0:T(8,128)(2,1)S(1)}, u32[]{:S(2)}, u32[]{:S(2)}) collective-permute-start(bf16[384,512]{1,0:T(8,128)(2,1)S(1)} %bitcast.185), channel_id=1, source_target_pairs={{0,4},{4,0},{8,12},{12,8},{16,20},{20,16},{24,28},{28,24},{1,5},{5... | collective-permute-start | bytes 1179656 | tf_op jit(solution)/shard_map/ppermute | solution.py:11
  224.4 12.9 %collective-permute-start.15 = (bf16[384,512]{1,0:T(8,128)(2,1)S(1)}, bf16[384,512]{1,0:T(8,128)(2,1)S(1)}, u32[]{:S(2)}, u32[]{:S(2)}) collective-permute-start(bf16[384,512]{1,0:T(8,128)(2,1)S(1)} %bitcast.183), channel_id=1, source_target_pairs={{0,8},{4,12},{8,0},{12,4},{16,24},{20,28},{24,16},{28,20},{1,9},{5... | collective-permute-start | bytes 1179656 | tf_op jit(solution)/shard_map/ppermute | solution.py:11
  230.9 12.0 %collective-permute-start.18 = (bf16[384,512]{1,0:T(8,128)(2,1)S(1)}, bf16[384,512]{1,0:T(8,128)(2,1)S(1)}, u32[]{:S(2)}, u32[]{:S(2)}) collective-permute-start(bf16[384,512]{1,0:T(8,128)(2,1)S(1)} %bitcast.184), channel_id=1, source_target_pairs={{0,1},{1,0},{2,3},{3,2},{4,5},{5,4},{6,7},{7,6},{8,9},{9,8},{10,11... | collective-permute-start | bytes 1179656 | tf_op jit(solution)/shard_map/ppermute | solution.py:11
  235.5 9.9 %collective-permute-start.13 = (bf16[192,512]{1,0:T(8,128)(2,1)S(1)}, bf16[192,512]{1,0:T(8,128)(2,1)S(1)}, u32[]{:S(2)}, u32[]{:S(2)}) collective-permute-start(bf16[192,512]{1,0:T(8,128)(2,1)S(1)} %bitcast.189), channel_id=1, source_target_pairs={{0,8},{4,12},{8,0},{12,4},{16,24},{20,28},{24,16},{28,20},{1,9},{5... | collective-permute-start | bytes 589832 | tf_op jit(solution)/shard_map/ppermute | solution.py:11
  237.4 8.4 %collective-permute-start.16 = (bf16[192,512]{1,0:T(8,128)(2,1)S(1)}, bf16[192,512]{1,0:T(8,128)(2,1)S(1)}, u32[]{:S(2)}, u32[]{:S(2)}) collective-permute-start(bf16[192,512]{1,0:T(8,128)(2,1)S(1)} %bitcast.190), channel_id=1, source_target_pairs={{0,1},{1,0},{2,3},{3,2},{4,5},{5,4},{6,7},{7,6},{8,9},{9,8},{10,11... | collective-permute-start | bytes 589832 | tf_op jit(solution)/shard_map/ppermute | solution.py:11
  243.8 7.4 %collective-permute-start.19 = (bf16[192,512]{1,0:T(8,128)(2,1)S(1)}, bf16[192,512]{1,0:T(8,128)(2,1)S(1)}, u32[]{:S(2)}, u32[]{:S(2)}) collective-permute-start(bf16[192,512]{1,0:T(8,128)(2,1)S(1)} %bitcast.191), channel_id=1, source_target_pairs={{0,4},{4,0},{8,12},{12,8},{16,20},{20,16},{24,28},{28,24},{1,5},{5... | collective-permute-start | bytes 589832 | tf_op jit(solution)/shard_map/ppermute | solution.py:11
  251.3 15.9 %collective-permute-start.20 = (bf16[96,1536]{1,0:T(8,128)(2,1)S(1)}, bf16[96,1536]{1,0:T(8,128)(2,1)S(1)}, u32[]{:S(2)}, u32[]{:S(2)}) collective-permute-start(bf16[96,1536]{1,0:T(8,128)(2,1)S(1)} %dynamic-slice_bitcast_fusion), channel_id=1, source_target_pairs={{0,16},{4,20},{8,24},{12,28},{16,0},{20,4},{24,8},{28,12},{1,17},{... | collective-permute-start | bytes 884744 | tf_op jit(solution)/shard_map/ppermute | solution.py:11
  (98 other events, 925.9 us)

commit v2 on v1

v2 whole, which is shorter than its diff:
```python
import functools

import jax
import jax.numpy as jnp
from jax import lax
from jax.experimental import pallas as pl
from jax.experimental.pallas import tpu as pltpu
from jax.sharding import PartitionSpec as P

epsilon = 1e-05
f32, bf16 = jnp.float32, jnp.bfloat16
LANES = 128
WIDE, NEAR = 32, 16
NT = (((1,), (1,)), ((), ()))
PARAMS = dict(vmem_limit_bytes=48 << 20)


def swap(value, axis, bit=0):
    size = lax.axis_size(axis)
    return lax.ppermute(value, axis, [(i, i ^ (1 << bit)) for i in range(size)])


def bits_of(axis):
    return [(axis, b) for b in range(lax.axis_size(axis).bit_length() - 1)]


class Halver:
    def __init__(self, terms):
        self.bits = bits_of("seq")[::-1] + bits_of("dp")[::-1]
        blocks = 1 << len(self.bits)
        rows = terms.shape[0] // blocks
        self.value = terms.reshape((2,) * len(self.bits) + (rows, terms.shape[1]))

    def step(self, bit):
        dim = self.bits.index(bit)
        mine = (lax.axis_index(bit[0]) >> bit[1]) & 1
        send = lax.dynamic_index_in_dim(self.value, 1 - mine, dim, keepdims=False)
        keep = lax.dynamic_index_in_dim(self.value, mine, dim, keepdims=False)
        shape = send.shape
        got = swap(send.reshape(-1, shape[-1]), *bit).reshape(shape)
        self.value = keep.astype(f32) + got.astype(f32)
        self.bits = self.bits[:dim] + self.bits[dim + 1 :]
        if self.bits:
            self.value = self.value.astype(bf16)


def scatter_sum(terms):
    thirds = [Halver(t) for t in terms]
    every = bits_of("dp") + bits_of("seq")
    turning, rest = every[:3], every[3:]
    for phase in range(len(turning)):
        for i, third in enumerate(thirds):
            third.step(turning[(i + phase) % len(turning)])
    merged = thirds[0]
    merged.value = jnp.concatenate([t.value for t in thirds], axis=-1)
    for bit in rest:
        merged.step(bit)
    return merged.value


def row_mask(info, first, rows, limit):
    place = info[0] + first + lax.broadcasted_iota(jnp.int32, (rows, 1), 0)
    return ((place >= 0) & (place < limit)).astype(f32)


def front_kernel(info, own, other, halo_own, halo_other, wv, wg, norm, rstd, hid, sig, slope, edge):
    half = own.shape[1]
    count = own.shape[0]
    mine = pl.multiple_of(info[3] * half, half)
    theirs = pl.multiple_of((1 - info[3]) * half, half)

    def normalize(a, b):
        a, b = a.astype(f32), b.astype(f32)
        width = 2 * half
        mean = (jnp.sum(a, 1, keepdims=True) + jnp.sum(b, 1, keepdims=True)) / width
        a, b = a - mean, b - mean
        var = (jnp.sum(a * a, 1, keepdims=True) + jnp.sum(b * b, 1, keepdims=True)) / width
        inverse = lax.rsqrt(var + epsilon)
        return (a * inverse).astype(bf16), (b * inverse).astype(bf16), inverse

    @pl.when(pl.program_id(0) == 0)
    def _():
        def body(i, _):
            rows = pl.ds(pl.multiple_of(i * 32, 32), 32)
            a, b, inverse = normalize(own[rows, :], other[rows, :])
            norm[rows, pl.ds(mine, half)] = a
            norm[rows, pl.ds(theirs, half)] = b
            rstd[rows, :] = jnp.broadcast_to(inverse, (32, LANES))
            return 0

        lax.fori_loop(0, count // 32, body, 0)
        for to, at in ((0, 0), (WIDE, WIDE + NEAR)):
            a, b, _ = normalize(halo_own[at : at + WIDE, :], halo_other[at : at + WIDE, :])
            edge[to : to + WIDE, pl.ds(mine, half)] = a
            edge[to : to + WIDE, pl.ds(theirs, half)] = b

    def gated(rows):
        value = jnp.dot(rows, wv[...], preferred_element_type=f32)
        gate = jnp.dot(rows, wg[...], preferred_element_type=f32)
        return value, jax.nn.sigmoid(gate)

    step = count // 4
    for c in range(0, count, step):
        value, s = gated(norm[c : c + step, :])
        keep = row_mask(info, c, step, info[1])
        vs = value * s * keep
        hid[WIDE + c : WIDE + c + step, :] = vs.astype(bf16)
        sig[c : c + step, :] = s * keep
        slope[c : c + step, :] = vs * (1.0 - s)
    value, s = gated(edge[...])
    vs = value * s
    hid[:WIDE, :] = (vs[:WIDE] * row_mask(info, -WIDE, WIDE, info[1])).astype(bf16)
    hid[WIDE + count :, :] = (vs[WIDE:] * row_mask(info, count, WIDE, info[1])).astype(bf16)


def whole(shape):
    return pl.BlockSpec(shape, lambda n: (0,) * len(shape))


def cost(flops, nbytes, trans=0):
    return pl.CostEstimate(flops=flops, bytes_accessed=nbytes, transcendentals=trans)


SMEM = pl.BlockSpec(memory_space=pltpu.SMEM)


def front(info, own, other, halo_own, halo_other, w_value, w_gate):
    count, half = own.shape
    width, channels = w_value.shape
    tile = channels // 3
    columns = lambda rows: pl.BlockSpec((rows, tile), lambda n: (0, n))
    return pl.pallas_call(
        front_kernel,
        grid=(channels // tile,),
        in_specs=[SMEM]
        + [whole(a.shape) for a in (own, other, halo_own, halo_other)]
        + [columns(width), columns(width)],
        out_specs=[
            whole((count, width)),
            whole((count, LANES)),
            columns(count + 2 * WIDE),
            columns(count),
            columns(count),
        ],
        out_shape=[
            jax.ShapeDtypeStruct((count, width), bf16),
            jax.ShapeDtypeStruct((count, LANES), f32),
            jax.ShapeDtypeStruct((count + 2 * WIDE, channels), bf16),
            jax.ShapeDtypeStruct((count, channels), f32),
            jax.ShapeDtypeStruct((count, channels), f32),
        ],
        scratch_shapes=[pltpu.VMEM((2 * WIDE, width), bf16)],
        compiler_params=pltpu.CompilerParams(**PARAMS),
        cost_estimate=cost(4 * count * width * channels, 20 << 20, count * channels),
        name="front",
    )(info, own, other, halo_own, halo_other, w_value, w_gate)


def upstream_kernel(info, own, other, halo_own, halo_other, w_out, full, out, edge):
    count, half = own.shape
    mine = pl.multiple_of(info[3] * half, half)
    theirs = pl.multiple_of((1 - info[3]) * half, half)

    @pl.when(pl.program_id(0) == 0)
    def _():
        for a, b, at in ((own, halo_own, mine), (other, halo_other, theirs)):
            full[:, pl.ds(at, half)] = a[...]
            edge[:NEAR, pl.ds(at, half)] = b[WIDE : WIDE + NEAR, :]
            edge[NEAR:, pl.ds(at, half)] = b[2 * WIDE + NEAR :, :]

    step = count // 4
    for c in range(0, count, step):
        out[NEAR + c : NEAR + c + step, :] = lax.dot_general(
            full[c : c + step, :], w_out[...], NT, preferred_element_type=f32
        )
    ends = lax.dot_general(edge[...], w_out[...], NT, preferred_element_type=f32)
    out[:NEAR, :] = ends[:NEAR]
    out[NEAR + count :, :] = ends[NEAR:]


def upstream(info, own, other, halo_own, halo_other, w_out):
    count, half = own.shape
    channels, width = w_out.shape
    tile = channels // 3
    return pl.pallas_call(
        upstream_kernel,
        grid=(channels // tile,),
        in_specs=[SMEM]
        + [whole(a.shape) for a in (own, other, halo_own, halo_other)]
        + [pl.BlockSpec((tile, width), lambda n: (n, 0))],
        out_specs=[
            whole((count, width)),
            pl.BlockSpec((count + 2 * NEAR, tile), lambda n: (0, n)),
        ],
        out_shape=[
            jax.ShapeDtypeStruct((count, width), bf16),
            jax.ShapeDtypeStruct((count + 2 * NEAR, channels), f32),
        ],
        scratch_shapes=[pltpu.VMEM((2 * NEAR, width), bf16)],
        compiler_params=pltpu.CompilerParams(**PARAMS),
        cost_estimate=cost(2 * count * width * channels, 10 << 20),
        name="upstream",
    )(info, own, other, halo_own, halo_other, w_out)


def tap_sums(source, base, groups, taps):
    sums = [None] * groups
    for residue in range(8):
        mine = list(range(residue, len(taps), 8))
        shifted = [
            source[pl.ds(base + 8 * i + residue, 8), :] for i in range(groups + len(mine) - 1)
        ]
        for i, k in enumerate(mine):
            for g in range(groups):
                term = shifted[g + i] * taps[k]
                sums[g] = term if sums[g] is None else sums[g] + term
    return sums


def tap_rows(taps, reverse=False):
    values = taps[...].astype(f32)
    order = range(taps.shape[0])
    return [
        jnp.broadcast_to(values[k : k + 1, :], (8, LANES))
        for k in (reversed(order) if reverse else order)
    ]


def paired(first, second):
    lane = lax.broadcasted_iota(jnp.int32, (first.shape[0], LANES), 1)
    return jnp.where(
        lane < LANES // 2,
        jnp.sum(first, axis=1, keepdims=True),
        jnp.sum(second, axis=1, keepdims=True),
    )


def conv_kernel(hid, taps, conv, stats, scratch, total, square):
    n = pl.program_id(0)
    rows = conv.shape[0]
    skip = WIDE - NEAR - (taps.shape[0] - 1) // 2
    scratch[: hid.shape[0], :] = hid[...].astype(f32)
    weights = tap_rows(taps)
    groups = 20

    @pl.when(n == 0)
    def _():
        total[...] = jnp.zeros_like(total)
        square[...] = jnp.zeros_like(square)

    def body(i, _):
        base = pl.multiple_of(i * 8 * groups, 8)
        for g, value in enumerate(tap_sums(scratch, base + skip, groups, weights)):
            at = pl.ds(base + 8 * g, 8)
            conv[at, :] = value
            total[at, :] += value
            square[at, :] += value * value
        return 0

    lax.fori_loop(0, rows // (8 * groups), body, 0)

    @pl.when(n == pl.num_programs(0) - 1)
    def _():
        stats[...] = paired(total[...], square[...])


def depthwise(hid, taps):
    rows, channels = hid.shape
    kept = rows - 2 * (WIDE - NEAR)
    columns = lambda r: pl.BlockSpec((r, LANES), lambda n: (0, n))
    return pl.pallas_call(
        conv_kernel,
        grid=(channels // LANES,),
        in_specs=[columns(rows), columns(taps.shape[0])],
        out_specs=[columns(kept), whole((kept, LANES))],
        out_shape=[
            jax.ShapeDtypeStruct((kept, channels), f32),
            jax.ShapeDtypeStruct((kept, LANES), f32),
        ],
        scratch_shapes=[
            pltpu.VMEM((rows + 16, LANES), f32),
            pltpu.VMEM((kept, LANES), f32),
            pltpu.VMEM((kept, LANES), f32),
        ],
        compiler_params=pltpu.CompilerParams(**PARAMS),
        cost_estimate=cost(62 * kept * channels, 4 << 20),
        name="depthwise",
    )(hid, taps)


def moments(first, second, width):
    mean = (first[:, :1] + second[:, :1]) / width
    half = LANES // 2
    square = (first[:, half : half + 1] + second[:, half : half + 1]) / width
    return mean, lax.rsqrt(square - mean * mean + epsilon)


def swish_kernel(conv, pull, own, other, swished, dswish, stats):
    mean, inverse = moments(own, other, 2 * conv.shape[1])
    zhat = (conv[...] - mean) * inverse
    s = jax.nn.sigmoid(zhat)
    zs = zhat * s
    swished[...] = zs.astype(bf16)
    d = pull[...] * (s + zs * (1.0 - s))
    dswish[...] = d
    stats[...] = paired(d, d * zhat)


def swish(conv, pull, own, other):
    rows, channels = conv.shape
    step = 160
    block = lambda c: pl.BlockSpec((step, c), lambda n: (n, 0))
    return pl.pallas_call(
        swish_kernel,
        grid=(rows // step,),
        in_specs=[block(channels), block(channels), block(LANES), block(LANES)],
        out_specs=[block(channels), block(channels), block(LANES)],
        out_shape=[
            jax.ShapeDtypeStruct((rows, channels), bf16),
            jax.ShapeDtypeStruct((rows, channels), f32),
            jax.ShapeDtypeStruct((rows, LANES), f32),
        ],
        compiler_params=pltpu.CompilerParams(**PARAMS),
        cost_estimate=cost(20 * rows * channels, 9 << 20, rows * channels),
        name="swish",
    )(conv, pull, own, other)


def back_kernel(info, dswish, conv, own, other, own2, other2, taps, sig, slope, dconv, dvg, scratch, coef, *, width):
    rows = dswish.shape[0]
    count = sig.shape[0]
    channels = width // 2

    @pl.when(pl.program_id(0) == 0)
    def _():
        mean, inverse = moments(own, other, width)
        half = LANES // 2
        shift = (own2[:, :1] + other2[:, :1]) / width
        cross = (own2[:, half : half + 1] + other2[:, half : half + 1]) / width
        keep = row_mask(info, -NEAR, rows, info[2])
        inverse = inverse * keep
        tilt = inverse * inverse * cross
        coef[0] = jnp.broadcast_to(inverse, (rows, LANES))
        coef[1] = jnp.broadcast_to(tilt, (rows, LANES))
        coef[2] = jnp.broadcast_to(tilt * mean - inverse * shift, (rows, LANES))

    d = (coef[0] * dswish[...] - coef[1] * conv[...] + coef[2]).astype(bf16)
    dconv[...] = d
    scratch[:rows, :] = d.astype(f32)
    weights = tap_rows(taps, reverse=True)
    groups = 16
    skip = NEAR - (taps.shape[0] - 1) // 2

    def body(i, _):
        base = pl.multiple_of(i * 8 * groups, 16)
        sums = tap_sums(scratch, base + skip, groups, weights)
        for g in range(0, groups, 2):
            at = pl.ds(base + 8 * g, 16)
            dh = jnp.concatenate(sums[g : g + 2], axis=0)
            dvg[0, at, :] = (dh * sig[at, :]).astype(bf16)
            dvg[1, at, :] = (dh * slope[at, :]).astype(bf16)
        return 0

    lax.fori_loop(0, count // (8 * groups), body, 0)


def back(info, third, dswish, conv, stats, stats2, taps, sig, slope):
    rows, channels = dswish.shape
    count = sig.shape[0]
    tiles = channels // LANES // 3
    columns = lambda r: pl.BlockSpec((r, LANES), lambda n: (0, third * tiles + n))
    local = lambda r: pl.BlockSpec((r, LANES), lambda n: (0, n))
    return pl.pallas_call(
        functools.partial(back_kernel, width=2 * channels),
        grid=(tiles,),
        in_specs=[SMEM, columns(rows), columns(rows)]
        + [whole((rows, LANES))] * 4
        + [columns(taps.shape[0]), columns(count), columns(count)],
        out_specs=[local(rows), pl.BlockSpec((2, count, LANES), lambda n: (0, 0, n))],
        out_shape=[
            jax.ShapeDtypeStruct((rows, tiles * LANES), bf16),
            jax.ShapeDtypeStruct((2, count, tiles * LANES), bf16),
        ],
        scratch_shapes=[
            pltpu.VMEM((rows + 16, LANES), f32),
            pltpu.VMEM((3, rows, LANES), f32),
        ],
        compiler_params=pltpu.CompilerParams(**PARAMS),
        cost_estimate=cost(70 * count * tiles * LANES, 5 << 20),
        name="back",
    )(info, dswish, conv, *stats, *stats2, taps, sig, slope)


def taps_kernel(dconv, hid, out, scratch, total):
    count = dconv.shape[0] - 2 * NEAR
    taps = out.shape[0]
    half = (taps - 1) // 2
    scratch[: dconv.shape[0], :] = dconv[...].astype(f32)
    total[...] = jnp.zeros_like(total)
    groups = 16

    def body(i, _):
        base = pl.multiple_of(i * 8 * groups, 16)
        h = []
        for g in range(0, groups, 2):
            both = hid[pl.ds(WIDE + base + 8 * g, 16), :].astype(f32)
            h += [both[:8], both[8:]]
        for residue in range(8):
            mine = list(range(residue, taps, 8))
            shifted = [
                scratch[pl.ds(base + NEAR - half + 8 * g + residue, 8), :]
                for g in range(groups + len(mine) - 1)
            ]
            for j, m in enumerate(mine):
                term = shifted[j] * h[0]
                for g in range(1, groups):
                    term = term + shifted[g + j] * h[g]
                total[taps - 1 - m] += term
        return 0

    lax.fori_loop(0, count // (8 * groups), body, 0)
    out[...] = jnp.sum(total[...], axis=1)


def taps_gradient(third, dconv, hid, taps):
    rows, channels = dconv.shape
    tiles = channels // LANES
    local = lambda r: pl.BlockSpec((r, LANES), lambda n: (0, n))
    return pl.pallas_call(
        taps_kernel,
        grid=(tiles,),
        in_specs=[
            local(rows),
            pl.BlockSpec((hid.shape[0], LANES), lambda n: (0, third * tiles + n)),
        ],
        out_specs=local(taps),
        out_shape=jax.ShapeDtypeStruct((taps, channels), f32),
        scratch_shapes=[
            pltpu.VMEM((rows + 16, LANES), f32),
            pltpu.VMEM((taps, 8, LANES), f32),
        ],
        compiler_params=pltpu.CompilerParams(**PARAMS),
        cost_estimate=cost(62 * rows * channels, 1 << 20),
        name="taps",
    )(dconv, hid)


def shards(inputs, lengths, cotangent, w_value, w_gate, kernel, w_out):
    x, ct = inputs[0], cotangent[0]
    count, channels = x.shape
    width = channels * lax.axis_size("tensor")
    core = lax.axis_index("tensor")
    peers = lax.axis_size("seq")
    info = jnp.stack(
        [lax.axis_index("seq") * count, lengths[0], jnp.int32(peers * count), core]
    ).astype(jnp.int32)

    up = [(i, i + 1) for i in range(peers - 1)]
    down = [(j, i) for i, j in up]
    before = lax.ppermute(jnp.concatenate([x[-WIDE:], ct[-NEAR:]]), "seq", up)
    after = lax.ppermute(jnp.concatenate([x[:WIDE], ct[:NEAR]]), "seq", down)
    halo = jnp.concatenate([before, after])
    x_other, ct_other, halo_other = swap(x, "tensor"), swap(ct, "tensor"), swap(halo, "tensor")

    ct_full, pull = upstream(info, ct, ct_other, halo, halo_other, w_out)
    norm, rstd, hid, sig, slope = front(info, x, x_other, halo, halo_other, w_value, w_gate)
    conv, stats = depthwise(hid, kernel)
    stats_other = swap(stats, "tensor")
    swished, dswish, stats2 = swish(conv, pull, stats, stats_other)
    stats2_other = swap(stats2, "tensor")
    swished = swished[NEAR : NEAR + count]

    third = channels // 3
    out_term = jnp.dot(ct_full.T, swished, preferred_element_type=f32).astype(bf16)
    out_grad = scatter_sum(jnp.split(out_term, 3, axis=1)).T

    dconvs, dvgs, terms = [], [], []
    for i in range(3):
        dconv, dvg = back(
            info, i, dswish, conv, (stats, stats_other), (stats2, stats2_other), kernel, sig, slope
        )
        dconvs.append(dconv)
        dvgs.append(dvg)
        terms.append(
            jnp.concatenate(
                [jnp.dot(norm.T, dvg[j], preferred_element_type=f32).astype(bf16) for j in (0, 1)],
                axis=1,
            )
        )
    grads = scatter_sum(terms)
    value_grad, gate_grad = (
        jnp.concatenate([grads[:, (2 * i + j) * third :][:, :third] for i in range(3)], axis=1)
        for j in (0, 1)
    )
    kernel_grad = jnp.concatenate(
        [taps_gradient(i, dconvs[i], hid, kernel.shape[0]) for i in range(3)], axis=1
    )
    for bit in bits_of("dp") + bits_of("seq"):
        kernel_grad = kernel_grad + swap(kernel_grad, *bit)

    def pair_scatter(product):
        theirs = product((1 - core) * channels).astype(bf16)
        got = swap(theirs, "tensor").astype(f32)
        return product(core * channels) + got

    def out_part(at):
        w = lax.dynamic_slice_in_dim(w_out, at, channels, 1)
        return jnp.dot(swished, w, preferred_element_type=f32)

    dvalues, dgates = (jnp.concatenate([dvg[j] for dvg in dvgs], axis=1) for j in (0, 1))

    def norm_part(at):
        wv = lax.dynamic_slice_in_dim(w_value, at, channels, 0)
        wg = lax.dynamic_slice_in_dim(w_gate, at, channels, 0)
        return jnp.dot(dvalues, wv.T, preferred_element_type=f32) + jnp.dot(
            dgates, wg.T, preferred_element_type=f32
        )

    output = (x.astype(f32) + pair_scatter(out_part)).astype(bf16)
    dnorm = pair_scatter(norm_part)
    xhat = lax.dynamic_slice_in_dim(norm, core * channels, channels, 1).astype(f32)
    sums = jnp.stack([jnp.sum(dnorm, axis=-1), jnp.sum(dnorm * xhat, axis=-1)])
    sums = (sums + swap(sums, "tensor")) / width
    input_gradient = ct.astype(f32) + rstd[:, :1] * (
        dnorm - sums[0][:, None] - xhat * sums[1][:, None]
    )
    return (
        output[None],
        input_gradient.astype(bf16)[None],
        value_grad,
        gate_grad,
        kernel_grad,
        out_grad,
    )


def solution(mesh):
    return jax.shard_map(
        shards,
        mesh=mesh,
        in_specs=(
            P("dp", "seq", "tensor"),
            P("dp"),
            P("dp", "seq", "tensor"),
            P(None, "tensor"),
            P(None, "tensor"),
            P(None, "tensor"),
            P("tensor", None),
        ),
        out_specs=(
            P("dp", "seq", "tensor"),
            P("dp", "seq", "tensor"),
            P(("seq", "dp"), "tensor"),
            P(("seq", "dp"), "tensor"),
            P(None, "tensor"),
            P("tensor", ("seq", "dp")),
        ),
        check_vma=False,
    )
```

time: 274 us -> 224 us (0.82); the launches traced: 269 us -> 223 us
  Pallas kernels: 0 us -> 51.8 us
  other arithmetic: 66.3 us -> 14.8 us
  local copies, waits for them, and re-layouts: 46 us -> 27.1 us
  matrix products: 32.7 us -> 22.5 us
  starting transfers between devices: 47.2 us -> 39.1 us
  waiting for transfers between devices: 73.4 us -> 65.5 us
    pallas_call x0 -> x10, Pallas kernels: none -> 51.8 us  [the longest x1 13.6 us: front(): pl.pallas_call(front_kernel, grid=(channels // tile,), in_specs=[SMEM] +...]
    reduce_sum x6 -> x0, other arithmetic: 27.9 us -> none  [the longest x1 10.7 us: shards(): jnp.sum(conv, axis=-1)]
    another operation x38 -> x2, local copies, waits for them, and re-layouts: 23.6 us -> 0.01 us  [shards(): sums = jnp.stack([jnp.sum(dnorm, axis=-1), jnp.sum(dnorm * xhat, axis=-1)])]
    convert_element_type x25 -> x18, other arithmetic: 23.6 us -> 4.66 us  [step(): self.value = self.value.astype(bf16)]
    dot_general x9 -> x13, matrix products: 32.7 us -> 22.5 us  [the longest x6 8.55 us: shards(): jnp.dot(norm.T, dvg[j], preferred_element_type=f32).astype(bf16)]
    ppermute x31 -> x32, waiting for transfers between devices: 70.7 us -> 60.6 us  [swap(): return lax.ppermute(value, axis, [(i, i ^ 1 << bit) for i in range(size)])]
    unnamed x174 -> x87, local copies, waits for them, and re-layouts: 4.2 us -> 9.36 us
    ppermute x4 -> x2, starting transfers between devices: 10.6 us -> 6.14 us  [the longest x1 4.85 us: shards(): before = lax.ppermute(jnp.concatenate([x[-WIDE:], ct[-NEAR:]]), 'seq', up)]
  transfers between devices with their start and end apart: 35 -> 34, of which waited for: 17 -> 13; matrix products, arithmetic and copies ran while one was open for 49% -> 23% of each run, Pallas kernels for 0% -> 21%
where the time goes in v2:
time: 224 us; the launch traced here: 223 us
  waiting for transfers between devices  65.5 us (29%)
  Pallas kernels  51.8 us (23%)
  starting transfers between devices  39.1 us (17%)
  local copies, waits for them, and re-layouts  27.1 us (12%)
  matrix products  22.5 us (10%)
  other arithmetic  14.8 us (7%)
    ppermute x32, waiting for transfers between devices, swap(): return lax.ppermute(value, axis, [(i, i ^ 1 << bit) for i in range(size)])  60.6 us
    ppermute x32, starting transfers between devices, swap(): return lax.ppermute(value, axis, [(i, i ^ 1 << bit) for i in range(size)])  32.9 us
    pallas_call x1, Pallas kernels, front(): pl.pallas_call(front_kernel, grid=(channels // tile,), in_specs=[SMEM] +...  13.6 us
    pallas_call x3, Pallas kernels, back(): pl.pallas_call(functools.partial(back_kernel, width=2 * channels), grid=(...  13 us
    unnamed x87, local copies, waits for them, and re-layouts  9.36 us
    dot_general x6, matrix products, shards(): jnp.dot(norm.T, dvg[j], preferred_element_type=f32).astype(bf16)  8.55 us
    concatenate x3, local copies, waits for them, and re-layouts, shards(): jnp.concatenate([jnp.dot(norm.T, dvg[j], preferred_element_type=f32).asty...  7.95 us
    pallas_call x1, Pallas kernels, depthwise(): pl.pallas_call(conv_kernel, grid=(channels // LANES,), in_specs=[columns(...  7.18 us
  transfers between devices with their start and end apart: 34, of which 13 were waited for; matrix products, arithmetic and copies ran while one was open for 23% of the time, Pallas kernels for 21%

profile of v2, /device:TPU:0, one launch (start us, length us, event | category | flops | bytes accessed | tf_op | source)
XLA Modules:
  0.0 223.0 jit_solution(2586398883256035042)
XLA Ops:
  2.8 4.9 %collective-permute-start.1 = (bf16[48,768]{1,0:T(8,128)(2,1)S(1)}, bf16[48,768]{1,0:T(8,128)(2,1)S(1)}, u32[]{:S(2)}, u32[]{:S(2)}) collective-permute-start(bf16[48,768]{1,0:T(8,128)(2,1)S(1)} %pad_maximum_fusion.14), channel_id=1, source_target_pairs={{0,4},{4,8},{8,12},{12,16},{16,20},{20,24},{24,28},{1,5},{5,9},{9,... | collective-permute-start | bytes 221192 | tf_op jit(solution)/shard_map/ppermute | solution.py:460
  9.7 4.3 %collective-permute-done.2 = bf16[48,768]{1,0:T(8,128)(2,1)S(1)} collective-permute-done((bf16[48,768]{1,0:T(8,128)(2,1)S(1)}, bf16[48,768]{1,0:T(8,128)(2,1)S(1)}, u32[]{:S(2)}, u32[]{:S(2)}) %collective-permute-start.2) | collective-permute-done | bytes 73760 | tf_op jit(solution)/shard_map/ppermute | solution.py:461
  18.9 13.6 %front.1 = (bf16[768,1536]{1,0:T(8,128)(2,1)}, f32[768,128]{1,0:T(8,128)S(1)}, bf16[832,768]{1,0:T(8,128)(2,1)S(1)}, f32[768,768]{1,0:T(8,128)}, f32[768,768]{1,0:T(8,128)}) custom-call(s32[4]{0:T(128)S(1)} %pad_add_fusion.info, bf16[768,768]{1,0:T(8,128)(2,1)S(1)} %bitcast.182, bf16[768,768]{1,0:T(8,128)(2,1)S(1)} %copy-done.15, ...), custom_call_target="tpu_custom_call" | custom-call | flops 3623878656 | bytes 20971520 | tf_op jit(solution)/shard_map/front/pallas_call | solution.py:132
  33.9 7.2 %depthwise.1 = (f32[800,768]{1,0:T(8,128)S(1)}, f32[800,128]{1,0:T(8,128)S(1)}) custom-call(bf16[832,768]{1,0:T(8,128)(2,1)S(1)} %get-tuple-element.24.hid, bf16[31,768]{1,0:T(8,128)(2,1)S(1)} %copy-done.4), custom_call_target="tpu_custom_call" | custom-call | flops 38092800 | bytes 4194304 | tf_op jit(solution)/shard_map/depthwise/pallas_call | solution.py:271
  44.8 6.7 %upstream.1 = (bf16[768,1536]{1,0:T(8,128)(2,1)S(1)}, f32[800,768]{1,0:T(8,128)}) custom-call(s32[4]{0:T(128)S(1)} %pad_add_fusion.info, bf16[768,768]{1,0:T(8,128)(2,1)S(1)} %bitcast.180, bf16[768,768]{1,0:T(8,128)(2,1)} %collective-permute-done.4.other, bf16[96,768]{1,0:T(8,128)(2,1)S(1)} %constant_dynamic-update-slice_fusion.halo_own, ...), custom_call_target="tpu_custom_call" | custom-call | flops 1811939328 | bytes 10485760 | tf_op jit(solution)/shard_map/upstream/pallas_call | solution.py:185
  51.5 4.9 %swish.1 = (bf16[800,768]{1,0:T(8,128)(2,1)S(1)}, f32[800,768]{1,0:T(8,128)S(1)}, f32[800,128]{1,0:T(8,128)S(1)}) custom-call(f32[800,768]{1,0:T(8,128)} %copy-done, f32[800,768]{1,0:T(8,128)} %get-tuple-element.26.pull, f32[800,128]{1,0:T(8,128)S(1)} %get-tuple-element.27.own, f32[800,128]{1,0:T(8,128)S(1)} %collective-permute-done.5.other), custom_call_target="tpu_custom_call" | custom-call | flops 12288000 | bytes 9437184 | tf_op jit(solution)/shard_map/swish/pallas_call | solution.py:313
  60.4 2.5 %collective-permute-start.27 = (bf16[768,256]{1,0:T(8,128)(2,1)S(1)}, bf16[768,256]{1,0:T(8,128)(2,1)S(1)}, u32[]{:S(2)}, u32[]{:S(2)}) collective-permute-start(bf16[768,256]{1,0:T(8,128)(2,1)S(1)} %bitcast.201), channel_id=1, source_target_pairs={{0,4},{4,0},{8,12},{12,8},{16,20},{20,16},{24,28},{28,24},{1,5},{5... | collective-permute-start | bytes 1179656 | tf_op jit(solution)/shard_map/ppermute | solution.py:20
  67.2 3.0 %collective-permute-done.24 = bf16[768,256]{1,0:T(8,128)(2,1)S(1)} collective-permute-done((bf16[768,256]{1,0:T(8,128)(2,1)S(1)}, bf16[768,256]{1,0:T(8,128)(2,1)S(1)}, u32[]{:S(2)}, u32[]{:S(2)}) %collective-permute-start.24) | collective-permute-done | bytes 393248 | tf_op jit(solution)/shard_map/ppermute | solution.py:20
  70.3 2.5 %collective-permute-start.25 = (bf16[384,256]{1,0:T(8,128)(2,1)S(1)}, bf16[384,256]{1,0:T(8,128)(2,1)}, u32[]{:S(2)}, u32[]{:S(2)}) collective-permute-start(bf16[384,256]{1,0:T(8,128)(2,1)S(1)} %bitcast.209), channel_id=1, source_target_pairs={{0,4},{4,0},{8,12},{12,8},{16,20},{20,16},{24,28},{28,24},{1,5},{5... | collective-permute-start | bytes 589832 | tf_op jit(solution)/shard_map/ppermute | solution.py:20
  77.7 4.4 %back.5 = (bf16[800,256]{1,0:T(8,128)(2,1)S(1)}, bf16[2,768,256]{2,1,0:T(8,128)(2,1)S(1)}) custom-call(s32[4]{0:T(128)S(1)} %pad_add_fusion.info, f32[800,768]{1,0:T(8,128)} %copy-done.1, f32[800,768]{1,0:T(8,128)} %copy-done, f32[800,128]{1,0:T(8,128)S(1)} %get-tuple-element.27.own, f32[800,128]{1,0:T(8,128)S(1)} %collective-permute-done.5.other, ...), custom_call_target="tpu_custom_call" | custom-call | flops 13762560 | bytes 5242880 | tf_op jit(solution)/shard_map/back/pallas_call | solution.py:373
  83.7 4.4 %back.4 = (bf16[800,256]{1,0:T(8,128)(2,1)S(1)}, bf16[2,768,256]{2,1,0:T(8,128)(2,1)S(1)}) custom-call(s32[4]{0:T(128)S(1)} %pad_add_fusion.info, f32[800,768]{1,0:T(8,128)} %copy-done.1, f32[800,768]{1,0:T(8,128)} %copy-done, f32[800,128]{1,0:T(8,128)S(1)} %get-tuple-element.27.own, f32[800,128]{1,0:T(8,128)S(1)} %collective-permute-done.5.other, ...), custom_call_target="tpu_custom_call" | custom-call | flops 13762560 | bytes 5242880 | tf_op jit(solution)/shard_map/back/pallas_call | solution.py:373
  92.7 4.2 %back.3 = (bf16[800,256]{1,0:T(8,128)(2,1)S(1)}, bf16[2,768,256]{2,1,0:T(8,128)(2,1)S(1)}) custom-call(s32[4]{0:T(128)S(1)} %pad_add_fusion.info, f32[800,768]{1,0:T(8,128)} %copy-done.1, f32[800,768]{1,0:T(8,128)} %copy-done, f32[800,128]{1,0:T(8,128)S(1)} %get-tuple-element.27.own, f32[800,128]{1,0:T(8,128)S(1)} %collective-permute-done.5.other, ...), custom_call_target="tpu_custom_call" | custom-call | flops 13762560 | bytes 5242880 | tf_op jit(solution)/shard_map/back/pallas_call | solution.py:373
  104.8 2.6 %copy.29 = bf16[1536,512]{1,0:T(8,128)(2,1)} copy(bf16[1536,512]{0,1:T(8,128)(2,1)} %pad_maximum_fusion.2) | data formatting | bytes 3145728 | tf_op jit(solution)/shard_map/concatenate | solution.py:485
  116.1 2.7 %copy.24 = bf16[1536,512]{1,0:T(8,128)(2,1)} copy(bf16[1536,512]{0,1:T(8,128)(2,1)} %pad_maximum_fusion.1) | data formatting | bytes 3145728 | tf_op jit(solution)/shard_map/concatenate | solution.py:485
  121.2 2.7 %copy.23 = bf16[1536,512]{1,0:T(8,128)(2,1)} copy(bf16[1536,512]{0,1:T(8,128)(2,1)} %pad_maximum_fusion) | data formatting | bytes 3145728 | tf_op jit(solution)/shard_map/concatenate | solution.py:485
  123.9 2.5 %fusion.11 = f32[768,768]{1,0:T(8,128)S(1)} fusion(bf16[1536,768]{1,0:T(8,128)(2,1)} %wv.1, s32[]{:T(128)S(6)} %select_n.82, bf16[768,256]{1,0:T(8,128)(2,1)S(1)} %copy-done.34, bf16[768,256]{1,0:T(8,128)(2,1)S(1)} %copy-done.35, bf16[768,256]{1,0:T(8,128)(2,1)S(1)} %copy-done.37), kind=kOutput, calls=%fused_computation.32 | convolution fusion | flops 909508608 | bytes 4718596 | tf_op jit(solution)/shard_map/dot_general | solution.py:515
  140.4 10.5 %collective-permute-done.26 = bf16[192,256]{1,0:T(8,128)(2,1)S(1)} collective-permute-done((bf16[192,256]{1,0:T(8,128)(2,1)S(1)}, bf16[192,256]{1,0:T(8,128)(2,1)S(1)}, u32[]{:S(2)}, u32[]{:S(2)}) %collective-permute-start.26) | collective-permute-done | bytes 98336 | tf_op jit(solution)/shard_map/ppermute | solution.py:20
  157.0 3.1 %collective-permute-start.23 = (f32[31,768]{1,0:T(8,128)S(1)}, f32[31,768]{1,0:T(8,128)S(1)}, u32[]{:S(2)}, u32[]{:S(2)}) collective-permute-start(f32[31,768]{1,0:T(8,128)S(1)} %add.207), channel_id=1, source_target_pairs={{0,16},{4,20},{8,24},{12,28},{16,0},{20,4},{24,8},{28,12},{1,17},{... | collective-permute-start | bytes 285704 | tf_op jit(solution)/shard_map/ppermute | solution.py:20
  160.3 6.0 %collective-permute-done.23 = f32[31,768]{1,0:T(8,128)S(1)} collective-permute-done((f32[31,768]{1,0:T(8,128)S(1)}, f32[31,768]{1,0:T(8,128)S(1)}, u32[]{:S(2)}, u32[]{:S(2)}) %collective-permute-start.23) | collective-permute-done | bytes 95264 | tf_op jit(solution)/shard_map/ppermute | solution.py:20
  168.7 3.5 %fusion.8 = bf16[1,768,768]{2,1,0:T(8,128)(2,1)} fusion(bf16[768,768]{1,0:T(8,128)(2,1)} %collective-permute-done.6, bf16[768,1536]{1,0:T(8,128)(2,1)S(1)} %copy-done.41, s32[]{:T(128)S(6)} %select_n.81, bf16[800,768]{1,0:T(8,128)(2,1)S(1)} %copy-done.13, bf16[1,768,768]{2,1,0:T(8,128)(2,1)S(1)} %copy-done.11), kind=kOutput, calls=%fused_computation.27 | convolution fusion | flops 908918784 | bytes 5898244 | tf_op jit(solution)/shard_map/dot_general | solution.py:508
  175.4 11.3 %collective-permute-done.13 = bf16[768,512]{1,0:T(8,128)(2,1)S(1)} collective-permute-done((bf16[768,512]{1,0:T(8,128)(2,1)S(1)}, bf16[768,512]{1,0:T(8,128)(2,1)S(1)}, u32[]{:S(2)}, u32[]{:S(2)}) %collective-permute-start.13) | collective-permute-done | bytes 786464 | tf_op jit(solution)/shard_map/ppermute | solution.py:20
  188.4 6.2 %collective-permute-done.11 = bf16[384,512]{1,0:T(8,128)(2,1)S(1)} collective-permute-done((bf16[384,512]{1,0:T(8,128)(2,1)S(1)}, bf16[384,512]{1,0:T(8,128)(2,1)S(1)}, u32[]{:S(2)}, u32[]{:S(2)}) %collective-permute-start.11) | collective-permute-done | bytes 393248 | tf_op jit(solution)/shard_map/ppermute | solution.py:20
  200.5 5.6 %collective-permute-done.15 = bf16[192,512]{1,0:T(8,128)(2,1)S(1)} collective-permute-done((bf16[192,512]{1,0:T(8,128)(2,1)S(1)}, bf16[192,512]{1,0:T(8,128)(2,1)S(1)}, u32[]{:S(2)}, u32[]{:S(2)}) %collective-permute-start.15) | collective-permute-done | bytes 196640 | tf_op jit(solution)/shard_map/ppermute | solution.py:20
  208.9 13.1 %collective-permute-done.19 = bf16[96,1536]{1,0:T(8,128)(2,1)S(1)} collective-permute-done((bf16[96,1536]{1,0:T(8,128)(2,1)S(1)}, bf16[96,1536]{1,0:T(8,128)(2,1)S(1)}, u32[]{:S(2)}, u32[]{:S(2)}) %collective-permute-start.19) | collective-permute-done | bytes 294944 | tf_op jit(solution)/shard_map/ppermute | solution.py:20
  (229 shorter events, 88.6 us)
Async XLA Ops:
  0.6 14.7 %collective-permute-start = (bf16[768,768]{1,0:T(8,128)(2,1)}, bf16[768,768]{1,0:T(8,128)(2,1)S(1)}, u32[]{:S(2)}, u32[]{:S(2)}) collective-permute-start(bf16[768,768]{1,0:T(8,128)(2,1)} %bitcast.181), channel_id=1, source_target_pairs={{0,2},{2,0},{1,3},{3,1},{4,6},{6,4},{5,7},{7,5},{8,10},{10,8},{9,1... | collective-permute-start | bytes 3538952 | tf_op jit(solution)/shard_map/ppermute | solution.py:20
  1.1 42.7 %collective-permute-start.4 = (bf16[768,768]{1,0:T(8,128)(2,1)}, bf16[768,768]{1,0:T(8,128)(2,1)}, u32[]{:S(2)}, u32[]{:S(2)}) collective-permute-start(bf16[768,768]{1,0:T(8,128)(2,1)} %bitcast.179), channel_id=1, source_target_pairs={{0,2},{2,0},{1,3},{3,1},{4,6},{6,4},{5,7},{7,5},{8,10},{10,8},{9,1... | collective-permute-start | bytes 3538952 | tf_op jit(solution)/shard_map/ppermute | solution.py:20
  58.7 11.4 %collective-permute-start.24 = (bf16[768,256]{1,0:T(8,128)(2,1)S(1)}, bf16[768,256]{1,0:T(8,128)(2,1)S(1)}, u32[]{:S(2)}, u32[]{:S(2)}) collective-permute-start(bf16[768,256]{1,0:T(8,128)(2,1)S(1)} %bitcast.208), channel_id=1, source_target_pairs={{0,1},{1,0},{2,3},{3,2},{4,5},{5,4},{6,7},{7,6},{8,9},{9,8},{10,11... | collective-permute-start | bytes 1179656 | tf_op jit(solution)/shard_map/ppermute | solution.py:20
  60.4 12.5 %collective-permute-start.27 = (bf16[768,256]{1,0:T(8,128)(2,1)S(1)}, bf16[768,256]{1,0:T(8,128)(2,1)S(1)}, u32[]{:S(2)}, u32[]{:S(2)}) collective-permute-start(bf16[768,256]{1,0:T(8,128)(2,1)S(1)} %bitcast.201), channel_id=1, source_target_pairs={{0,4},{4,0},{8,12},{12,8},{16,20},{20,16},{24,28},{28,24},{1,5},{5... | collective-permute-start | bytes 1179656 | tf_op jit(solution)/shard_map/ppermute | solution.py:20
  62.9 12.3 %collective-permute-start.30 = (bf16[768,256]{1,0:T(8,128)(2,1)S(1)}, bf16[768,256]{1,0:T(8,128)(2,1)S(1)}, u32[]{:S(2)}, u32[]{:S(2)}) collective-permute-start(bf16[768,256]{1,0:T(8,128)(2,1)S(1)} %bitcast.199), channel_id=1, source_target_pairs={{0,8},{4,12},{8,0},{12,4},{16,24},{20,28},{24,16},{28,20},{1,9},{5... | collective-permute-start | bytes 1179656 | tf_op jit(solution)/shard_map/ppermute | solution.py:20
  64.6 13.1 %collective-permute-start.7 = (f32[800,128]{1,0:T(8,128)S(1)}, f32[800,128]{1,0:T(8,128)S(1)}, u32[]{:S(2)}, u32[]{:S(2)}) collective-permute-start(f32[800,128]{1,0:T(8,128)S(1)} %get-tuple-element.31.own2), channel_id=1, source_target_pairs={{0,2},{2,0},{1,3},{3,1},{4,6},{6,4},{5,7},{7,5},{8,10},{10,8},{9,1... | collective-permute-start | bytes 1228808 | tf_op jit(solution)/shard_map/ppermute | solution.py:20
  66.7 102.0 %collective-permute-start.6 = (bf16[768,768]{1,0:T(8,128)(2,1)}, bf16[768,768]{1,0:T(8,128)(2,1)}, u32[]{:S(2)}, u32[]{:S(2)}) collective-permute-start(bf16[768,768]{1,0:T(8,128)(2,1)} %convolution_convert_fusion.7), channel_id=1, source_target_pairs={{0,2},{2,0},{1,3},{3,1},{4,6},{6,4},{5,7},{7,5},{8,10},{10,8},{9,1... | collective-permute-start | bytes 3538952 | tf_op jit(solution)/shard_map/ppermute | solution.py:20
  70.3 61.9 %collective-permute-start.25 = (bf16[384,256]{1,0:T(8,128)(2,1)S(1)}, bf16[384,256]{1,0:T(8,128)(2,1)}, u32[]{:S(2)}, u32[]{:S(2)}) collective-permute-start(bf16[384,256]{1,0:T(8,128)(2,1)S(1)} %bitcast.209), channel_id=1, source_target_pairs={{0,4},{4,0},{8,12},{12,8},{16,20},{20,16},{24,28},{28,24},{1,5},{5... | collective-permute-start | bytes 589832 | tf_op jit(solution)/shard_map/ppermute | solution.py:20
  73.7 61.1 %collective-permute-start.28 = (bf16[384,256]{1,0:T(8,128)(2,1)}, bf16[384,256]{1,0:T(8,128)(2,1)}, u32[]{:S(2)}, u32[]{:S(2)}) collective-permute-start(bf16[384,256]{1,0:T(8,128)(2,1)} %bitcast.63), channel_id=1, source_target_pairs={{0,8},{4,12},{8,0},{12,4},{16,24},{20,28},{24,16},{28,20},{1,9},{5... | collective-permute-start | bytes 589832 | tf_op jit(solution)/shard_map/ppermute | solution.py:20
  76.2 60.4 %collective-permute-start.31 = (bf16[384,256]{1,0:T(8,128)(2,1)}, bf16[384,256]{1,0:T(8,128)(2,1)}, u32[]{:S(2)}, u32[]{:S(2)}) collective-permute-start(bf16[384,256]{1,0:T(8,128)(2,1)} %bitcast.73), channel_id=1, source_target_pairs={{0,1},{1,0},{2,3},{3,2},{4,5},{5,4},{6,7},{7,6},{8,9},{9,8},{10,11... | collective-permute-start | bytes 589832 | tf_op jit(solution)/shard_map/ppermute | solution.py:20
  114.2 15.8 %collective-permute-start.20 = (f32[31,768]{1,0:T(8,128)S(1)}, f32[31,768]{1,0:T(8,128)}, u32[]{:S(2)}, u32[]{:S(2)}) collective-permute-start(f32[31,768]{1,0:T(8,128)S(1)} %pad_maximum_fusion.13), channel_id=1, source_target_pairs={{0,1},{1,0},{2,3},{3,2},{4,5},{5,4},{6,7},{7,6},{8,9},{9,8},{10,11... | collective-permute-start | bytes 285704 | tf_op jit(solution)/shard_map/ppermute | solution.py:20
  130.9 41.3 %collective-permute-start.16 = (bf16[768,512]{1,0:T(8,128)(2,1)S(1)}, bf16[768,512]{1,0:T(8,128)(2,1)S(1)}, u32[]{:S(2)}, u32[]{:S(2)}) collective-permute-start(bf16[768,512]{1,0:T(8,128)(2,1)S(1)} %bitcast.193), channel_id=1, source_target_pairs={{0,8},{4,12},{8,0},{12,4},{16,24},{20,28},{24,16},{28,20},{1,9},{5... | collective-permute-start | bytes 2359304 | tf_op jit(solution)/shard_map/ppermute | solution.py:20
  132.2 41.8 %collective-permute-start.10 = (bf16[768,512]{1,0:T(8,128)(2,1)S(1)}, bf16[768,512]{1,0:T(8,128)(2,1)S(1)}, u32[]{:S(2)}, u32[]{:S(2)}) collective-permute-start(bf16[768,512]{1,0:T(8,128)(2,1)S(1)} %bitcast.192), channel_id=1, source_target_pairs={{0,1},{1,0},{2,3},{3,2},{4,5},{5,4},{6,7},{7,6},{8,9},{9,8},{10,11... | collective-permute-start | bytes 2359304 | tf_op jit(solution)/shard_map/ppermute | solution.py:20
  136.5 14.3 %collective-permute-start.26 = (bf16[192,256]{1,0:T(8,128)(2,1)S(1)}, bf16[192,256]{1,0:T(8,128)(2,1)S(1)}, u32[]{:S(2)}, u32[]{:S(2)}) collective-permute-start(bf16[192,256]{1,0:T(8,128)(2,1)S(1)} %bitcast.218), channel_id=1, source_target_pairs={{0,8},{4,12},{8,0},{12,4},{16,24},{20,28},{24,16},{28,20},{1,9},{5... | collective-permute-start | bytes 294920 | tf_op jit(solution)/shard_map/ppermute | solution.py:20
  139.5 12.5 %collective-permute-start.29 = (bf16[192,256]{1,0:T(8,128)(2,1)S(1)}, bf16[192,256]{1,0:T(8,128)(2,1)S(1)}, u32[]{:S(2)}, u32[]{:S(2)}) collective-permute-start(bf16[192,256]{1,0:T(8,128)(2,1)S(1)} %bitcast.216), channel_id=1, source_target_pairs={{0,1},{1,0},{2,3},{3,2},{4,5},{5,4},{6,7},{7,6},{8,9},{9,8},{10,11... | collective-permute-start | bytes 294920 | tf_op jit(solution)/shard_map/ppermute | solution.py:20
  155.6 12.3 %collective-permute-start.33 = (bf16[96,768]{1,0:T(8,128)(2,1)S(1)}, bf16[96,768]{1,0:T(8,128)(2,1)S(1)}, u32[]{:S(2)}, u32[]{:S(2)}) collective-permute-start(bf16[96,768]{1,0:T(8,128)(2,1)S(1)} %dynamic-slice_bitcast_fusion.1), channel_id=1, source_target_pairs={{0,16},{4,20},{8,24},{12,28},{16,0},{20,4},{24,8},{28,12},{1,17},{... | collective-permute-start | bytes 442376 | tf_op jit(solution)/shard_map/ppermute | solution.py:20
  157.0 9.2 %collective-permute-start.23 = (f32[31,768]{1,0:T(8,128)S(1)}, f32[31,768]{1,0:T(8,128)S(1)}, u32[]{:S(2)}, u32[]{:S(2)}) collective-permute-start(f32[31,768]{1,0:T(8,128)S(1)} %add.207), channel_id=1, source_target_pairs={{0,16},{4,20},{8,24},{12,28},{16,0},{20,4},{24,8},{28,12},{1,17},{... | collective-permute-start | bytes 285704 | tf_op jit(solution)/shard_map/ppermute | solution.py:20
  166.2 20.5 %collective-permute-start.13 = (bf16[768,512]{1,0:T(8,128)(2,1)S(1)}, bf16[768,512]{1,0:T(8,128)(2,1)S(1)}, u32[]{:S(2)}, u32[]{:S(2)}) collective-permute-start(bf16[768,512]{1,0:T(8,128)(2,1)S(1)} %bitcast.195), channel_id=1, source_target_pairs={{0,4},{4,0},{8,12},{12,8},{16,20},{20,16},{24,28},{28,24},{1,5},{5... | collective-permute-start | bytes 2359304 | tf_op jit(solution)/shard_map/ppermute | solution.py:20
  167.9 29.1 %collective-permute-start.8 = (bf16[768,768]{1,0:T(8,128)(2,1)S(1)}, bf16[768,768]{1,0:T(8,128)(2,1)S(1)}, u32[]{:S(2)}, u32[]{:S(2)}) collective-permute-start(bf16[768,768]{1,0:T(8,128)(2,1)S(1)} %add_convert_fusion), channel_id=1, source_target_pairs={{0,2},{2,0},{1,3},{3,1},{4,6},{6,4},{5,7},{7,5},{8,10},{10,8},{9,1... | collective-permute-start | bytes 3538952 | tf_op jit(solution)/shard_map/ppermute | solution.py:20
  172.5 14.6 %collective-permute-start.17 = (bf16[384,512]{1,0:T(8,128)(2,1)S(1)}, bf16[384,512]{1,0:T(8,128)(2,1)S(1)}, u32[]{:S(2)}, u32[]{:S(2)}) collective-permute-start(bf16[384,512]{1,0:T(8,128)(2,1)S(1)} %bitcast.197), channel_id=1, source_target_pairs={{0,1},{1,0},{2,3},{3,2},{4,5},{5,4},{6,7},{7,6},{8,9},{9,8},{10,11... | collective-permute-start | bytes 1179656 | tf_op jit(solution)/shard_map/ppermute | solution.py:20
  174.3 20.3 %collective-permute-start.11 = (bf16[384,512]{1,0:T(8,128)(2,1)S(1)}, bf16[384,512]{1,0:T(8,128)(2,1)S(1)}, u32[]{:S(2)}, u32[]{:S(2)}) collective-permute-start(bf16[384,512]{1,0:T(8,128)(2,1)S(1)} %bitcast.206), channel_id=1, source_target_pairs={{0,4},{4,0},{8,12},{12,8},{16,20},{20,16},{24,28},{28,24},{1,5},{5... | collective-permute-start | bytes 1179656 | tf_op jit(solution)/shard_map/ppermute | solution.py:20
  187.0 9.9 %collective-permute-start.14 = (bf16[384,512]{1,0:T(8,128)(2,1)S(1)}, bf16[384,512]{1,0:T(8,128)(2,1)S(1)}, u32[]{:S(2)}, u32[]{:S(2)}) collective-permute-start(bf16[384,512]{1,0:T(8,128)(2,1)S(1)} %bitcast.198), channel_id=1, source_target_pairs={{0,8},{4,12},{8,0},{12,4},{16,24},{20,28},{24,16},{28,20},{1,9},{5... | collective-permute-start | bytes 1179656 | tf_op jit(solution)/shard_map/ppermute | solution.py:20
  187.3 13.1 %collective-permute-start.18 = (bf16[192,512]{1,0:T(8,128)(2,1)S(1)}, bf16[192,512]{1,0:T(8,128)(2,1)S(1)}, u32[]{:S(2)}, u32[]{:S(2)}) collective-permute-start(bf16[192,512]{1,0:T(8,128)(2,1)S(1)} %bitcast.210), channel_id=1, source_target_pairs={{0,4},{4,0},{8,12},{12,8},{16,20},{20,16},{24,28},{28,24},{1,5},{5... | collective-permute-start | bytes 589832 | tf_op jit(solution)/shard_map/ppermute | solution.py:20
  206.3 15.7 %collective-permute-start.19 = (bf16[96,1536]{1,0:T(8,128)(2,1)S(1)}, bf16[96,1536]{1,0:T(8,128)(2,1)S(1)}, u32[]{:S(2)}, u32[]{:S(2)}) collective-permute-start(bf16[96,1536]{1,0:T(8,128)(2,1)S(1)} %dynamic-slice_bitcast_fusion), channel_id=1, source_target_pairs={{0,16},{4,20},{8,24},{12,28},{16,0},{20,4},{24,8},{28,12},{1,17},{... | collective-permute-start | bytes 884744 | tf_op jit(solution)/shard_map/ppermute | solution.py:20
  (53 other events, 244.3 us)

commit v3 on v0

v3 whole, which is shorter than its diff:
```python
import functools

import jax
import jax.numpy as jnp
from jax import lax
from jax.experimental import pallas as pl
from jax.experimental.pallas import tpu as pltpu
from jax.sharding import PartitionSpec as P

epsilon = 1e-05
f32, bf16 = jnp.float32, jnp.bfloat16
LANES = 128
WIDE, NEAR = 32, 16
NN = (((1,), (0,)), ((), ()))
NT = (((1,), (1,)), ((), ()))
TN = (((0,), (0,)), ((), ()))
VMEM = pl.BlockSpec(memory_space=pltpu.VMEM)
SMEM = pl.BlockSpec(memory_space=pltpu.SMEM)
ANY = pl.BlockSpec(memory_space=pl.ANY)


def dot(a, b, dims=NN):
    return lax.dot_general(a, b, dims, preferred_element_type=f32)


def run(kernel, info, args, outs, scratch=(), after=(), limit=16):
    def body(*refs):
        lead = 1 + len(args)
        kernel(*refs[:lead], *refs[lead + len(after) :])

    return pl.pallas_call(
        body,
        in_specs=[SMEM] + [VMEM] * len(args) + [ANY] * len(after),
        out_specs=[VMEM] * len(outs),
        out_shape=[pltpu.VMEM(shape, dtype) for shape, dtype in outs],
        scratch_shapes=list(scratch),
        compiler_params=pltpu.CompilerParams(vmem_limit_bytes=limit << 20),
        cost_estimate=pl.CostEstimate(flops=COST, bytes_accessed=COST, transcendentals=0),
        name=kernel.__name__ if hasattr(kernel, "__name__") else kernel.func.__name__,
    )(info, *[pltpu.with_memory_space_constraint(a, pltpu.VMEM) for a in args], *after)


COST = 1 << 12


def swap(value, axis, bit=0):
    size = lax.axis_size(axis)
    return lax.ppermute(value, axis, [(i, i ^ (1 << bit)) for i in range(size)])


def bits_of(axis):
    return [(axis, b) for b in range(lax.axis_size(axis).bit_length() - 1)]


def every_bit():
    return bits_of("dp") + bits_of("seq")


class Halver:
    def __init__(self, keep, send, bit, rows):
        self.bits = every_bit()[::-1]
        self.rows = rows
        self.merge(keep, send, bit)

    def merge(self, keep, send, bit):
        got = swap(send, *bit)
        value = keep.astype(f32) + got.astype(f32)
        self.bits.remove(bit)
        if self.bits:
            value = value.astype(bf16)
        self.value = value.reshape((2,) * len(self.bits) + (self.rows, value.shape[-1]))

    def step(self, bit):
        dim = self.bits.index(bit)
        mine = (lax.axis_index(bit[0]) >> bit[1]) & 1
        columns = self.value.shape[-1]
        send = lax.dynamic_index_in_dim(self.value, 1 - mine, dim, keepdims=False)
        keep = lax.dynamic_index_in_dim(self.value, mine, dim, keepdims=False)
        self.merge(keep.reshape(-1, columns), send.reshape(-1, columns), bit)


def scatter_sum(halves, rows):
    every = every_bit()
    turning, rest = every[:3], every[3:]
    thirds = [Halver(*half, turning[i], rows) for i, half in enumerate(halves)]
    for phase in range(1, len(turning)):
        for i, third in enumerate(thirds):
            third.step(turning[(i + phase) % len(turning)])
    merged = thirds[0]
    merged.value = jnp.concatenate([t.value for t in thirds], axis=-1)
    for bit in rest:
        merged.step(bit)
    return merged.value


def store_halves(info, bit, start, value, keep, send, rows):
    for mine in (0, 1):

        @pl.when(info[4 + bit] == mine)
        def _():
            for r in range(0, value.shape[0], rows):
                block = (start + r) // rows
                to = ((block >> (bit + 1)) << bit) | (block & ((1 << bit) - 1))
                target = keep if (block >> bit) & 1 == mine else send
                target[to * rows : (to + 1) * rows, :] = value[r : r + rows, :]


def row_mask(info, first, rows, limit):
    place = info[0] + first + lax.broadcasted_iota(jnp.int32, (rows, 1), 0)
    return ((place >= 0) & (place < limit)).astype(f32)


def halves_at(info, half):
    return (
        pl.multiple_of(info[3] * half, half),
        pl.multiple_of((1 - info[3]) * half, half),
    )


def upstream(info, own, other, w_out, full, pull):
    count, half = own.shape
    mine, theirs = halves_at(info, half)
    full[:, pl.ds(mine, half)] = own[...]
    full[:, pl.ds(theirs, half)] = other[...]
    step = count // 2
    for c in range(0, count, step):
        pull[c : c + step, :] = dot(full[c : c + step, :], w_out[...], NT)


def front(info, own, other, halo_own, halo_other, wv, wg, w_out, norm, rstd, hid, sig, slope, ends, edge):
    count, half = own.shape
    channels = wv.shape[1]
    mine, theirs = halves_at(info, half)

    def normalize(to, a, b):
        a, b = a.astype(f32), b.astype(f32)
        width = 2 * half
        mean = (jnp.sum(a, 1, keepdims=True) + jnp.sum(b, 1, keepdims=True)) / width
        a, b = a - mean, b - mean
        var = jnp.sum(a * a, 1, keepdims=True) + jnp.sum(b * b, 1, keepdims=True)
        inverse = lax.rsqrt(var / width + epsilon)
        norm[to, pl.ds(mine, half)] = (a * inverse).astype(bf16)
        norm[to, pl.ds(theirs, half)] = (b * inverse).astype(bf16)
        return inverse

    chunk = 64

    def body(i, _):
        at = pl.multiple_of(i * chunk, chunk)
        inverse = normalize(
            pl.ds(pl.multiple_of(WIDE + at, WIDE), chunk),
            own[pl.ds(at, chunk), :],
            other[pl.ds(at, chunk), :],
        )
        rstd[pl.ds(at, chunk), :] = jnp.broadcast_to(inverse, (chunk, LANES))
        return 0

    lax.fori_loop(0, count // chunk, body, 0)
    for to, at in ((0, 0), (WIDE + count, WIDE + NEAR)):
        normalize(pl.ds(to, WIDE), halo_own[at : at + WIDE, :], halo_other[at : at + WIDE, :])
    for a, at in ((halo_own, mine), (halo_other, theirs)):
        edge[:NEAR, pl.ds(at, half)] = a[WIDE : WIDE + NEAR, :]
        edge[NEAR:, pl.ds(at, half)] = a[2 * WIDE + NEAR :, :]
    ends[...] = dot(edge[...], w_out[...], NT)

    tile = channels // 3
    rows = count + 2 * WIDE
    step = rows // 2
    for n in range(0, channels, tile):
        cols = slice(n, n + tile)
        for c in range(0, rows, step):
            value = dot(norm[c : c + step, :], wv[:, cols])
            s = jax.nn.sigmoid(dot(norm[c : c + step, :], wg[:, cols]))
            keep = row_mask(info, c - WIDE, step, info[1])
            vs = value * s * keep
            hid[c : c + step, cols] = vs.astype(bf16)
            low, high = max(c, WIDE), min(c + step, WIDE + count)
            part = slice(low - c, high - c)
            sig[low - WIDE : high - WIDE, cols] = (s * keep)[part]
            slope[low - WIDE : high - WIDE, cols] = (vs * (1.0 - s))[part]


def tap_sums(source, base, groups, taps):
    sums = [None] * groups
    for residue in range(8):
        mine = list(range(residue, len(taps), 8))
        shifted = [
            source[pl.ds(base + 8 * i + residue, 8), :] for i in range(groups + len(mine) - 1)
        ]
        for i, k in enumerate(mine):
            for g in range(groups):
                term = shifted[g + i] * taps[k]
                sums[g] = term if sums[g] is None else sums[g] + term
    return sums


def tap_rows(taps, cols, reverse=False):
    values = taps[:, cols].astype(f32)
    order = range(taps.shape[0])
    return [
        jnp.broadcast_to(values[k : k + 1, :], (8, LANES))
        for k in (reversed(order) if reverse else order)
    ]


def lane_tile(n):
    return pl.ds(pl.multiple_of(n * LANES, LANES), LANES)


def paired(first, second):
    lane = lax.broadcasted_iota(jnp.int32, (first.shape[0], LANES), 1)
    return jnp.where(
        lane < LANES // 2,
        jnp.sum(first, axis=1, keepdims=True),
        jnp.sum(second, axis=1, keepdims=True),
    )


def depthwise(info, hid, taps, conv, stats, scratch, total, square):
    rows = conv.shape[0]
    skip = WIDE - NEAR - (taps.shape[0] - 1) // 2
    groups = 20
    total[...] = jnp.zeros_like(total)
    square[...] = jnp.zeros_like(square)

    def tile(n, _):
        cols = lane_tile(n)
        scratch[: hid.shape[0], :] = hid[:, cols].astype(f32)
        weights = tap_rows(taps, cols)

        def body(i, _):
            base = pl.multiple_of(i * 8 * groups, 8)
            for g, value in enumerate(tap_sums(scratch, base + skip, groups, weights)):
                at = pl.ds(base + 8 * g, 8)
                conv[at, cols] = value
                total[at, :] += value
                square[at, :] += value * value
            return 0

        lax.fori_loop(0, rows // (8 * groups), body, 0)
        return 0

    lax.fori_loop(0, conv.shape[1] // LANES, tile, 0)
    stats[...] = paired(total[...], square[...])


def moments(first, second, width):
    mean = (first[:, :1] + second[:, :1]) / width
    half = LANES // 2
    square = (first[:, half : half + 1] + second[:, half : half + 1]) / width
    return mean, lax.rsqrt(square - mean * mean + epsilon)


def swish(info, conv, pull, ends, own, other, swished, dswish, stats):
    count, channels = pull.shape

    def part(at, g, rows):
        to = pl.ds(at, rows)
        mean, inverse = moments(own[to, :], other[to, :], 2 * channels)
        zhat = (conv[to, :] - mean) * inverse
        s = jax.nn.sigmoid(zhat)
        zs = zhat * s
        d = g * (s + zs * (1.0 - s))
        dswish[to, :] = d
        stats[to, :] = paired(d, d * zhat)
        return zs.astype(bf16)

    part(0, ends[:NEAR, :], NEAR)
    part(NEAR + count, ends[NEAR:, :], NEAR)
    step = 32

    def body(i, _):
        at = pl.multiple_of(i * step, step)
        rows = pl.ds(at, step)
        swished[rows, :] = part(pl.multiple_of(at + NEAR, NEAR), pull[rows, :], step)
        return 0

    lax.fori_loop(0, count // step, body, 0)


def out_terms(info, full, swished, *halves, rows):
    width = full.shape[1]
    cols = swished.shape[1] // 3
    step = width // 4
    for i in range(3):
        for c in range(0, width, step):
            r = dot(full[:, c : c + step], swished[:, i * cols : (i + 1) * cols], TN)
            store_halves(info, i, c, r.astype(bf16), halves[2 * i], halves[2 * i + 1], rows)


def back(info, dswish, conv, own, other, own2, other2, taps, sig, slope, norm, dconv, dvg, keep, send, scratch, coef, *, third, block):
    rows, channels = dswish.shape
    count = sig.shape[0]
    width = 2 * channels
    mean, inverse = moments(own[...], other[...], width)
    half = LANES // 2
    shift = (own2[:, :1] + other2[:, :1]) / width
    cross = (own2[:, half : half + 1] + other2[:, half : half + 1]) / width
    inverse = inverse * row_mask(info, -NEAR, rows, info[2])
    tilt = inverse * inverse * cross
    coef[0] = jnp.broadcast_to(inverse, (rows, LANES))
    coef[1] = jnp.broadcast_to(tilt, (rows, LANES))
    coef[2] = jnp.broadcast_to(tilt * mean - inverse * shift, (rows, LANES))
    tiles = channels // LANES // 3
    groups = 16
    skip = NEAR - (taps.shape[0] - 1) // 2

    def tile(n, _):
        local = lane_tile(n)
        cols = lane_tile(third * tiles + n)
        d = (coef[0] * dswish[:, cols] - coef[1] * conv[:, cols] + coef[2]).astype(bf16)
        dconv[:, local] = d
        scratch[:rows, :] = d.astype(f32)
        weights = tap_rows(taps, cols, reverse=True)

        def body(i, _):
            base = pl.multiple_of(i * 8 * groups, 16)
            sums = tap_sums(scratch, base + skip, groups, weights)
            for g in range(0, groups, 2):
                at = pl.ds(base + 8 * g, 16)
                dh = jnp.concatenate(sums[g : g + 2], axis=0)
                dvg[at, local] = (dh * sig[at, cols]).astype(bf16)
                dvg[at, lane_tile(tiles + n)] = (dh * slope[at, cols]).astype(bf16)
            return 0

        lax.fori_loop(0, count // (8 * groups), body, 0)
        return 0

    lax.fori_loop(0, tiles, tile, 0)
    step = width // 4
    for c in range(0, width, step):
        r = dot(norm[WIDE : WIDE + count, c : c + step], dvg[...], TN)
        store_halves(info, third, c, r.astype(bf16), keep, send, block)


def taps_sums(info, dconv, hid, out, scratch, total, *, third):
    rows, channels = dconv.shape
    count = rows - 2 * NEAR
    taps = out.shape[0]
    half = (taps - 1) // 2
    groups = 16
    tiles = channels // LANES

    def tile(n, _):
        local = lane_tile(n)
        cols = lane_tile(third * tiles + n)
        scratch[:rows, :] = dconv[:, local].astype(f32)
        total[...] = jnp.zeros_like(total)

        def body(i, _):
            base = pl.multiple_of(i * 8 * groups, 16)
            h = []
            for g in range(0, groups, 2):
                both = hid[pl.ds(pl.multiple_of(WIDE + base + 8 * g, 16), 16), cols].astype(f32)
                h += [both[:8], both[8:]]
            for residue in range(8):
                mine = list(range(residue, taps, 8))
                shifted = [
                    scratch[pl.ds(base + NEAR - half + 8 * g + residue, 8), :]
                    for g in range(groups + len(mine) - 1)
                ]
                for j, m in enumerate(mine):
                    term = shifted[j] * h[0]
                    for g in range(1, groups):
                        term = term + shifted[g + j] * h[g]
                    total[taps - 1 - m] += term
            return 0

        lax.fori_loop(0, count // (8 * groups), body, 0)
        out[:, local] = jnp.sum(total[...], axis=1)
        return 0

    lax.fori_loop(0, tiles, tile, 0)


def out_half(info, swished, w_out, result, *, own):
    half = result.shape[1]
    at = halves_at(info, half)[0 if own else 1]
    step = swished.shape[0] // 2
    for c in range(0, swished.shape[0], step):
        part = dot(swished[c : c + step, :], w_out[:, pl.ds(at, half)])
        result[c : c + step, :] = part.astype(result.dtype)


def norm_half(info, a, b, c, wv, wg, result, *, own):
    count, half = result.shape
    at = halves_at(info, half)[0 if own else 1]
    third = half // 3
    step = count // 2
    for r in range(0, count, step):
        total = None
        for i, dvg in enumerate((a, b, c)):
            cols = slice(i * third, (i + 1) * third)
            for j, w in enumerate((wv, wg)):
                part = dot(
                    dvg[r : r + step, j * third : (j + 1) * third], w[pl.ds(at, half), cols], NT
                )
                total = part if total is None else total + part
        result[r : r + step, :] = total.astype(result.dtype)


def norm_sums(info, mine, got, norm, total, stats):
    count, half = mine.shape
    at = halves_at(info, half)[0]
    step = 32

    def body(i, _):
        rows = pl.ds(pl.multiple_of(i * step, step), step)
        xhat = norm[pl.ds(pl.multiple_of(i * step + WIDE, step), step), pl.ds(at, half)]
        d = mine[rows, :] + got[rows, :].astype(f32)
        total[rows, :] = d
        stats[rows, :] = paired(d, d * xhat.astype(f32))
        return 0

    lax.fori_loop(0, count // step, body, 0)


def shards(inputs, lengths, cotangent, w_value, w_gate, kernel, w_out):
    x, ct = inputs[0], cotangent[0]
    count, channels = x.shape
    width = channels * lax.axis_size("tensor")
    core = lax.axis_index("tensor")
    peers = lax.axis_size("seq")
    every = every_bit()
    block = width >> len(every)
    taps = kernel.shape[0]
    info = jnp.stack(
        [lax.axis_index("seq") * count, lengths[0], jnp.int32(peers * count), core]
        + [(lax.axis_index(a) >> b) & 1 for a, b in every]
    ).astype(jnp.int32)

    up = [(i, i + 1) for i in range(peers - 1)]
    down = [(j, i) for i, j in up]
    x_other, ct_other = swap(x, "tensor"), swap(ct, "tensor")
    before = lax.ppermute(jnp.concatenate([x[-WIDE:], ct[-NEAR:]]), "seq", up)
    after = lax.ppermute(jnp.concatenate([x[:WIDE], ct[:NEAR]]), "seq", down)
    halo = jnp.concatenate([before, after])
    halo_other = swap(halo, "tensor")

    rows, ext = count + 2 * NEAR, count + 2 * WIDE
    full, pull = run(
        upstream, info, [ct, ct_other, w_out], [((count, width), bf16), ((count, channels), f32)]
    )
    norm, rstd, hid, sig, slope, ends = run(
        front,
        info,
        [x, x_other, halo, halo_other, w_value, w_gate, w_out],
        [
            ((ext, width), bf16),
            ((count, LANES), f32),
            ((ext, channels), bf16),
            ((count, channels), f32),
            ((count, channels), f32),
            ((2 * NEAR, channels), f32),
        ],
        scratch=[pltpu.VMEM((2 * NEAR, width), bf16)],
        after=[pull],
    )
    row_sums = ((rows, LANES), f32)
    column = pltpu.VMEM((rows, LANES), f32)
    conv, stats = run(
        depthwise,
        info,
        [hid, kernel],
        [((rows, channels), f32), row_sums],
        scratch=[pltpu.VMEM((ext + 16, LANES), f32), column, column],
    )
    stats_other = swap(stats, "tensor")
    swished, dswish, stats2 = run(
        swish,
        info,
        [conv, pull, ends, stats, stats_other],
        [((count, channels), bf16), ((rows, channels), f32), row_sums],
    )
    stats2_other = swap(stats2, "tensor")

    third = channels // 3
    half_block = (width // 2, third)
    halves = run(
        functools.partial(out_terms, rows=block), info, [full, swished], [(half_block, bf16)] * 6
    )
    out_grad = scatter_sum([(halves[2 * i], halves[2 * i + 1]) for i in range(3)], block).T

    dconvs, dvgs, halves = [], [], []
    last = halves
    for i in range(3):
        dconv, dvg, keep, send = run(
            functools.partial(back, third=i, block=block),
            info,
            [dswish, conv, stats, stats_other, stats2, stats2_other, kernel, sig, slope, norm],
            [
                ((rows, third), bf16),
                ((count, 2 * third), bf16),
                ((width // 2, 2 * third), bf16),
                ((width // 2, 2 * third), bf16),
            ],
            scratch=[pltpu.VMEM((rows + 16, LANES), f32), pltpu.VMEM((3, rows, LANES), f32)],
            after=last,
        )
        last = [send]
        dconvs.append(dconv)
        dvgs.append(dvg)
        halves.append((keep, send))
    grads = scatter_sum(halves, block)
    value_grad, gate_grad = (
        jnp.concatenate([grads[:, (2 * i + j) * third :][:, :third] for i in range(3)], axis=1)
        for j in (0, 1)
    )
    kernel_grad = jnp.concatenate(
        [
            run(
                functools.partial(taps_sums, third=i),
                info,
                [dconvs[i], hid],
                [((taps, third), f32)],
                scratch=[pltpu.VMEM((rows + 16, LANES), f32), pltpu.VMEM((taps, 8, LANES), f32)],
                after=last,
            )[0]
            for i in range(3)
        ],
        axis=1,
    )
    for bit in every:
        kernel_grad = kernel_grad + swap(kernel_grad, *bit)

    theirs, mine = (
        run(
            functools.partial(norm_half, own=own),
            info,
            [*dvgs, w_value, w_gate],
            [((count, channels), f32 if own else bf16)],
            after=last,
        )[0]
        for own in (False, True)
    )
    dnorm, stats3 = run(
        norm_sums,
        info,
        [mine, swap(theirs, "tensor"), norm],
        [((count, channels), f32), ((count, LANES), f32)],
    )
    sums = (stats3 + swap(stats3, "tensor")) / width
    xhat = lax.dynamic_slice(norm, (WIDE, core * channels), (count, channels)).astype(f32)
    input_gradient = ct.astype(f32) + rstd[:, :1] * (
        dnorm - sums[:, :1] - xhat * sums[:, LANES // 2 : LANES // 2 + 1]
    )

    theirs, mine = (
        run(
            functools.partial(out_half, own=own),
            info,
            [swished, w_out],
            [((count, channels), f32 if own else bf16)],
            after=last,
        )[0]
        for own in (False, True)
    )
    output = x.astype(f32) + mine + swap(theirs, "tensor").astype(f32)
    return (
        output.astype(bf16)[None],
        input_gradient.astype(bf16)[None],
        value_grad,
        gate_grad,
        kernel_grad,
        out_grad,
    )


def solution(mesh):
    return jax.shard_map(
        shards,
        mesh=mesh,
        in_specs=(
            P("dp", "seq", "tensor"),
            P("dp"),
            P("dp", "seq", "tensor"),
            P(None, "tensor"),
            P(None, "tensor"),
            P(None, "tensor"),
            P("tensor", None),
        ),
        out_specs=(
            P("dp", "seq", "tensor"),
            P("dp", "seq", "tensor"),
            P(("seq", "dp"), "tensor"),
            P(("seq", "dp"), "tensor"),
            P(None, "tensor"),
            P("tensor", ("seq", "dp")),
        ),
        check_vma=False,
    )
```

time: 681 us -> 214 us (0.31)
  waiting for transfers between devices: 512 us -> 51.7 us
  Pallas kernels: 0 us -> 69 us
  other arithmetic: 82.8 us -> 15.2 us
  matrix products: 41.3 us -> 0 us
  starting transfers between devices: 11.6 us -> 39.6 us
  local copies, waits for them, and re-layouts: 8.19 us -> 35.6 us
  between operations: 16.6 us -> 2.04 us
  blocking collectives: 8.05 us -> 0 us
    reduce_scatter x5 -> x0, waiting for transfers between devices: 428 us -> none  [the longest x1 143 us: shards(): lax.psum_scatter(out_term, ('seq', 'dp'), scatter_dimension=1, tiled=True)]
    pallas_call x0 -> x16, Pallas kernels: none -> 69 us  [run(): pl.pallas_call(body, in_specs=[SMEM] + [VMEM] * len(args) + [ANY] * len(a...]
    psum x1 -> x0, waiting for transfers between devices: 65 us -> none  [shards(): kernel_grad = lax.psum(kernel_term, ('seq', 'dp'))]
    reduce_sum x6 -> x0, other arithmetic: 58.7 us -> none  [the longest x2 42.5 us: shards(): jnp.sum(padded[offset:offset + count] * slope, axis=0)]
    ppermute x4 -> x34, waiting for transfers between devices: 4.62 us -> 51.7 us  [the longest x32 46.8 us: swap(): return lax.ppermute(value, axis, [(i, i ^ 1 << bit) for i in range(size)])]
    dot_general x9 -> x0, matrix products: 41.3 us -> none  [the longest x1 6.98 us: shards(): jnp.dot(upstream_whole, w_out.T, preferred_element_type=jnp.float32)]
    ppermute x4 -> x34, starting transfers between devices: 11.1 us -> 39.6 us  [the longest x32 33.5 us: swap(): return lax.ppermute(value, axis, [(i, i ^ 1 << bit) for i in range(size)])]
    unnamed x197 -> x113, local copies, waits for them, and re-layouts: 4.57 us -> 31.1 us
  transfers between devices with their start and end apart: 12 -> 34, of which waited for: 7 -> 12; matrix products, arithmetic and copies ran while one was open for 14% -> 9% of each run, Pallas kernels for 0% -> 18%
where the time goes in v3:
time: 214 us; the launch traced here: 213 us
  Pallas kernels  69 us (32%)
  waiting for transfers between devices  51.7 us (24%)
  starting transfers between devices  39.6 us (19%)
  local copies, waits for them, and re-layouts  35.6 us (17%)
  other arithmetic  15.2 us (7%)
    pallas_call x16, Pallas kernels, run(): pl.pallas_call(body, in_specs=[SMEM] + [VMEM] * len(args) + [ANY] * len(a...  69 us
    ppermute x32, waiting for transfers between devices, swap(): return lax.ppermute(value, axis, [(i, i ^ 1 << bit) for i in range(size)])  46.8 us
    ppermute x32, starting transfers between devices, swap(): return lax.ppermute(value, axis, [(i, i ^ 1 << bit) for i in range(size)])  33.5 us
    unnamed x113, local copies, waits for them, and re-layouts  31.1 us
    convert_element_type x18, other arithmetic, merge(): value = value.astype(bf16)  7.77 us
    ppermute x1, starting transfers between devices, shards(): before = lax.ppermute(jnp.concatenate([x[-WIDE:], ct[-NEAR:]]), 'seq', up)  4.85 us
    ppermute x1, waiting for transfers between devices, shards(): after = lax.ppermute(jnp.concatenate([x[:WIDE], ct[:NEAR]]), 'seq', down)  4.29 us
  transfers between devices with their start and end apart: 34, of which 12 were waited for; matrix products, arithmetic and copies ran while one was open for 9% of the time, Pallas kernels for 18%

profile of v3, /device:TPU:0, one launch (start us, length us, event | category | flops | bytes accessed | tf_op | source)
XLA Modules:
  0.0 213.2 jit_solution(12654534940898442528)
XLA Ops:
  2.8 4.9 %collective-permute-start.1 = (bf16[48,768]{1,0:T(8,128)(2,1)S(1)}, bf16[48,768]{1,0:T(8,128)(2,1)S(1)}, u32[]{:S(2)}, u32[]{:S(2)}) collective-permute-start(bf16[48,768]{1,0:T(8,128)(2,1)S(1)} %pad_maximum_fusion.5), channel_id=1, source_target_pairs={{0,4},{4,8},{8,12},{12,16},{16,20},{20,24},{24,28},{1,5},{5,9},{9,... | collective-permute-start | bytes 221192 | tf_op jit(solution)/shard_map/ppermute | solution.py:435
  9.7 4.3 %collective-permute-done.2 = bf16[48,768]{1,0:T(8,128)(2,1)S(1)} collective-permute-done((bf16[48,768]{1,0:T(8,128)(2,1)S(1)}, bf16[48,768]{1,0:T(8,128)(2,1)S(1)}, u32[]{:S(2)}, u32[]{:S(2)}) %collective-permute-start.2) | collective-permute-done | bytes 73760 | tf_op jit(solution)/shard_map/ppermute | solution.py:436
  17.7 2.7 %upstream.1 = (bf16[768,1536]{1,0:T(8,128)(2,1)S(1)}, f32[768,768]{1,0:T(8,128)S(1)}) custom-call(s32[8]{0:T(128)S(1)} %stack.27.refs_0_, bf16[768,768]{1,0:T(8,128)(2,1)S(1)} %bitcast.127, bf16[768,768]{1,0:T(8,128)(2,1)S(1)} %collective-permute-done.4.refs_2_, bf16[768,1536]{1,0:T(8,128)(2,1)S(1)} %copy-done.2), custom_call_target="tpu_custom_call" | custom-call | flops 4096 | bytes 4096 | tf_op jit(solution)/shard_map/upstream/pallas_call | solution.py:31
  25.6 8.4 %front.1 = (bf16[832,1536]{1,0:T(8,128)(2,1)S(1)}, f32[768,128]{1,0:T(8,128)S(1)}, bf16[832,768]{1,0:T(8,128)(2,1)S(1)}, f32[768,768]{1,0:T(8,128)S(1)}, f32[768,768]{1,0:T(8,128)S(1)}, /*index=5*/f32[32,768]{1,0:T(8,128)S(1)}) custom-call(s32[8]{0:T(128)S(1)} %stack.27.refs_0_, bf16[768,768]{1,0:T(8,128)(2,1)S(1)} %bitcast.125, ...), custom_call_target="tpu_custom_call" | custom-call | flops 4096 | bytes 4096 | tf_op jit(solution)/shard_map/front/pallas_call | solution.py:31
  35.5 6.7 %depthwise.1 = (f32[800,768]{1,0:T(8,128)S(1)}, f32[800,128]{1,0:T(8,128)S(1)}) custom-call(s32[8]{0:T(128)S(1)} %stack.27.refs_0_, bf16[832,768]{1,0:T(8,128)(2,1)S(1)} %get-tuple-element.40.refs_1_.refs_2_, bf16[31,768]{1,0:T(8,128)(2,1)S(1)} %copy-done.41), custom_call_target="tpu_custom_call" | custom-call | flops 4096 | bytes 4096 | tf_op jit(solution)/shard_map/depthwise/pallas_call | solution.py:31
  44.2 7.2 %swish.1 = (bf16[768,768]{1,0:T(8,128)(2,1)S(1)}, f32[800,768]{1,0:T(8,128)S(1)}, f32[800,128]{1,0:T(8,128)S(1)}) custom-call(s32[8]{0:T(128)S(1)} %stack.27.refs_0_, f32[800,768]{1,0:T(8,128)S(1)} %get-tuple-element.41.refs_1_.refs_2_, f32[768,768]{1,0:T(8,128)S(1)} %get-tuple-element.39.refs_8_.refs_2_, f32[32,768]{1,0:T(8,128)S(1)} %get-tuple-element.42.refs_3_, ...), custom_call_target="tpu_custom_call" | custom-call | flops 4096 | bytes 4096 | tf_op jit(solution)/shard_map/swish/pallas_call | solution.py:31
  52.9 7.5 %out_terms.1 = (bf16[768,256]{1,0:T(8,128)(2,1)S(1)}, bf16[768,256]{1,0:T(8,128)(2,1)}, bf16[768,256]{1,0:T(8,128)(2,1)S(1)}, bf16[768,256]{1,0:T(8,128)(2,1)}, ...) custom-call(s32[8]{0:T(128)S(1)} %stack.27.refs_0_, bf16[768,1536]{1,0:T(8,128)(2,1)S(1)} %get-tuple-element.65.refs_1_, ...), custom_call_target="tpu_custom_call" | custom-call | flops 4096 | bytes 4096 | tf_op jit(solution)/shard_map/out_terms/pallas_call | solution.py:31
  64.9 2.4 %collective-permute-start.27 = (bf16[768,256]{1,0:T(8,128)(2,1)}, bf16[768,256]{1,0:T(8,128)(2,1)}, u32[]{:S(2)}, u32[]{:S(2)}) collective-permute-start(bf16[768,256]{1,0:T(8,128)(2,1)} %get-tuple-element.69), channel_id=1, source_target_pairs={{0,4},{4,0},{8,12},{12,8},{16,20},{20,16},{24,28},{28,24},{1,5},{5... | collective-permute-start | bytes 1179656 | tf_op jit(solution)/shard_map/ppermute | solution.py:48
  68.9 6.2 %collective-permute-done.24 = bf16[768,256]{1,0:T(8,128)(2,1)} collective-permute-done((bf16[768,256]{1,0:T(8,128)(2,1)}, bf16[768,256]{1,0:T(8,128)(2,1)}, u32[]{:S(2)}, u32[]{:S(2)}) %collective-permute-start.24) | collective-permute-done | bytes 393248 | tf_op jit(solution)/shard_map/ppermute | solution.py:48
  76.5 2.5 %collective-permute-start.25 = (bf16[384,256]{1,0:T(8,128)(2,1)S(1)}, bf16[384,256]{1,0:T(8,128)(2,1)S(1)}, u32[]{:S(2)}, u32[]{:S(2)}) collective-permute-start(bf16[384,256]{1,0:T(8,128)(2,1)S(1)} %bitcast.150), channel_id=1, source_target_pairs={{0,4},{4,0},{8,12},{12,8},{16,20},{20,16},{24,28},{28,24},{1,5},{5... | collective-permute-start | bytes 589832 | tf_op jit(solution)/shard_map/ppermute | solution.py:48
  87.5 6.4 %back.3 = (bf16[800,256]{1,0:T(8,128)(2,1)S(1)}, bf16[768,512]{1,0:T(8,128)(2,1)S(1)}, bf16[768,512]{1,0:T(8,128)(2,1)S(1)}, bf16[768,512]{1,0:T(8,128)(2,1)}) custom-call(s32[8]{0:T(128)S(1)} %stack.27.refs_0_, f32[800,768]{1,0:T(8,128)S(1)} %copy-done.6, f32[800,768]{1,0:T(8,128)S(1)} %copy-done.1, f32[800,128]{1,0:T(8,128)S(1)} %get-tuple-element.43.refs_4_.refs_3_, ...), custom_call_target="tpu_custom_call" | custom-call | flops 4096 | bytes 4096 | tf_op jit(solution)/shard_map/back/pallas_call | solution.py:31
  95.6 5.6 %back.4 = (bf16[800,256]{1,0:T(8,128)(2,1)S(1)}, bf16[768,512]{1,0:T(8,128)(2,1)S(1)}, bf16[768,512]{1,0:T(8,128)(2,1)S(1)}, bf16[768,512]{1,0:T(8,128)(2,1)S(1)}) custom-call(s32[8]{0:T(128)S(1)} %stack.27.refs_0_, f32[800,768]{1,0:T(8,128)S(1)} %copy-done.6, f32[800,768]{1,0:T(8,128)S(1)} %copy-done.1, f32[800,128]{1,0:T(8,128)S(1)} %get-tuple-element.43.refs_4_.refs_3_, ...), custom_call_target="tpu_custom_call" | custom-call | flops 4096 | bytes 4096 | tf_op jit(solution)/shard_map/back/pallas_call | solution.py:31
  105.3 5.7 %back.5 = (bf16[800,256]{1,0:T(8,128)(2,1)S(1)}, bf16[768,512]{1,0:T(8,128)(2,1)S(1)}, bf16[768,512]{1,0:T(8,128)(2,1)S(1)}, bf16[768,512]{1,0:T(8,128)(2,1)S(1)}) custom-call(s32[8]{0:T(128)S(1)} %stack.27.refs_0_, f32[800,768]{1,0:T(8,128)S(1)} %copy-done.6, f32[800,768]{1,0:T(8,128)S(1)} %copy-done.1, f32[800,128]{1,0:T(8,128)S(1)} %copy-done.20, ...), custom_call_target="tpu_custom_call" | custom-call | flops 4096 | bytes 4096 | tf_op jit(solution)/shard_map/back/pallas_call | solution.py:31
  111.1 2.5 %taps_sums.3 = f32[31,256]{1,0:T(8,128)S(1)} custom-call(s32[8]{0:T(128)S(1)} %stack.27.refs_0_, bf16[800,256]{1,0:T(8,128)(2,1)S(1)} %get-tuple-element.62.refs_1_, bf16[832,768]{1,0:T(8,128)(2,1)S(1)} %copy-done.16, bf16[768,512]{1,0:T(8,128)(2,1)S(1)} %get-tuple-element.52.refs_3_.refs_6_), custom_call_target="tpu_custom_call" | custom-call | flops 4096 | bytes 4096 | tf_op jit(solution)/shard_map/taps_sums/pallas_call | solution.py:31
  113.6 2.5 %taps_sums.4 = f32[31,256]{1,0:T(8,128)S(1)} custom-call(s32[8]{0:T(128)S(1)} %stack.27.refs_0_, bf16[800,256]{1,0:T(8,128)(2,1)S(1)} %get-tuple-element.63.refs_1_, bf16[832,768]{1,0:T(8,128)(2,1)S(1)} %copy-done.16, bf16[768,512]{1,0:T(8,128)(2,1)S(1)} %get-tuple-element.52.refs_3_.refs_6_), custom_call_target="tpu_custom_call" | custom-call | flops 4096 | bytes 4096 | tf_op jit(solution)/shard_map/taps_sums/pallas_call | solution.py:31
  116.1 2.5 %taps_sums.5 = f32[31,256]{1,0:T(8,128)S(1)} custom-call(s32[8]{0:T(128)S(1)} %stack.27.refs_0_, bf16[800,256]{1,0:T(8,128)(2,1)S(1)} %get-tuple-element.64.refs_1_, bf16[832,768]{1,0:T(8,128)(2,1)S(1)} %copy-done.16, bf16[768,512]{1,0:T(8,128)(2,1)S(1)} %get-tuple-element.52.refs_3_.refs_6_), custom_call_target="tpu_custom_call" | custom-call | flops 4096 | bytes 4096 | tf_op jit(solution)/shard_map/taps_sums/pallas_call | solution.py:31
  130.7 15.1 %collective-permute-done.29 = bf16[192,256]{1,0:T(8,128)(2,1)S(1)} collective-permute-done((bf16[192,256]{1,0:T(8,128)(2,1)S(1)}, bf16[192,256]{1,0:T(8,128)(2,1)S(1)}, u32[]{:S(2)}, u32[]{:S(2)}) %collective-permute-start.29) | collective-permute-done | bytes 98336 | tf_op jit(solution)/shard_map/ppermute | solution.py:48
  159.3 2.6 %norm_half.3 = bf16[768,768]{1,0:T(8,128)(2,1)S(1)} custom-call(s32[8]{0:T(128)S(1)} %stack.27.refs_0_, bf16[768,512]{1,0:T(8,128)(2,1)S(1)} %copy-done.31, bf16[768,512]{1,0:T(8,128)(2,1)S(1)} %copy-done.34, bf16[768,512]{1,0:T(8,128)(2,1)S(1)} %copy-done.37, bf16[1536,768]{1,0:T(8,128)(2,1)S(1)} %copy-done.8, bf16[1536,768]{1,0:T(8,128)(2,1)S(1)} %copy-done.10, ...), custom_call_target="tpu_custom_call" | custom-call | flops 4096 | bytes 4096 | tf_op jit(solution)/shard_map/norm_half/pallas_call | solution.py:31
  162.0 2.6 %norm_half.2.refs_1_ = f32[768,768]{1,0:T(8,128)S(1)} custom-call(s32[8]{0:T(128)S(1)} %stack.27.refs_0_, bf16[768,512]{1,0:T(8,128)(2,1)S(1)} %copy-done.32, bf16[768,512]{1,0:T(8,128)(2,1)S(1)} %copy-done.35, bf16[768,512]{1,0:T(8,128)(2,1)S(1)} %copy-done.38, bf16[1536,768]{1,0:T(8,128)(2,1)S(1)} %copy-done.8, bf16[1536,768]{1,0:T(8,128)(2,1)S(1)} %copy-done.10, ...), custom_call_target="tpu_custom_call" | custom-call | flops 4096 | bytes 4096 | tf_op jit(solution)/shard_map/norm_half/pallas_call | solution.py:31
  179.3 5.5 %collective-permute-done.11 = bf16[384,512]{1,0:T(8,128)(2,1)S(1)} collective-permute-done((bf16[384,512]{1,0:T(8,128)(2,1)S(1)}, bf16[384,512]{1,0:T(8,128)(2,1)S(1)}, u32[]{:S(2)}, u32[]{:S(2)}) %collective-permute-start.11) | collective-permute-done | bytes 393248 | tf_op jit(solution)/shard_map/ppermute | solution.py:48
  185.0 2.2 %collective-permute-start.12 = (bf16[192,512]{1,0:T(8,128)(2,1)S(1)}, bf16[192,512]{1,0:T(8,128)(2,1)S(1)}, u32[]{:S(2)}, u32[]{:S(2)}) collective-permute-start(bf16[192,512]{1,0:T(8,128)(2,1)S(1)} %bitcast.151), channel_id=1, source_target_pairs={{0,8},{4,12},{8,0},{12,4},{16,24},{20,28},{24,16},{28,20},{1,9},{5... | collective-permute-start | bytes 589832 | tf_op jit(solution)/shard_map/ppermute | solution.py:48
  190.5 2.9 %norm_sums.1 = (f32[768,768]{1,0:T(8,128)S(1)}, f32[768,128]{1,0:T(8,128)S(1)}) custom-call(s32[8]{0:T(128)S(1)} %stack.27.refs_0_, f32[768,768]{1,0:T(8,128)S(1)} %norm_half.2.refs_1_, bf16[768,768]{1,0:T(8,128)(2,1)S(1)} %collective-permute-done.8.refs_2_, bf16[832,1536]{1,0:T(8,128)(2,1)S(1)} %get-tuple-element.49.refs_10_.refs_3_), custom_call_target="tpu_custom_call" | custom-call | flops 4096 | bytes 4096 | tf_op jit(solution)/shard_map/norm_sums/pallas_call | solution.py:31
  195.3 3.0 %collective-permute-start.19 = (bf16[96,1536]{1,0:T(8,128)(2,1)S(1)}, bf16[96,1536]{1,0:T(8,128)(2,1)S(1)}, u32[]{:S(2)}, u32[]{:S(2)}) collective-permute-start(bf16[96,1536]{1,0:T(8,128)(2,1)S(1)} %dynamic-slice_bitcast_fusion), channel_id=1, source_target_pairs={{0,16},{4,20},{8,24},{12,28},{16,0},{20,4},{24,8},{28,12},{1,17},{... | collective-permute-start | bytes 884744 | tf_op jit(solution)/shard_map/ppermute | solution.py:48
  200.4 11.8 %collective-permute-done.19 = bf16[96,1536]{1,0:T(8,128)(2,1)S(1)} collective-permute-done((bf16[96,1536]{1,0:T(8,128)(2,1)S(1)}, bf16[96,1536]{1,0:T(8,128)(2,1)S(1)}, u32[]{:S(2)}, u32[]{:S(2)}) %collective-permute-start.19) | collective-permute-done | bytes 294944 | tf_op jit(solution)/shard_map/ppermute | solution.py:48
  (227 shorter events, 87.6 us)
Async XLA Ops:
  0.6 14.1 %collective-permute-start.4 = (bf16[768,768]{1,0:T(8,128)(2,1)}, bf16[768,768]{1,0:T(8,128)(2,1)S(1)}, u32[]{:S(2)}, u32[]{:S(2)}) collective-permute-start(bf16[768,768]{1,0:T(8,128)(2,1)} %bitcast.126), channel_id=1, source_target_pairs={{0,2},{2,0},{1,3},{3,1},{4,6},{6,4},{5,7},{7,5},{8,10},{10,8},{9,1... | collective-permute-start | bytes 3538952 | tf_op jit(solution)/shard_map/ppermute | solution.py:48
  1.1 19.2 %collective-permute-start = (bf16[768,768]{1,0:T(8,128)(2,1)}, bf16[768,768]{1,0:T(8,128)(2,1)S(1)}, u32[]{:S(2)}, u32[]{:S(2)}) collective-permute-start(bf16[768,768]{1,0:T(8,128)(2,1)} %bitcast.124), channel_id=1, source_target_pairs={{0,2},{2,0},{1,3},{3,1},{4,6},{6,4},{5,7},{7,5},{8,10},{10,8},{9,1... | collective-permute-start | bytes 3538952 | tf_op jit(solution)/shard_map/ppermute | solution.py:48
  63.4 11.7 %collective-permute-start.24 = (bf16[768,256]{1,0:T(8,128)(2,1)}, bf16[768,256]{1,0:T(8,128)(2,1)}, u32[]{:S(2)}, u32[]{:S(2)}) collective-permute-start(bf16[768,256]{1,0:T(8,128)(2,1)} %get-tuple-element.67), channel_id=1, source_target_pairs={{0,1},{1,0},{2,3},{3,2},{4,5},{5,4},{6,7},{7,6},{8,9},{9,8},{10,11... | collective-permute-start | bytes 1179656 | tf_op jit(solution)/shard_map/ppermute | solution.py:48
  64.9 14.1 %collective-permute-start.27 = (bf16[768,256]{1,0:T(8,128)(2,1)}, bf16[768,256]{1,0:T(8,128)(2,1)}, u32[]{:S(2)}, u32[]{:S(2)}) collective-permute-start(bf16[768,256]{1,0:T(8,128)(2,1)} %get-tuple-element.69), channel_id=1, source_target_pairs={{0,4},{4,0},{8,12},{12,8},{16,20},{20,16},{24,28},{28,24},{1,5},{5... | collective-permute-start | bytes 1179656 | tf_op jit(solution)/shard_map/ppermute | solution.py:48
  67.3 14.7 %collective-permute-start.30 = (bf16[768,256]{1,0:T(8,128)(2,1)}, bf16[768,256]{1,0:T(8,128)(2,1)S(1)}, u32[]{:S(2)}, u32[]{:S(2)}) collective-permute-start(bf16[768,256]{1,0:T(8,128)(2,1)} %copy-done.53), channel_id=1, source_target_pairs={{0,8},{4,12},{8,0},{12,4},{16,24},{20,28},{24,16},{28,20},{1,9},{5... | collective-permute-start | bytes 1179656 | tf_op jit(solution)/shard_map/ppermute | solution.py:48
  68.9 14.2 %collective-permute-start.6 = (f32[800,128]{1,0:T(8,128)}, f32[800,128]{1,0:T(8,128)S(1)}, u32[]{:S(2)}, u32[]{:S(2)}) collective-permute-start(f32[800,128]{1,0:T(8,128)} %copy-done.27), channel_id=1, source_target_pairs={{0,2},{2,0},{1,3},{3,1},{4,6},{6,4},{5,7},{7,5},{8,10},{10,8},{9,1... | collective-permute-start | bytes 1228808 | tf_op jit(solution)/shard_map/ppermute | solution.py:48
  76.5 48.0 %collective-permute-start.25 = (bf16[384,256]{1,0:T(8,128)(2,1)S(1)}, bf16[384,256]{1,0:T(8,128)(2,1)S(1)}, u32[]{:S(2)}, u32[]{:S(2)}) collective-permute-start(bf16[384,256]{1,0:T(8,128)(2,1)S(1)} %bitcast.150), channel_id=1, source_target_pairs={{0,4},{4,0},{8,12},{12,8},{16,20},{20,16},{24,28},{28,24},{1,5},{5... | collective-permute-start | bytes 589832 | tf_op jit(solution)/shard_map/ppermute | solution.py:48
  80.4 44.7 %collective-permute-start.28 = (bf16[384,256]{1,0:T(8,128)(2,1)S(1)}, bf16[384,256]{1,0:T(8,128)(2,1)S(1)}, u32[]{:S(2)}, u32[]{:S(2)}) collective-permute-start(bf16[384,256]{1,0:T(8,128)(2,1)S(1)} %bitcast.149), channel_id=1, source_target_pairs={{0,8},{4,12},{8,0},{12,4},{16,24},{20,28},{24,16},{28,20},{1,9},{5... | collective-permute-start | bytes 589832 | tf_op jit(solution)/shard_map/ppermute | solution.py:48
  120.2 8.3 %collective-permute-start.31 = (bf16[384,256]{1,0:T(8,128)(2,1)S(1)}, bf16[384,256]{1,0:T(8,128)(2,1)S(1)}, u32[]{:S(2)}, u32[]{:S(2)}) collective-permute-start(bf16[384,256]{1,0:T(8,128)(2,1)S(1)} %bitcast.152), channel_id=1, source_target_pairs={{0,1},{1,0},{2,3},{3,2},{4,5},{5,4},{6,7},{7,6},{8,9},{9,8},{10,11... | collective-permute-start | bytes 589832 | tf_op jit(solution)/shard_map/ppermute | solution.py:48
  120.8 51.4 %collective-permute-start.10 = (bf16[768,512]{1,0:T(8,128)(2,1)}, bf16[768,512]{1,0:T(8,128)(2,1)}, u32[]{:S(2)}, u32[]{:S(2)}) collective-permute-start(bf16[768,512]{1,0:T(8,128)(2,1)} %get-tuple-element.50.refs_11_), channel_id=1, source_target_pairs={{0,1},{1,0},{2,3},{3,2},{4,5},{5,4},{6,7},{7,6},{8,9},{9,8},{10,11... | collective-permute-start | bytes 2359304 | tf_op jit(solution)/shard_map/ppermute | solution.py:48
  125.1 20.7 %collective-permute-start.29 = (bf16[192,256]{1,0:T(8,128)(2,1)S(1)}, bf16[192,256]{1,0:T(8,128)(2,1)S(1)}, u32[]{:S(2)}, u32[]{:S(2)}) collective-permute-start(bf16[192,256]{1,0:T(8,128)(2,1)S(1)} %bitcast.156), channel_id=1, source_target_pairs={{0,1},{1,0},{2,3},{3,2},{4,5},{5,4},{6,7},{7,6},{8,9},{9,8},{10,11... | collective-permute-start | bytes 294920 | tf_op jit(solution)/shard_map/ppermute | solution.py:48
  128.7 17.2 %collective-permute-start.32 = (bf16[192,256]{1,0:T(8,128)(2,1)S(1)}, bf16[192,256]{1,0:T(8,128)(2,1)S(1)}, u32[]{:S(2)}, u32[]{:S(2)}) collective-permute-start(bf16[192,256]{1,0:T(8,128)(2,1)S(1)} %bitcast.157), channel_id=1, source_target_pairs={{0,4},{4,0},{8,12},{12,8},{16,20},{20,16},{24,28},{28,24},{1,5},{5... | collective-permute-start | bytes 294920 | tf_op jit(solution)/shard_map/ppermute | solution.py:48
  130.0 19.7 %collective-permute-start.22 = (f32[31,768]{1,0:T(8,128)S(1)}, f32[31,768]{1,0:T(8,128)}, u32[]{:S(2)}, u32[]{:S(2)}) collective-permute-start(f32[31,768]{1,0:T(8,128)S(1)} %add.167), channel_id=1, source_target_pairs={{0,8},{4,12},{8,0},{12,4},{16,24},{20,28},{24,16},{28,20},{1,9},{5... | collective-permute-start | bytes 285704 | tf_op jit(solution)/shard_map/ppermute | solution.py:48
  146.7 23.3 %collective-permute-start.33 = (bf16[96,768]{1,0:T(8,128)(2,1)}, bf16[96,768]{1,0:T(8,128)(2,1)}, u32[]{:S(2)}, u32[]{:S(2)}) collective-permute-start(bf16[96,768]{1,0:T(8,128)(2,1)} %dynamic-slice_bitcast_fusion.1), channel_id=1, source_target_pairs={{0,16},{4,20},{8,24},{12,28},{16,0},{20,4},{24,8},{28,12},{1,17},{... | collective-permute-start | bytes 442376 | tf_op jit(solution)/shard_map/ppermute | solution.py:48
  148.0 26.3 %collective-permute-start.16 = (bf16[768,512]{1,0:T(8,128)(2,1)S(1)}, bf16[768,512]{1,0:T(8,128)(2,1)}, u32[]{:S(2)}, u32[]{:S(2)}) collective-permute-start(bf16[768,512]{1,0:T(8,128)(2,1)S(1)} %get-tuple-element.52.refs_3_.refs_6_), channel_id=1, source_target_pairs={{0,8},{4,12},{8,0},{12,4},{16,24},{20,28},{24,16},{28,20},{1,9},{5... | collective-permute-start | bytes 2359304 | tf_op jit(solution)/shard_map/ppermute | solution.py:48
  150.7 18.7 %collective-permute-start.23 = (f32[31,768]{1,0:T(8,128)S(1)}, f32[31,768]{1,0:T(8,128)S(1)}, u32[]{:S(2)}, u32[]{:S(2)}) collective-permute-start(f32[31,768]{1,0:T(8,128)S(1)} %add.168), channel_id=1, source_target_pairs={{0,16},{4,20},{8,24},{12,28},{16,0},{20,4},{24,8},{28,12},{1,17},{... | collective-permute-start | bytes 285704 | tf_op jit(solution)/shard_map/ppermute | solution.py:48
  152.2 24.6 %collective-permute-start.13 = (bf16[768,512]{1,0:T(8,128)(2,1)}, bf16[768,512]{1,0:T(8,128)(2,1)S(1)}, u32[]{:S(2)}, u32[]{:S(2)}) collective-permute-start(bf16[768,512]{1,0:T(8,128)(2,1)} %copy-done.42), channel_id=1, source_target_pairs={{0,4},{4,0},{8,12},{12,8},{16,20},{20,16},{24,28},{28,24},{1,5},{5... | collective-permute-start | bytes 2359304 | tf_op jit(solution)/shard_map/ppermute | solution.py:48
  169.4 24.1 %collective-permute-start.7 = (bf16[768,768]{1,0:T(8,128)(2,1)S(1)}, bf16[768,768]{1,0:T(8,128)(2,1)S(1)}, u32[]{:S(2)}, u32[]{:S(2)}) collective-permute-start(bf16[768,768]{1,0:T(8,128)(2,1)S(1)} %out_half.3), channel_id=1, source_target_pairs={{0,2},{2,0},{1,3},{3,1},{4,6},{6,4},{5,7},{7,5},{8,10},{10,8},{9,1... | collective-permute-start | bytes 3538952 | tf_op jit(solution)/shard_map/ppermute | solution.py:48
  170.1 20.5 %collective-permute-start.8 = (bf16[768,768]{1,0:T(8,128)(2,1)S(1)}, bf16[768,768]{1,0:T(8,128)(2,1)S(1)}, u32[]{:S(2)}, u32[]{:S(2)}) collective-permute-start(bf16[768,768]{1,0:T(8,128)(2,1)S(1)} %norm_half.3), channel_id=1, source_target_pairs={{0,2},{2,0},{1,3},{3,1},{4,6},{6,4},{5,7},{7,5},{8,10},{10,8},{9,1... | collective-permute-start | bytes 3538952 | tf_op jit(solution)/shard_map/ppermute | solution.py:48
  173.7 11.1 %collective-permute-start.11 = (bf16[384,512]{1,0:T(8,128)(2,1)S(1)}, bf16[384,512]{1,0:T(8,128)(2,1)S(1)}, u32[]{:S(2)}, u32[]{:S(2)}) collective-permute-start(bf16[384,512]{1,0:T(8,128)(2,1)S(1)} %bitcast.148), channel_id=1, source_target_pairs={{0,4},{4,0},{8,12},{12,8},{16,20},{20,16},{24,28},{28,24},{1,5},{5... | collective-permute-start | bytes 1179656 | tf_op jit(solution)/shard_map/ppermute | solution.py:48
  175.8 11.3 %collective-permute-start.17 = (bf16[384,512]{1,0:T(8,128)(2,1)S(1)}, bf16[384,512]{1,0:T(8,128)(2,1)S(1)}, u32[]{:S(2)}, u32[]{:S(2)}) collective-permute-start(bf16[384,512]{1,0:T(8,128)(2,1)S(1)} %bitcast.147), channel_id=1, source_target_pairs={{0,1},{1,0},{2,3},{3,2},{4,5},{5,4},{6,7},{7,6},{8,9},{9,8},{10,11... | collective-permute-start | bytes 1179656 | tf_op jit(solution)/shard_map/ppermute | solution.py:48
  177.2 11.6 %collective-permute-start.14 = (bf16[384,512]{1,0:T(8,128)(2,1)S(1)}, bf16[384,512]{1,0:T(8,128)(2,1)S(1)}, u32[]{:S(2)}, u32[]{:S(2)}) collective-permute-start(bf16[384,512]{1,0:T(8,128)(2,1)S(1)} %bitcast.146), channel_id=1, source_target_pairs={{0,8},{4,12},{8,0},{12,4},{16,24},{20,28},{24,16},{28,20},{1,9},{5... | collective-permute-start | bytes 1179656 | tf_op jit(solution)/shard_map/ppermute | solution.py:48
  185.0 9.9 %collective-permute-start.12 = (bf16[192,512]{1,0:T(8,128)(2,1)S(1)}, bf16[192,512]{1,0:T(8,128)(2,1)S(1)}, u32[]{:S(2)}, u32[]{:S(2)}) collective-permute-start(bf16[192,512]{1,0:T(8,128)(2,1)S(1)} %bitcast.151), channel_id=1, source_target_pairs={{0,8},{4,12},{8,0},{12,4},{16,24},{20,28},{24,16},{28,20},{1,9},{5... | collective-permute-start | bytes 589832 | tf_op jit(solution)/shard_map/ppermute | solution.py:48
  195.3 16.9 %collective-permute-start.19 = (bf16[96,1536]{1,0:T(8,128)(2,1)S(1)}, bf16[96,1536]{1,0:T(8,128)(2,1)S(1)}, u32[]{:S(2)}, u32[]{:S(2)}) collective-permute-start(bf16[96,1536]{1,0:T(8,128)(2,1)S(1)} %dynamic-slice_bitcast_fusion), channel_id=1, source_target_pairs={{0,16},{4,20},{8,24},{12,28},{16,0},{20,4},{24,8},{28,12},{1,17},{... | collective-permute-start | bytes 884744 | tf_op jit(solution)/shard_map/ppermute | solution.py:48
  (66 other events, 372.6 us)

commit v4 on v3

--- a/solution.py
+++ b/solution.py
@@ -17,30 +17,36 @@
 VMEM = pl.BlockSpec(memory_space=pltpu.VMEM)
 SMEM = pl.BlockSpec(memory_space=pltpu.SMEM)
 ANY = pl.BlockSpec(memory_space=pl.ANY)
+HBM = pl.BlockSpec(memory_space=pltpu.HBM)
 
 
 def dot(a, b, dims=NN):
     return lax.dot_general(a, b, dims, preferred_element_type=f32)
 
 
-def run(kernel, info, args, outs, scratch=(), after=(), limit=16):
+def run(kernel, info, args, outs, scratch=(), after=(), limit=8, space=VMEM, to=VMEM):
     def body(*refs):
         lead = 1 + len(args)
-        kernel(*refs[:lead], *refs[lead + len(after) :])
-
-    return pl.pallas_call(
+        rest = refs[lead + len(after) :]
+        kernel(*refs[:lead], *rest[: len(outs)], *rest[len(outs) + 1 :])
+        rest[len(outs)][...] = jnp.zeros((8, LANES), f32)
+
+    args = [pltpu.with_memory_space_constraint(a, space.memory_space) for a in args]
+    *results, mark = pl.pallas_call(
         body,
-        in_specs=[SMEM] + [VMEM] * len(args) + [ANY] * len(after),
-        out_specs=[VMEM] * len(outs),
-        out_shape=[pltpu.VMEM(shape, dtype) for shape, dtype in outs],
+        in_specs=[SMEM] + [space] * len(args) + [ANY] * len(after),
+        out_specs=[to] * len(outs) + [VMEM],
+        out_shape=[to.memory_space(shape, dtype) for shape, dtype in outs]
+        + [pltpu.VMEM((8, LANES), f32)],
         scratch_shapes=list(scratch),
         compiler_params=pltpu.CompilerParams(vmem_limit_bytes=limit << 20),
         cost_estimate=pl.CostEstimate(flops=COST, bytes_accessed=COST, transcendentals=0),
         name=kernel.__name__ if hasattr(kernel, "__name__") else kernel.func.__name__,
-    )(info, *[pltpu.with_memory_space_constraint(a, pltpu.VMEM) for a in args], *after)
-
-
-COST = 1 << 12
+    )(info, *args, *after)
+    return *results, mark
+
+
+COST = 1 << 10
 
 
 def swap(value, axis, bit=0):
@@ -56,53 +62,125 @@
     return bits_of("dp") + bits_of("seq")
 
 
-class Halver:
-    def __init__(self, keep, send, bit, rows):
-        self.bits = every_bit()[::-1]
-        self.rows = rows
-        self.merge(keep, send, bit)
-
-    def merge(self, keep, send, bit):
-        got = swap(send, *bit)
-        value = keep.astype(f32) + got.astype(f32)
-        self.bits.remove(bit)
-        if self.bits:
-            value = value.astype(bf16)
-        self.value = value.reshape((2,) * len(self.bits) + (self.rows, value.shape[-1]))
-
-    def step(self, bit):
-        dim = self.bits.index(bit)
-        mine = (lax.axis_index(bit[0]) >> bit[1]) & 1
-        columns = self.value.shape[-1]
-        send = lax.dynamic_index_in_dim(self.value, 1 - mine, dim, keepdims=False)
-        keep = lax.dynamic_index_in_dim(self.value, mine, dim, keepdims=False)
-        self.merge(keep.reshape(-1, columns), send.reshape(-1, columns), bit)
-
-
-def scatter_sum(halves, rows):
-    every = every_bit()
-    turning, rest = every[:3], every[3:]
-    thirds = [Halver(*half, turning[i], rows) for i, half in enumerate(halves)]
-    for phase in range(1, len(turning)):
-        for i, third in enumerate(thirds):
-            third.step(turning[(i + phase) % len(turning)])
-    merged = thirds[0]
-    merged.value = jnp.concatenate([t.value for t in thirds], axis=-1)
-    for bit in rest:
-        merged.step(bit)
-    return merged.value
-
-
-def store_halves(info, bit, start, value, keep, send, rows):
-    for mine in (0, 1):
-
-        @pl.when(info[4 + bit] == mine)
-        def _():
-            for r in range(0, value.shape[0], rows):
-                block = (start + r) // rows
-                to = ((block >> (bit + 1)) << bit) | (block & ((1 << bit) - 1))
-                target = keep if (block >> bit) & 1 == mine else send
-                target[to * rows : (to + 1) * rows, :] = value[r : r + rows, :]
+def split_rows(info, bit, place, total, rows, keep, send, load):
+    run_length = rows << place
+    for j in range(total // (2 * run_length)):
+        for put, side in ((keep, info[4 + bit]), (send, 1 - info[4 + bit])):
+            if run_length % 32:
+                low, high = (
+                    load(slice((2 * j + i) * run_length, (2 * j + i + 1) * run_length))
+                    for i in (0, 1)
+                )
+                value = jnp.where(side == 0, low, high)
+            else:
+                at = pl.multiple_of((2 * j + side) * run_length, run_length)
+                value = load(pl.ds(at, run_length))
+            put(j * run_length, value)
+
+
+def put_into(target):
+    def put(at, value):
+        target[at : at + value.shape[0], :] = value
+
+    return put
+
+
+def put_folded(target, first, half):
+    columns = target.shape[1] // 2
+
+    def put(at, value):
+        length = value.shape[0]
+        for low in range(0, length, min(length, half)):
+            part = value[low : low + min(length, half)]
+            side, row = divmod(at + low, half)
+            to = slice(first + row, first + row + part.shape[0])
+            target[to, side * columns : (side + 1) * columns] = part
+
+    return put
+
+
+def add(a, b):
+    return (a.astype(f32) + b.astype(f32)).astype(bf16)
+
+
+def first_split(info, product, okept, ogot, vkeep, okeep, send, *, third, rows):
+    total = product.shape[0]
+    split_rows(info, third, third, total, rows, put_into(vkeep), put_into(send), lambda at: product[at, :])
+    before = (third + 2) % 3
+    place = third - (before < third)
+    fold = put_folded(send, total // 2, total // 8)
+    load = lambda at: add(okept[at, :], ogot[at, :])
+    split_rows(info, third, place, total // 2, rows, put_into(okeep), fold, load)
+
+
+def unfold(got, first, rows, target):
+    half = rows // 2
+    columns = target.shape[1]
+    target[:half, :] = got[first:, :columns]
+    target[half:, :] = got[first:, columns:]
+
+
+def second_split(info, vkept, okept, got, vkeep, okeep, send, flat, *, third, rows):
+    total = vkept.shape[0]
+    bit = (third + 1) % 3
+    left = [b for b in range(3) if b != third]
+    load = lambda at: add(vkept[at, :], got[at, :])
+    split_rows(info, bit, left.index(bit), total, rows, put_into(vkeep), put_into(send), load)
+    unfold(got, total, total // 2, flat)
+    fold = put_folded(send, total // 2, total // 8)
+    load = lambda at: add(okept[at, :], flat[at, :])
+    split_rows(info, bit, 0, total // 2, rows, put_into(okeep), fold, load)
+
+
+def third_split(info, vkept, okept, got, vkeep, okeep, send, flat, *, third, rows):
+    total = vkept.shape[0]
+    load = lambda at: add(vkept[at, :], got[at, :])
+    split_rows(info, (third + 2) % 3, 0, total, rows, put_into(vkeep), put_into(send), load)
+    unfold(got, total, total // 2, flat)
+    okeep[...] = add(okept[...], flat[...])
+
+
+def last_split(info, vkept, okept, got, keep, send, *, rows):
+    total, columns = vkept.shape
+
+    def put(target):
+        def to(at, value):
+            target[at : at + value.shape[0], : value.shape[1]] = value
+
+        return to
+
+    load = lambda at: add(vkept[at, :], got[at, :])
+    split_rows(info, 3, 0, total, rows, put(keep), put(send), load)
+
+    def side(target):
+        def to(at, value):
+            target[at : at + value.shape[0], columns:] = value
+
+        return to
+
+    split_rows(info, 3, 0, total, rows, side(keep), side(send), lambda at: okept[at, :])
+
+
+def send_bit(value, bit):
+    return swap(value, *every_bit()[bit])
+
+
+def finish(keep, send, rows):
+    value = keep.astype(f32) + send_bit(send, 3).astype(f32)
+    for bit in range(4, len(every_bit())):
+        axis, place = every_bit()[bit]
+        value = value.astype(bf16).reshape(-1, 2, rows, value.shape[1])
+        mine = (lax.axis_index(axis) >> place) & 1
+        keep, send = (
+            lax.dynamic_index_in_dim(value, side, 1, keepdims=False) for side in (mine, 1 - mine)
+        )
+        shape = (-1, value.shape[-1])
+        value = keep.reshape(shape).astype(f32) + send_bit(send.reshape(shape), bit).astype(f32)
+    return value
+
+
+def sigmoid(v):
+    return 0.5 + 0.5 * jnp.tanh(0.5 * v)
 
 
 def row_mask(info, first, rows, limit):
@@ -115,6 +193,43 @@
         pl.multiple_of(info[3] * half, half),
         pl.multiple_of((1 - info[3]) * half, half),
     )
+
+
+def prepare(info, *refs):
+    count = (len(refs) - 1) // 2
+    sem = refs[-1]
+    copies = [
+        pltpu.make_async_copy(refs[i], refs[count + i], sem.at[i]) for i in range(count)
+    ]
+    for c in copies:
+        c.start()
+    for c in copies:
+        c.wait()
+
+
+def pick(info, x, ct, last, first, sem):
+    count = x.shape[0]
+    copies = [
+        pltpu.make_async_copy(source.at[a : a + n], target.at[b : b + n], sem.at[i])
+        for i, (source, target, a, b, n) in enumerate(
+            (
+                (x, last, count - WIDE, 0, WIDE),
+                (ct, last, count - NEAR, WIDE, NEAR),
+                (x, first, 0, 0, WIDE),
+                (ct, first, 0, WIDE, NEAR),
+            )
+        )
+    ]
+    for c in copies:
+        c.start()
+    for c in copies:
+        c.wait()
+
+
+def pack(info, before, after, halo):
+    rows = before.shape[0]
+    halo[:rows, :] = before[...]
+    halo[rows:, :] = after[...]
 
 
 def upstream(info, own, other, w_out, full, pull):
@@ -124,7 +239,7 @@
     full[:, pl.ds(theirs, half)] = other[...]
     step = count // 2
     for c in range(0, count, step):
-        pull[c : c + step, :] = dot(full[c : c + step, :], w_out[...], NT)
+        pull[c : c + step, :] = dot(full[c : c + step, :], w_out[...], NT).astype(bf16)
 
 
 def front(info, own, other, halo_own, halo_other, wv, wg, w_out, norm, rstd, hid, sig, slope, ends, edge):
@@ -155,7 +270,7 @@
         rstd[pl.ds(at, chunk), :] = jnp.broadcast_to(inverse, (chunk, LANES))
         return 0
 
-    lax.fori_loop(0, count // chunk, body, 0)
+    lax.fori_loop(0, count // chunk, body, 0, unroll=2)
     for to, at in ((0, 0), (WIDE + count, WIDE + NEAR)):
         normalize(pl.ds(to, WIDE), halo_own[at : at + WIDE, :], halo_other[at : at + WIDE, :])
     for a, at in ((halo_own, mine), (halo_other, theirs)):
@@ -170,14 +285,14 @@
         cols = slice(n, n + tile)
         for c in range(0, rows, step):
             value = dot(norm[c : c + step, :], wv[:, cols])
-            s = jax.nn.sigmoid(dot(norm[c : c + step, :], wg[:, cols]))
+            s = sigmoid(dot(norm[c : c + step, :], wg[:, cols]))
             keep = row_mask(info, c - WIDE, step, info[1])
             vs = value * s * keep
             hid[c : c + step, cols] = vs.astype(bf16)
             low, high = max(c, WIDE), min(c + step, WIDE + count)
             part = slice(low - c, high - c)
-            sig[low - WIDE : high - WIDE, cols] = (s * keep)[part]
-            slope[low - WIDE : high - WIDE, cols] = (vs * (1.0 - s))[part]
+            sig[low - WIDE : high - WIDE, cols] = (s * keep)[part].astype(bf16)
+            slope[low - WIDE : high - WIDE, cols] = (vs * (1.0 - s))[part].astype(bf16)
 
 
 def tap_sums(source, base, groups, taps):
@@ -258,7 +373,7 @@
         to = pl.ds(at, rows)
         mean, inverse = moments(own[to, :], other[to, :], 2 * channels)
         zhat = (conv[to, :] - mean) * inverse
-        s = jax.nn.sigmoid(zhat)
+        s = sigmoid(zhat)
         zs = zhat * s
         d = g * (s + zs * (1.0 - s))
         dswish[to, :] = d
@@ -272,23 +387,27 @@
     def body(i, _):
         at = pl.multiple_of(i * step, step)
         rows = pl.ds(at, step)
-        swished[rows, :] = part(pl.multiple_of(at + NEAR, NEAR), pull[rows, :], step)
+        g = pull[rows, :].astype(f32)
+        swished[rows, :] = part(pl.multiple_of(at + NEAR, NEAR), g, step)
         return 0
 
-    lax.fori_loop(0, count // step, body, 0)
-
-
-def out_terms(info, full, swished, *halves, rows):
+    lax.fori_loop(0, count // step, body, 0, unroll=2)
+
+
+def out_terms(info, full, swished, *refs, rows):
+    halves, product = refs[:-1], refs[-1]
     width = full.shape[1]
     cols = swished.shape[1] // 3
     step = width // 4
+    for c in range(0, width, step):
+        product[c : c + step, :] = dot(full[:, c : c + step], swished[...], TN).astype(bf16)
     for i in range(3):
-        for c in range(0, width, step):
-            r = dot(full[:, c : c + step], swished[:, i * cols : (i + 1) * cols], TN)
-            store_halves(info, i, c, r.astype(bf16), halves[2 * i], halves[2 * i + 1], rows)
-
-
-def back(info, dswish, conv, own, other, own2, other2, taps, sig, slope, norm, dconv, dvg, keep, send, scratch, coef, *, third, block):
+        load = lambda at: product[at, i * cols : (i + 1) * cols]
+        keep, send = (put_into(half) for half in halves[2 * i : 2 * i + 2])
+        split_rows(info, i, i, width, rows, keep, send, load)
+
+
+def back(info, dswish, conv, own, other, own2, other2, taps, sig, slope, norm, dconv, dvg, product, scratch, coef, *, third):
     rows, channels = dswish.shape
     count = sig.shape[0]
     width = 2 * channels
@@ -330,7 +449,7 @@
     step = width // 4
     for c in range(0, width, step):
         r = dot(norm[WIDE : WIDE + count, c : c + step], dvg[...], TN)
-        store_halves(info, third, c, r.astype(bf16), keep, send, block)
+        product[c : c + step, :] = r.astype(bf16)
 
 
 def taps_sums(info, dconv, hid, out, scratch, total, *, third):
@@ -373,21 +492,26 @@
     lax.fori_loop(0, tiles, tile, 0)
 
 
+def add_taps(info, value, got, result):
+    result[...] = value[...] + got[...]
+
+
 def out_half(info, swished, w_out, result, *, own):
     half = result.shape[1]
     at = halves_at(info, half)[0 if own else 1]
     step = swished.shape[0] // 2
-    for c in range(0, swished.shape[0], step):
-        part = dot(swished[c : c + step, :], w_out[:, pl.ds(at, half)])
-        result[c : c + step, :] = part.astype(result.dtype)
-
-
-def norm_half(info, a, b, c, wv, wg, result, *, own):
-    count, half = result.shape
+    for r in range(0, swished.shape[0], step):
+        part = dot(swished[r : r + step, :], w_out[:, pl.ds(at, half)])
+        result[r : r + step, :] = part.astype(result.dtype)
+
+
+def norm_half(info, a, b, c, wv, wg, *results, own):
+    half = results[0].shape[1]
     at = halves_at(info, half)[0 if own else 1]
     third = half // 3
-    step = count // 2
-    for r in range(0, count, step):
+    step = a.shape[0] // 2
+    for n, result in enumerate(results):
+        r = n * step
         total = None
         for i, dvg in enumerate((a, b, c)):
             cols = slice(i * third, (i + 1) * third)
@@ -396,23 +520,61 @@
                     dvg[r : r + step, j * third : (j + 1) * third], w[pl.ds(at, half), cols], NT
                 )
                 total = part if total is None else total + part
-        result[r : r + step, :] = total.astype(result.dtype)
-
-
-def norm_sums(info, mine, got, norm, total, stats):
-    count, half = mine.shape
+        result[...] = total.astype(result.dtype)
+
+
+def norm_sums(info, mine0, mine1, got0, got1, norm, total, stats):
+    count, half = total.shape
     at = halves_at(info, half)[0]
     step = 32
-
-    def body(i, _):
-        rows = pl.ds(pl.multiple_of(i * step, step), step)
-        xhat = norm[pl.ds(pl.multiple_of(i * step + WIDE, step), step), pl.ds(at, half)]
-        d = mine[rows, :] + got[rows, :].astype(f32)
-        total[rows, :] = d
-        stats[rows, :] = paired(d, d * xhat.astype(f32))
-        return 0
-
-    lax.fori_loop(0, count // step, body, 0)
+    for n, (mine, got) in enumerate(((mine0, got0), (mine1, got1))):
+        start = n * count // 2
+
+        def body(i, _):
+            here = pl.multiple_of(i * step, step)
+            rows, to = pl.ds(here, step), pl.ds(start + here, step)
+            xhat = norm[pl.ds(WIDE + start + here, step), pl.ds(at, half)]
+            d = mine[rows, :] + got[rows, :].astype(f32)
+            total[to, :] = d
+            stats[to, :] = paired(d, d * xhat.astype(f32))
+            return 0
+
+        lax.fori_loop(0, count // 2 // step, body, 0, unroll=2)
+
+
+def written(result, buffer, sem, part):
+    count, step = buffer.shape[0], buffer.shape[0] // sem.shape[0]
+    copies = []
+    for i in range(sem.shape[0]):
+        rows = slice(i * step, (i + 1) * step)
+        buffer[rows, :] = part(i * step, step)
+        copies.append(pltpu.make_async_copy(buffer.at[rows], result.at[rows], sem.at[i]))
+        copies[-1].start()
+    for c in copies:
+        c.wait()
+
+
+def input_rows(info, ct, total, norm, rstd, own, other, result, buffer, sem):
+    count, half = total.shape
+    at = halves_at(info, half)[0]
+
+    def part(first, step):
+        rows = slice(first, first + step)
+        xhat = norm[WIDE + first : WIDE + first + step, pl.ds(at, half)].astype(f32)
+        sums = (own[rows, :] + other[rows, :]) / (2 * half)
+        mean, cross = sums[:, :1], sums[:, LANES // 2 : LANES // 2 + 1]
+        gradient = rstd[rows, :1] * (total[rows, :] - mean - xhat * cross)
+        return (ct[rows, :].astype(f32) + gradient).astype(bf16)
+
+    written(result, buffer, sem, part)
+
+
+def output_rows(info, x, mine, got, result, buffer, sem):
+    def part(first, step):
+        rows = slice(first, first + step)
+        return (x[rows, :].astype(f32) + mine[rows, :] + got[rows, :].astype(f32)).astype(bf16)
+
+    written(result, buffer, sem, part)
 
 
 def shards(inputs, lengths, cotangent, w_value, w_gate, kernel, w_out):
@@ -432,33 +594,52 @@
     up = [(i, i + 1) for i in range(peers - 1)]
     down = [(j, i) for i, j in up]
     x_other, ct_other = swap(x, "tensor"), swap(ct, "tensor")
-    before = lax.ppermute(jnp.concatenate([x[-WIDE:], ct[-NEAR:]]), "seq", up)
-    after = lax.ppermute(jnp.concatenate([x[:WIDE], ct[:NEAR]]), "seq", down)
-    halo = jnp.concatenate([before, after])
+    last, first, mark = run(
+        pick,
+        info,
+        [x, ct],
+        [((WIDE + NEAR, channels), bf16)] * 2,
+        scratch=[pltpu.SemaphoreType.DMA((4,))],
+        space=HBM,
+    )
+    before, after = lax.ppermute(last, "seq", up), lax.ppermute(first, "seq", down)
+    moved = [x, ct, w_value, w_gate, w_out]
+    xv, ctv, wv, wg, wo, mark = run(
+        prepare,
+        info,
+        moved,
+        [(a.shape, bf16) for a in moved],
+        scratch=[pltpu.SemaphoreType.DMA((len(moved),))],
+        after=[mark],
+        space=HBM,
+    )
+
+    rows, ext = count + 2 * NEAR, count + 2 * WIDE
+    full, pull, mark = run(
+        upstream, info, [ctv, ct_other, wo], [((count, width), bf16), ((count, channels), bf16)]
+    )
+    halo, mark = run(
+        pack, info, [before, after], [((2 * (WIDE + NEAR), channels), bf16)], after=[mark]
+    )
     halo_other = swap(halo, "tensor")
-
-    rows, ext = count + 2 * NEAR, count + 2 * WIDE
-    full, pull = run(
-        upstream, info, [ct, ct_other, w_out], [((count, width), bf16), ((count, channels), f32)]
-    )
-    norm, rstd, hid, sig, slope, ends = run(
+    norm, rstd, hid, sig, slope, ends, _ = run(
         front,
         info,
-        [x, x_other, halo, halo_other, w_value, w_gate, w_out],
+        [xv, x_other, halo, halo_other, wv, wg, wo],
         [
             ((ext, width), bf16),
             ((count, LANES), f32),
             ((ext, channels), bf16),
-            ((count, channels), f32),
-            ((count, channels), f32),
+            ((count, channels), bf16),
+            ((count, channels), bf16),
             ((2 * NEAR, channels), f32),
         ],
         scratch=[pltpu.VMEM((2 * NEAR, width), bf16)],
-        after=[pull],
+        after=[mark],
     )
     row_sums = ((rows, LANES), f32)
     column = pltpu.VMEM((rows, LANES), f32)
-    conv, stats = run(
+    conv, stats, _ = run(
         depthwise,
         info,
         [hid, kernel],
@@ -466,7 +647,7 @@
         scratch=[pltpu.VMEM((ext + 16, LANES), f32), column, column],
     )
     stats_other = swap(stats, "tensor")
-    swished, dswish, stats2 = run(
+    swished, dswish, stats2, _ = run(
         swish,
         info,
         [conv, pull, ends, stats, stats_other],
@@ -475,90 +656,175 @@
     stats2_other = swap(stats2, "tensor")
 
     third = channels // 3
-    half_block = (width // 2, third)
-    halves = run(
-        functools.partial(out_terms, rows=block), info, [full, swished], [(half_block, bf16)] * 6
-    )
-    out_grad = scatter_sum([(halves[2 * i], halves[2 * i + 1]) for i in range(3)], block).T
-
-    dconvs, dvgs, halves = [], [], []
-    last = halves
+    *out_parts, mark = run(
+        functools.partial(out_terms, rows=block),
+        info,
+        [full, swished],
+        [((width // 2, third), bf16)] * 6,
+        scratch=[pltpu.VMEM((width, channels), bf16)],
+    )
+    out_got = [send_bit(out_parts[2 * i + 1], i) for i in range(3)]
+
+    def out_part(own, mark):
+        return run(
+            functools.partial(out_half, own=own),
+            info,
+            [swished, wo],
+            [((count, channels), f32 if own else bf16)],
+            after=[mark],
+        )
+
+    dconvs, dvgs, kept, got = [], [], [], []
     for i in range(3):
-        dconv, dvg, keep, send = run(
-            functools.partial(back, third=i, block=block),
+        dconv, dvg, product, mark = run(
+            functools.partial(back, third=i),
             info,
             [dswish, conv, stats, stats_other, stats2, stats2_other, kernel, sig, slope, norm],
+            [((rows, third), bf16), ((count, 2 * third), bf16), ((width, 2 * third), bf16)],
+            scratch=[pltpu.VMEM((rows + 16, LANES), f32), pltpu.VMEM((3, rows, LANES), f32)],
+            after=[mark],
+        )
+        if i == 0:
+            out_theirs, mark = out_part(False, mark)
+            out_other = swap(out_theirs, "tensor")
+            out_mine, mark = out_part(True, mark)
+        previous = (i + 2) % 3
+        vkeep, okeep, send, mark = run(
+            functools.partial(first_split, third=i, rows=block),
+            info,
+            [product, out_parts[2 * previous], out_got[previous]],
             [
-                ((rows, third), bf16),
-                ((count, 2 * third), bf16),
                 ((width // 2, 2 * third), bf16),
-                ((width // 2, 2 * third), bf16),
+                ((width // 4, third), bf16),
+                ((width // 2 + width // 8, 2 * third), bf16),
             ],
-            scratch=[pltpu.VMEM((rows + 16, LANES), f32), pltpu.VMEM((3, rows, LANES), f32)],
-            after=last,
-        )
-        last = [send]
+            after=[mark, *out_got],
+        )
         dconvs.append(dconv)
         dvgs.append(dvg)
-        halves.append((keep, send))
-    grads = scatter_sum(halves, block)
-    value_grad, gate_grad = (
-        jnp.concatenate([grads[:, (2 * i + j) * third :][:, :third] for i in range(3)], axis=1)
-        for j in (0, 1)
-    )
-    kernel_grad = jnp.concatenate(
-        [
-            run(
-                functools.partial(taps_sums, third=i),
-                info,
-                [dconvs[i], hid],
-                [((taps, third), f32)],
-                scratch=[pltpu.VMEM((rows + 16, LANES), f32), pltpu.VMEM((taps, 8, LANES), f32)],
-                after=last,
-            )[0]
-            for i in range(3)
-        ],
-        axis=1,
-    )
-    for bit in every:
-        kernel_grad = kernel_grad + swap(kernel_grad, *bit)
-
-    theirs, mine = (
-        run(
+        kept.append((vkeep, okeep))
+        got.append(send_bit(send, i))
+
+    def second(i, mark):
+        vkeep, okeep, send, mark = run(
+            functools.partial(second_split, third=i, rows=block),
+            info,
+            [*kept[i], got[i]],
+            [
+                ((width // 4, 2 * third), bf16),
+                ((width // 8, third), bf16),
+                ((width // 4 + width // 16, 2 * third), bf16),
+            ],
+            scratch=[pltpu.VMEM((width // 4, third), bf16)],
+            after=[mark],
+        )
+        kept[i], got[i] = (vkeep, okeep), send_bit(send, (i + 1) % 3)
+        return mark
+
+    def third_step(i, mark):
+        vkeep, okeep, send, mark = run(
+            functools.partial(third_split, third=i, rows=block),
+            info,
+            [*kept[i], got[i]],
+            [
+                ((width // 8, 2 * third), bf16),
+                ((width // 8, third), bf16),
+                ((width // 8, 2 * third), bf16),
+            ],
+            scratch=[pltpu.VMEM((width // 8, third), bf16)],
+            after=[mark],
+        )
+        kept[i], got[i] = (vkeep, okeep), send_bit(send, (i + 2) % 3)
+        return mark
+
+    def last_step(i, mark):
+        keep, send, mark = run(
+            functools.partial(last_split, rows=block),
+            info,
+            [*kept[i], got[i]],
+            [((width // 16, 3 * third), bf16)] * 2,
+            after=[mark],
+        )
+        return finish(keep, send, block), mark
+
+    def norm_part(own, mark):
+        return run(
             functools.partial(norm_half, own=own),
             info,
-            [*dvgs, w_value, w_gate],
-            [((count, channels), f32 if own else bf16)],
-            after=last,
-        )[0]
-        for own in (False, True)
-    )
-    dnorm, stats3 = run(
+            [*dvgs, wv, wg],
+            [((count // 2, channels), f32 if own else bf16)] * 2,
+            after=[mark],
+        )
+
+    def taps_part(i, mark):
+        return run(
+            functools.partial(taps_sums, third=i),
+            info,
+            [dconvs[i], hid],
+            [((taps, third), f32)],
+            scratch=[pltpu.VMEM((rows + 16, LANES), f32), pltpu.VMEM((taps, 8, LANES), f32)],
+            after=[mark],
+        )
+
+    def final(kernel, args, mark):
+        return run(
+            kernel,
+            info,
+            args,
+            [((count, channels), bf16)],
+            scratch=[pltpu.VMEM((count, channels), bf16), pltpu.SemaphoreType.DMA((4,))],
+            after=[mark],
+            to=HBM,
+        )
+
+    def taps_step(bit, value, mark):
+        return run(
+            add_taps, info, [value, send_bit(value, bit)], [(value.shape, f32)], after=[mark]
+        )
+
+    parts = []
+    for i in range(3):
+        part, mark = taps_part(i, mark)
+        parts.append(part)
+    kernel_grad = jnp.concatenate(parts, axis=1)
+    *theirs, mark = norm_part(False, mark)
+    theirs = [swap(t, "tensor") for t in theirs]
+    *mine, mark = norm_part(True, mark)
+    mark = second(0, mark)
+    kernel_grad, mark = taps_step(0, kernel_grad, mark)
+    mark = second(1, mark)
+    dnorm, stats3, mark = run(
         norm_sums,
         info,
-        [mine, swap(theirs, "tensor"), norm],
+        [*mine, *theirs, norm],
         [((count, channels), f32), ((count, LANES), f32)],
-    )
-    sums = (stats3 + swap(stats3, "tensor")) / width
-    xhat = lax.dynamic_slice(norm, (WIDE, core * channels), (count, channels)).astype(f32)
-    input_gradient = ct.astype(f32) + rstd[:, :1] * (
-        dnorm - sums[:, :1] - xhat * sums[:, LANES // 2 : LANES // 2 + 1]
-    )
-
-    theirs, mine = (
-        run(
-            functools.partial(out_half, own=own),
-            info,
-            [swished, w_out],
-            [((count, channels), f32 if own else bf16)],
-            after=last,
-        )[0]
-        for own in (False, True)
-    )
-    output = x.astype(f32) + mine + swap(theirs, "tensor").astype(f32)
+        after=[mark],
+    )
+    stats3_other = swap(stats3, "tensor")
+    output, mark = final(output_rows, [x, out_mine, out_other], mark)
+    kernel_grad, mark = taps_step(1, kernel_grad, mark)
+    mark = second(2, mark)
+    input_gradient, mark = final(
+        input_rows, [ct, dnorm, norm, rstd, stats3, stats3_other], mark
+    )
+    mark = third_step(0, mark)
+    kernel_grad, mark = taps_step(2, kernel_grad, mark)
+    for i in (1, 2):
+        mark = third_step(i, mark)
+    for bit in range(3, len(every)):
+        kernel_grad, mark = taps_step(bit, kernel_grad, mark)
+    totals = []
+    for i in range(3):
+        total, mark = last_step(i, mark)
+        totals.append(total)
+    value_grad, gate_grad = (
+        jnp.concatenate([t[:, j * third : (j + 1) * third] for t in totals], axis=1)
+        for j in (0, 1)
+    )
+    out_grad = jnp.concatenate([totals[(i + 1) % 3][:, 2 * third :] for i in range(3)], axis=1).T
     return (
-        output.astype(bf16)[None],
-        input_gradient.astype(bf16)[None],
+        output[None],
+        input_gradient[None],
         value_grad,
         gate_grad,
         kernel_grad,

time: 214 us -> 151 us (0.71)
  local copies, waits for them, and re-layouts: 35.6 us -> 0.82 us
  waiting for transfers between devices: 51.7 us -> 37.6 us
  other arithmetic: 15.2 us -> 1.68 us
  Pallas kernels: 69 us -> 80.1 us
  starting transfers between devices: 39.6 us -> 29.2 us
    unnamed x113 -> x9, local copies, waits for them, and re-layouts: 31.1 us -> 0.67 us
    pallas_call x16 -> x37, Pallas kernels: 69 us -> 80.1 us  [run(): pl.pallas_call(body, in_specs=[SMEM] + [space] * len(args) + [ANY] * len(...]
    ppermute x32 -> x28, starting transfers between devices: 33.5 us -> 23.1 us  [swap(): return lax.ppermute(value, axis, [(i, i ^ 1 << bit) for i in range(size)])]
    ppermute x32 -> x28, waiting for transfers between devices: 46.8 us -> 37.6 us  [swap(): return lax.ppermute(value, axis, [(i, i ^ 1 << bit) for i in range(size)])]
    convert_element_type x18 -> x0, other arithmetic: 7.77 us -> none  [merge(): value = value.astype(bf16)]
    ppermute x2, waiting for transfers between devices: 4.94 us -> 0.01 us  [the longest x1 0.01 us: shards(): lax.ppermute(last, 'seq', up)]
    slice x5 -> x3, local copies, waits for them, and re-layouts: 3.2 us -> 0.06 us  [shards(): totals[(i + 1) % 3][:, 2 * third:]]
    broadcast_in_dim x2 -> x0, other arithmetic: 3.13 us -> none  [the longest x1 1.73 us: shards(): input_gradient.astype(bf16)[None]]
  transfers between devices with their start and end apart: 34 -> 30, of which waited for: 12 -> 12; matrix products, arithmetic and copies ran while one was open for 9% -> 1% of each run, Pallas kernels for 18% -> 38%
where the time goes in v4:
time: 151 us
  Pallas kernels  80.1 us (53%)
  waiting for transfers between devices  37.6 us (25%)
  starting transfers between devices  29.2 us (19%)
  between operations  1.71 us (1%)
  other arithmetic  1.68 us (1%)
    pallas_call x37, Pallas kernels, run(): pl.pallas_call(body, in_specs=[SMEM] + [space] * len(args) + [ANY] * len(...  80.1 us
    ppermute x28, waiting for transfers between devices, swap(): return lax.ppermute(value, axis, [(i, i ^ 1 << bit) for i in range(size)])  37.6 us
    ppermute x28, starting transfers between devices, swap(): return lax.ppermute(value, axis, [(i, i ^ 1 << bit) for i in range(size)])  23.1 us
    ppermute x1, starting transfers between devices, shards(): lax.ppermute(last, 'seq', up)  4.85 us
  transfers between devices with their start and end apart: 30, of which 12 were waited for; matrix products, arithmetic and copies ran while one was open for 1% of the time, Pallas kernels for 38%

profile of v4, /device:TPU:0, one launch (start us, length us, event | category | flops | bytes accessed | tf_op | source)
XLA Modules:
  0.0 151.2 jit_solution(11727270090211646583)
XLA Ops:
  3.4 4.9 %collective-permute-start.1 = (bf16[48,768]{1,0:T(8,128)(2,1)S(1)}, bf16[48,768]{1,0:T(8,128)(2,1)S(1)}, u32[]{:S(2)}, u32[]{:S(2)}) collective-permute-start(bf16[48,768]{1,0:T(8,128)(2,1)S(1)} %get-tuple-element.126), channel_id=1, source_target_pairs={{0,4},{4,8},{8,12},{12,16},{16,20},{20,24},{24,28},{1,5},{5,9},{9,... | collective-permute-start | bytes 221192 | tf_op jit(solution)/shard_map/ppermute | solution.py:605
  9.6 5.0 %prepare.1 = (bf16[768,768]{1,0:T(8,128)(2,1)S(1)}, bf16[768,768]{1,0:T(8,128)(2,1)S(1)}, bf16[1536,768]{1,0:T(8,128)(2,1)S(1)}, bf16[1536,768]{1,0:T(8,128)(2,1...) custom-call(s32[8]{0:T(128)S(1)} %stack.27.refs_0_, bf16[768,768]{1,0:T(8,128)(2,1)} %bitcast.18, ...), custom_call_target="tpu_custom_call" | custom-call | flops 1024 | bytes 1024 | tf_op jit(solution)/shard_map/prepare/pallas_call | solution.py:35
  14.5 2.7 %upstream.1 = (bf16[768,1536]{1,0:T(8,128)(2,1)S(1)}, bf16[768,768]{1,0:T(8,128)(2,1)S(1)}, f32[8,128]{1,0:T(8,128)S(1)}) custom-call(s32[8]{0:T(128)S(1)} %stack.27.refs_0_, bf16[768,768]{1,0:T(8,128)(2,1)S(1)} %get-tuple-element.128.refs_1_, bf16[768,768]{1,0:T(8,128)(2,1)S(1)} %collective-permute-done.3.refs_2_, ...), custom_call_target="tpu_custom_call" | custom-call | flops 1024 | bytes 1024 | tf_op jit(solution)/shard_map/upstream/pallas_call | solution.py:35
  19.2 7.8 %front.1 = (bf16[832,1536]{1,0:T(8,128)(2,1)S(1)}, f32[768,128]{1,0:T(8,128)S(1)}, bf16[832,768]{1,0:T(8,128)(2,1)S(1)}, bf16[768,768]{1,0:T(8,128)(2,1)S(1)}, b...) custom-call(s32[8]{0:T(128)S(1)} %stack.27.refs_0_, ...), custom_call_target="tpu_custom_call" | custom-call | flops 1024 | bytes 1024 | tf_op jit(solution)/shard_map/front/pallas_call | solution.py:35
  27.0 7.0 %depthwise.1 = (f32[800,768]{1,0:T(8,128)S(1)}, f32[800,128]{1,0:T(8,128)S(1)}, f32[8,128]{1,0:T(8,128)}) custom-call(s32[8]{0:T(128)S(1)} %stack.27.refs_0_, bf16[832,768]{1,0:T(8,128)(2,1)S(1)} %get-tuple-element.135.refs_1_.refs_2_, bf16[31,768]{1,0:T(8,128)(2,1)S(1)} %copy-done.2), custom_call_target="tpu_custom_call" | custom-call | flops 1024 | bytes 1024 | tf_op jit(solution)/shard_map/depthwise/pallas_call | solution.py:35
  35.8 5.2 %swish.1 = (bf16[768,768]{1,0:T(8,128)(2,1)S(1)}, f32[800,768]{1,0:T(8,128)S(1)}, f32[800,128]{1,0:T(8,128)S(1)}, f32[8,128]{1,0:T(8,128)}) custom-call(s32[8]{0:T(128)S(1)} %stack.27.refs_0_, f32[800,768]{1,0:T(8,128)S(1)} %get-tuple-element.136.refs_1_.refs_2_, bf16[768,768]{1,0:T(8,128)(2,1)S(1)} %get-tuple-element.137.refs_2_, ...), custom_call_target="tpu_custom_call" | custom-call | flops 1024 | bytes 1024 | tf_op jit(solution)/shard_map/swish/pallas_call | solution.py:35
  41.2 2.8 %out_terms.1 = (bf16[768,256]{1,0:T(8,128)(2,1)S(1)}, bf16[768,256]{1,0:T(8,128)(2,1)S(1)}, bf16[768,256]{1,0:T(8,128)(2,1)S(1)}, bf16[768,256]{1,0:T(8,128)(2,1...) custom-call(s32[8]{0:T(128)S(1)} %stack.27.refs_0_, ...), custom_call_target="tpu_custom_call" | custom-call | flops 1024 | bytes 1024 | tf_op jit(solution)/shard_map/out_terms/pallas_call | solution.py:35
  44.0 3.7 %collective-permute-start.8 = (bf16[768,256]{1,0:T(8,128)(2,1)S(1)}, bf16[768,256]{1,0:T(8,128)(2,1)S(1)}, u32[]{:S(2)}, u32[]{:S(2)}) collective-permute-start(bf16[768,256]{1,0:T(8,128)(2,1)S(1)} %get-tuple-element.155), channel_id=1, source_target_pairs={{0,8},{4,12},{8,0},{12,4},{16,24},{20,28},{24,16},{28,20},{1,9},{5... | collective-permute-start | bytes 1179656 | tf_op jit(solution)/shard_map/ppermute | solution.py:54
  49.8 4.8 %back.3 = (bf16[800,256]{1,0:T(8,128)(2,1)S(1)}, bf16[768,512]{1,0:T(8,128)(2,1)S(1)}, bf16[1536,512]{1,0:T(8,128)(2,1)S(1)}, f32[8,128]{1,0:T(8,128)S(1)}) custom-call(s32[8]{0:T(128)S(1)} %stack.27.refs_0_, f32[800,768]{1,0:T(8,128)S(1)} %get-tuple-element.141.refs_1_, f32[800,768]{1,0:T(8,128)S(1)} %get-tuple-element.136.refs_1_.refs_2_, ...), custom_call_target="tpu_custom_call" | custom-call | flops 1024 | bytes 1024 | tf_op jit(solution)/shard_map/back/pallas_call | solution.py:35
  61.3 5.0 %back.4 = (bf16[800,256]{1,0:T(8,128)(2,1)S(1)}, bf16[768,512]{1,0:T(8,128)(2,1)S(1)}, bf16[1536,512]{1,0:T(8,128)(2,1)S(1)}, f32[8,128]{1,0:T(8,128)S(1)}) custom-call(s32[8]{0:T(128)S(1)} %stack.27.refs_0_, f32[800,768]{1,0:T(8,128)S(1)} %get-tuple-element.141.refs_1_, f32[800,768]{1,0:T(8,128)S(1)} %get-tuple-element.136.refs_1_.refs_2_, ...), custom_call_target="tpu_custom_call" | custom-call | flops 1024 | bytes 1024 | tf_op jit(solution)/shard_map/back/pallas_call | solution.py:35
  67.7 4.8 %back.5 = (bf16[800,256]{1,0:T(8,128)(2,1)S(1)}, bf16[768,512]{1,0:T(8,128)(2,1)S(1)}, bf16[1536,512]{1,0:T(8,128)(2,1)S(1)}, f32[8,128]{1,0:T(8,128)S(1)}) custom-call(s32[8]{0:T(128)S(1)} %stack.27.refs_0_, f32[800,768]{1,0:T(8,128)S(1)} %get-tuple-element.141.refs_1_, f32[800,768]{1,0:T(8,128)S(1)} %get-tuple-element.136.refs_1_.refs_2_, ...), custom_call_target="tpu_custom_call" | custom-call | flops 1024 | bytes 1024 | tf_op jit(solution)/shard_map/back/pallas_call | solution.py:35
  73.8 2.5 %taps_sums.3 = (f32[31,256]{1,0:T(8,128)S(1)}, f32[8,128]{1,0:T(8,128)S(1)}) custom-call(s32[8]{0:T(128)S(1)} %stack.27.refs_0_, bf16[800,256]{1,0:T(8,128)(2,1)S(1)} %get-tuple-element.168.refs_1_, bf16[832,768]{1,0:T(8,128)(2,1)S(1)} %get-tuple-element.135.refs_1_.refs_2_, f32[8,128]{1,0:T(8,128)S(1)} %get-tuple-element.172.refs_3_), custom_call_target="tpu_custom_call" | custom-call | flops 1024 | bytes 1024 | tf_op jit(solution)/shard_map/taps_sums/pallas_call | solution.py:35
  76.3 2.5 %taps_sums.4 = (f32[31,256]{1,0:T(8,128)S(1)}, f32[8,128]{1,0:T(8,128)S(1)}) custom-call(s32[8]{0:T(128)S(1)} %stack.27.refs_0_, bf16[800,256]{1,0:T(8,128)(2,1)S(1)} %get-tuple-element.167.refs_1_, bf16[832,768]{1,0:T(8,128)(2,1)S(1)} %get-tuple-element.135.refs_1_.refs_2_, f32[8,128]{1,0:T(8,128)S(1)} %get-tuple-element.173.refs_3_), custom_call_target="tpu_custom_call" | custom-call | flops 1024 | bytes 1024 | tf_op jit(solution)/shard_map/taps_sums/pallas_call | solution.py:35
  78.8 2.5 %taps_sums.5 = (f32[31,256]{1,0:T(8,128)S(1)}, f32[8,128]{1,0:T(8,128)S(1)}) custom-call(s32[8]{0:T(128)S(1)} %stack.27.refs_0_, bf16[800,256]{1,0:T(8,128)(2,1)S(1)} %get-tuple-element.166.refs_1_, bf16[832,768]{1,0:T(8,128)(2,1)S(1)} %get-tuple-element.135.refs_1_.refs_2_, f32[8,128]{1,0:T(8,128)S(1)} %get-tuple-element.174.refs_3_), custom_call_target="tpu_custom_call" | custom-call | flops 1024 | bytes 1024 | tf_op jit(solution)/shard_map/taps_sums/pallas_call | solution.py:35
  82.9 2.6 %norm_half.2 = (bf16[384,768]{1,0:T(8,128)(2,1)S(1)}, bf16[384,768]{1,0:T(8,128)(2,1)S(1)}, f32[8,128]{1,0:T(8,128)S(1)}) custom-call(s32[8]{0:T(128)S(1)} %stack.27.refs_0_, bf16[768,512]{1,0:T(8,128)(2,1)S(1)} %get-tuple-element.152.refs_1_, bf16[768,512]{1,0:T(8,128)(2,1)S(1)} %get-tuple-element.160.refs_2_, ...), custom_call_target="tpu_custom_call" | custom-call | flops 1024 | bytes 1024 | tf_op jit(solution)/shard_map/norm_half/pallas_call | solution.py:35
  86.6 2.6 %norm_half.3 = (f32[384,768]{1,0:T(8,128)S(1)}, f32[384,768]{1,0:T(8,128)S(1)}, f32[8,128]{1,0:T(8,128)S(1)}) custom-call(s32[8]{0:T(128)S(1)} %stack.27.refs_0_, bf16[768,512]{1,0:T(8,128)(2,1)S(1)} %get-tuple-element.152.refs_1_, bf16[768,512]{1,0:T(8,128)(2,1)S(1)} %get-tuple-element.160.refs_2_, bf16[768,512]{1,0:T(8,128)(2,1)S(1)} %get-tuple-element.165.refs_3_, ...), custom_call_target="tpu_custom_call" | custom-call | flops 1024 | bytes 1024 | tf_op jit(solution)/shard_map/norm_half/pallas_call | solution.py:35
  93.4 2.0 %norm_sums.1 = (f32[768,768]{1,0:T(8,128)S(1)}, f32[768,128]{1,0:T(8,128)S(1)}, f32[8,128]{1,0:T(8,128)S(1)}) custom-call(s32[8]{0:T(128)S(1)} %stack.27.refs_0_, f32[384,768]{1,0:T(8,128)S(1)} %get-tuple-element.177.refs_1_, f32[384,768]{1,0:T(8,128)S(1)} %get-tuple-element.178.refs_2_, bf16[384,768]{1,0:T(8,128)(2,1)S(1)} %collective-permute-done.11.refs_3_, ...), custom_call_target="tpu_custom_call" | custom-call | flops 1024 | bytes 1024 | tf_op jit(solution)/shard_map/norm_sums/pallas_call | solution.py:35
  99.1 7.1 %collective-permute-done.18.refs_2_ = f32[31,768]{1,0:T(8,128)S(1)} collective-permute-done((f32[31,768]{1,0:T(8,128)S(1)}, f32[31,768]{1,0:T(8,128)S(1)}, u32[]{:S(2)}, u32[]{:S(2)}) %collective-permute-start.18) | collective-permute-done | bytes 95264 | tf_op jit(solution)/shard_map/ppermute | solution.py:54
  109.2 2.2 %input_rows.1 = (bf16[768,768]{1,0:T(8,128)(2,1)}, f32[8,128]{1,0:T(8,128)S(1)}) custom-call(s32[8]{0:T(128)S(1)} %stack.27.refs_0_, bf16[768,768]{1,0:T(8,128)(2,1)S(1)} %bitcast.15, f32[768,768]{1,0:T(8,128)S(1)} %get-tuple-element.196.refs_2_, bf16[832,1536]{1,0:T(8,128)(2,1)S(1)} %get-tuple-element.145.refs_10_.refs_5_.refs_3_, ...), custom_call_target="tpu_custom_call" | custom-call | flops 1024 | bytes 1024 | tf_op jit(solution)/shard_map/input_rows/pallas_call | solution.py:35
  114.1 5.5 %collective-permute-done.21.refs_2_ = f32[31,768]{1,0:T(8,128)S(1)} collective-permute-done((f32[31,768]{1,0:T(8,128)S(1)}, f32[31,768]{1,0:T(8,128)S(1)}, u32[]{:S(2)}, u32[]{:S(2)}) %collective-permute-start.21) | collective-permute-done | bytes 95264 | tf_op jit(solution)/shard_map/ppermute | solution.py:54
  120.2 2.6 %collective-permute-start.22 = (f32[31,768]{1,0:T(8,128)S(1)}, f32[31,768]{1,0:T(8,128)S(1)}, u32[]{:S(2)}, u32[]{:S(2)}) collective-permute-start(f32[31,768]{1,0:T(8,128)S(1)} %get-tuple-element.216.refs_1_), channel_id=1, source_target_pairs={{0,16},{4,20},{8,24},{12,28},{16,0},{20,4},{24,8},{28,12},{1,17},{... | collective-permute-start | bytes 285704 | tf_op jit(solution)/shard_map/ppermute | solution.py:54
  124.7 2.1 %collective-permute-done.22.refs_2_ = f32[31,768]{1,0:T(8,128)S(1)} collective-permute-done((f32[31,768]{1,0:T(8,128)S(1)}, f32[31,768]{1,0:T(8,128)S(1)}, u32[]{:S(2)}, u32[]{:S(2)}) %collective-permute-start.22) | collective-permute-done | bytes 95264 | tf_op jit(solution)/shard_map/ppermute | solution.py:54
  132.2 6.9 %collective-permute-done.25 = bf16[96,768]{1,0:T(8,128)(2,1)S(1)} collective-permute-done((bf16[96,768]{1,0:T(8,128)(2,1)S(1)}, bf16[96,768]{1,0:T(8,128)(2,1)S(1)}, u32[]{:S(2)}, u32[]{:S(2)}) %collective-permute-start.25) | collective-permute-done | bytes 147488 | tf_op jit(solution)/shard_map/ppermute | solution.py:54
  141.9 7.6 %collective-permute-done.29 = bf16[96,768]{1,0:T(8,128)(2,1)S(1)} collective-permute-done((bf16[96,768]{1,0:T(8,128)(2,1)S(1)}, bf16[96,768]{1,0:T(8,128)(2,1)S(1)}, u32[]{:S(2)}, u32[]{:S(2)}) %collective-permute-start.29) | collective-permute-done | bytes 147488 | tf_op jit(solution)/shard_map/ppermute | solution.py:54
  (92 shorter events, 47.3 us)
Async XLA Ops:
  0.6 13.9 %collective-permute-start.3 = (bf16[768,768]{1,0:T(8,128)(2,1)}, bf16[768,768]{1,0:T(8,128)(2,1)S(1)}, u32[]{:S(2)}, u32[]{:S(2)}) collective-permute-start(bf16[768,768]{1,0:T(8,128)(2,1)} %bitcast.12), channel_id=1, source_target_pairs={{0,2},{2,0},{1,3},{3,1},{4,6},{6,4},{5,7},{7,5},{8,10},{10,8},{9,1... | collective-permute-start | bytes 3538952 | tf_op jit(solution)/shard_map/ppermute | solution.py:54
  1.1 16.7 %collective-permute-start = (bf16[768,768]{1,0:T(8,128)(2,1)}, bf16[768,768]{1,0:T(8,128)(2,1)S(1)}, u32[]{:S(2)}, u32[]{:S(2)}) collective-permute-start(bf16[768,768]{1,0:T(8,128)(2,1)} %bitcast.16), channel_id=1, source_target_pairs={{0,2},{2,0},{1,3},{3,1},{4,6},{6,4},{5,7},{7,5},{8,10},{10,8},{9,1... | collective-permute-start | bytes 3538952 | tf_op jit(solution)/shard_map/ppermute | solution.py:54
  3.4 13.8 %collective-permute-start.1 = (bf16[48,768]{1,0:T(8,128)(2,1)S(1)}, bf16[48,768]{1,0:T(8,128)(2,1)S(1)}, u32[]{:S(2)}, u32[]{:S(2)}) collective-permute-start(bf16[48,768]{1,0:T(8,128)(2,1)S(1)} %get-tuple-element.126), channel_id=1, source_target_pairs={{0,4},{4,8},{8,12},{12,16},{16,20},{20,24},{24,28},{1,5},{5,9},{9,... | collective-permute-start | bytes 221192 | tf_op jit(solution)/shard_map/ppermute | solution.py:605
  8.3 9.0 %collective-permute-start.2 = (bf16[48,768]{1,0:T(8,128)(2,1)S(1)}, bf16[48,768]{1,0:T(8,128)(2,1)S(1)}, u32[]{:S(2)}, u32[]{:S(2)}) collective-permute-start(bf16[48,768]{1,0:T(8,128)(2,1)S(1)} %get-tuple-element.127), channel_id=1, source_target_pairs={{4,0},{8,4},{12,8},{16,12},{20,16},{24,20},{28,24},{5,1},{9,5},{13... | collective-permute-start | bytes 221192 | tf_op jit(solution)/shard_map/ppermute | solution.py:605
  41.1 8.7 %collective-permute-start.6 = (f32[800,128]{1,0:T(8,128)S(1)}, f32[800,128]{1,0:T(8,128)S(1)}, u32[]{:S(2)}, u32[]{:S(2)}) collective-permute-start(f32[800,128]{1,0:T(8,128)S(1)} %get-tuple-element.142.refs_5_), channel_id=1, source_target_pairs={{0,2},{2,0},{1,3},{3,1},{4,6},{6,4},{5,7},{7,5},{8,10},{10,8},{9,1... | collective-permute-start | bytes 1228808 | tf_op jit(solution)/shard_map/ppermute | solution.py:54
  44.0 13.8 %collective-permute-start.8 = (bf16[768,256]{1,0:T(8,128)(2,1)S(1)}, bf16[768,256]{1,0:T(8,128)(2,1)S(1)}, u32[]{:S(2)}, u32[]{:S(2)}) collective-permute-start(bf16[768,256]{1,0:T(8,128)(2,1)S(1)} %get-tuple-element.155), channel_id=1, source_target_pairs={{0,8},{4,12},{8,0},{12,4},{16,24},{20,28},{24,16},{28,20},{1,9},{5... | collective-permute-start | bytes 1179656 | tf_op jit(solution)/shard_map/ppermute | solution.py:54
  47.6 11.1 %collective-permute-start.9 = (bf16[768,256]{1,0:T(8,128)(2,1)S(1)}, bf16[768,256]{1,0:T(8,128)(2,1)S(1)}, u32[]{:S(2)}, u32[]{:S(2)}) collective-permute-start(bf16[768,256]{1,0:T(8,128)(2,1)S(1)} %get-tuple-element.157), channel_id=1, source_target_pairs={{0,1},{1,0},{2,3},{3,2},{4,5},{5,4},{6,7},{7,6},{8,9},{9,8},{10,11... | collective-permute-start | bytes 1179656 | tf_op jit(solution)/shard_map/ppermute | solution.py:54
  49.1 10.8 %collective-permute-start.10 = (bf16[768,256]{1,0:T(8,128)(2,1)S(1)}, bf16[768,256]{1,0:T(8,128)(2,1)S(1)}, u32[]{:S(2)}, u32[]{:S(2)}) collective-permute-start(bf16[768,256]{1,0:T(8,128)(2,1)S(1)} %get-tuple-element.158), channel_id=1, source_target_pairs={{0,4},{4,0},{8,12},{12,8},{16,20},{20,16},{24,28},{28,24},{1,5},{5... | collective-permute-start | bytes 1179656 | tf_op jit(solution)/shard_map/ppermute | solution.py:54
  60.7 25.4 %collective-permute-start.15 = (bf16[960,512]{1,0:T(8,128)(2,1)S(1)}, bf16[960,512]{1,0:T(8,128)(2,1)S(1)}, u32[]{:S(2)}, u32[]{:S(2)}) collective-permute-start(bf16[960,512]{1,0:T(8,128)(2,1)S(1)} %get-tuple-element.189), channel_id=1, source_target_pairs={{0,1},{1,0},{2,3},{3,2},{4,5},{5,4},{6,7},{7,6},{8,9},{9,8},{10,11... | collective-permute-start | bytes 2949128 | tf_op jit(solution)/shard_map/ppermute | solution.py:54
  61.3 35.6 %collective-permute-start.7 = (bf16[768,768]{1,0:T(8,128)(2,1)S(1)}, bf16[768,768]{1,0:T(8,128)(2,1)S(1)}, u32[]{:S(2)}, u32[]{:S(2)}) collective-permute-start(bf16[768,768]{1,0:T(8,128)(2,1)S(1)} %get-tuple-element.151), channel_id=1, source_target_pairs={{0,2},{2,0},{1,3},{3,1},{4,6},{6,4},{5,7},{7,5},{8,10},{10,8},{9,1... | collective-permute-start | bytes 3538952 | tf_op jit(solution)/shard_map/ppermute | solution.py:54
  67.0 24.2 %collective-permute-start.13 = (bf16[960,512]{1,0:T(8,128)(2,1)S(1)}, bf16[960,512]{1,0:T(8,128)(2,1)S(1)}, u32[]{:S(2)}, u32[]{:S(2)}) collective-permute-start(bf16[960,512]{1,0:T(8,128)(2,1)S(1)} %get-tuple-element.183), channel_id=1, source_target_pairs={{0,4},{4,0},{8,12},{12,8},{16,20},{20,16},{24,28},{28,24},{1,5},{5... | collective-permute-start | bytes 2949128 | tf_op jit(solution)/shard_map/ppermute | solution.py:54
  73.3 33.5 %collective-permute-start.17 = (bf16[960,512]{1,0:T(8,128)(2,1)S(1)}, bf16[960,512]{1,0:T(8,128)(2,1)S(1)}, u32[]{:S(2)}, u32[]{:S(2)}) collective-permute-start(bf16[960,512]{1,0:T(8,128)(2,1)S(1)} %get-tuple-element.201), channel_id=1, source_target_pairs={{0,8},{4,12},{8,0},{12,4},{16,24},{20,28},{24,16},{28,20},{1,9},{5... | collective-permute-start | bytes 2949128 | tf_op jit(solution)/shard_map/ppermute | solution.py:54
  86.1 7.3 %collective-permute-start.11 = (bf16[384,768]{1,0:T(8,128)(2,1)S(1)}, bf16[384,768]{1,0:T(8,128)(2,1)S(1)}, u32[]{:S(2)}, u32[]{:S(2)}) collective-permute-start(bf16[384,768]{1,0:T(8,128)(2,1)S(1)} %get-tuple-element.179), channel_id=1, source_target_pairs={{0,2},{2,0},{1,3},{3,1},{4,6},{6,4},{5,7},{7,5},{8,10},{10,8},{9,1... | collective-permute-start | bytes 1769480 | tf_op jit(solution)/shard_map/ppermute | solution.py:54
  86.1 7.3 %collective-permute-start.12 = (bf16[384,768]{1,0:T(8,128)(2,1)S(1)}, bf16[384,768]{1,0:T(8,128)(2,1)S(1)}, u32[]{:S(2)}, u32[]{:S(2)}) collective-permute-start(bf16[384,768]{1,0:T(8,128)(2,1)S(1)} %get-tuple-element.180), channel_id=1, source_target_pairs={{0,2},{2,0},{1,3},{3,1},{4,6},{6,4},{5,7},{7,5},{8,10},{10,8},{9,1... | collective-permute-start | bytes 1769480 | tf_op jit(solution)/shard_map/ppermute | solution.py:54
  91.3 20.1 %collective-permute-start.19 = (bf16[480,512]{1,0:T(8,128)(2,1)S(1)}, bf16[480,512]{1,0:T(8,128)(2,1)S(1)}, u32[]{:S(2)}, u32[]{:S(2)}) collective-permute-start(bf16[480,512]{1,0:T(8,128)(2,1)S(1)} %get-tuple-element.209), channel_id=1, source_target_pairs={{0,4},{4,0},{8,12},{12,8},{16,20},{20,16},{24,28},{28,24},{1,5},{5... | collective-permute-start | bytes 1474568 | tf_op jit(solution)/shard_map/ppermute | solution.py:54
  95.4 13.8 %collective-permute-start.16 = (f32[768,128]{1,0:T(8,128)S(1)}, f32[768,128]{1,0:T(8,128)S(1)}, u32[]{:S(2)}, u32[]{:S(2)}) collective-permute-start(f32[768,128]{1,0:T(8,128)S(1)} %get-tuple-element.198.refs_5_), channel_id=1, source_target_pairs={{0,2},{2,0},{1,3},{3,1},{4,6},{6,4},{5,7},{7,5},{8,10},{10,8},{9,1... | collective-permute-start | bytes 1179656 | tf_op jit(solution)/shard_map/ppermute | solution.py:54
  95.5 10.8 %collective-permute-start.18 = (f32[31,768]{1,0:T(8,128)S(1)}, f32[31,768]{1,0:T(8,128)S(1)}, u32[]{:S(2)}, u32[]{:S(2)}) collective-permute-start(f32[31,768]{1,0:T(8,128)S(1)} %get-tuple-element.202.refs_1_), channel_id=1, source_target_pairs={{0,4},{4,0},{8,12},{12,8},{16,20},{20,16},{24,28},{28,24},{1,5},{5... | collective-permute-start | bytes 285704 | tf_op jit(solution)/shard_map/ppermute | solution.py:54
  96.9 25.9 %collective-permute-start.24 = (bf16[480,512]{1,0:T(8,128)(2,1)S(1)}, bf16[480,512]{1,0:T(8,128)(2,1)S(1)}, u32[]{:S(2)}, u32[]{:S(2)}) collective-permute-start(bf16[480,512]{1,0:T(8,128)(2,1)S(1)} %get-tuple-element.222), channel_id=1, source_target_pairs={{0,8},{4,12},{8,0},{12,4},{16,24},{20,28},{24,16},{28,20},{1,9},{5... | collective-permute-start | bytes 1474568 | tf_op jit(solution)/shard_map/ppermute | solution.py:54
  107.6 16.5 %collective-permute-start.23 = (bf16[480,512]{1,0:T(8,128)(2,1)S(1)}, bf16[480,512]{1,0:T(8,128)(2,1)S(1)}, u32[]{:S(2)}, u32[]{:S(2)}) collective-permute-start(bf16[480,512]{1,0:T(8,128)(2,1)S(1)} %get-tuple-element.219), channel_id=1, source_target_pairs={{0,1},{1,0},{2,3},{3,2},{4,5},{5,4},{6,7},{7,6},{8,9},{9,8},{10,11... | collective-permute-start | bytes 1474568 | tf_op jit(solution)/shard_map/ppermute | solution.py:54
  112.0 15.3 %collective-permute-start.20 = (bf16[192,512]{1,0:T(8,128)(2,1)S(1)}, bf16[192,512]{1,0:T(8,128)(2,1)S(1)}, u32[]{:S(2)}, u32[]{:S(2)}) collective-permute-start(bf16[192,512]{1,0:T(8,128)(2,1)S(1)} %get-tuple-element.213), channel_id=1, source_target_pairs={{0,8},{4,12},{8,0},{12,4},{16,24},{20,28},{24,16},{28,20},{1,9},{5... | collective-permute-start | bytes 589832 | tf_op jit(solution)/shard_map/ppermute | solution.py:54
  128.0 11.1 %collective-permute-start.25 = (bf16[96,768]{1,0:T(8,128)(2,1)S(1)}, bf16[96,768]{1,0:T(8,128)(2,1)S(1)}, u32[]{:S(2)}, u32[]{:S(2)}) collective-permute-start(bf16[96,768]{1,0:T(8,128)(2,1)S(1)} %get-tuple-element.228), channel_id=1, source_target_pairs={{0,16},{4,20},{8,24},{12,28},{16,0},{20,4},{24,8},{28,12},{1,17},{... | collective-permute-start | bytes 442376 | tf_op jit(solution)/shard_map/ppermute | solution.py:54
  130.9 9.8 %collective-permute-start.27 = (bf16[96,768]{1,0:T(8,128)(2,1)S(1)}, bf16[96,768]{1,0:T(8,128)(2,1)S(1)}, u32[]{:S(2)}, u32[]{:S(2)}) collective-permute-start(bf16[96,768]{1,0:T(8,128)(2,1)S(1)} %get-tuple-element.234), channel_id=1, source_target_pairs={{0,16},{4,20},{8,24},{12,28},{16,0},{20,4},{24,8},{28,12},{1,17},{... | collective-permute-start | bytes 442376 | tf_op jit(solution)/shard_map/ppermute | solution.py:54
  132.2 8.5 %collective-permute-start.28 = (bf16[192,512]{1,0:T(8,128)(2,1)S(1)}, bf16[192,512]{1,0:T(8,128)(2,1)S(1)}, u32[]{:S(2)}, u32[]{:S(2)}) collective-permute-start(bf16[192,512]{1,0:T(8,128)(2,1)S(1)} %get-tuple-element.237), channel_id=1, source_target_pairs={{0,4},{4,0},{8,12},{12,8},{16,20},{20,16},{24,28},{28,24},{1,5},{5... | collective-permute-start | bytes 589832 | tf_op jit(solution)/shard_map/ppermute | solution.py:54
  141.9 7.6 %collective-permute-start.29 = (bf16[96,768]{1,0:T(8,128)(2,1)S(1)}, bf16[96,768]{1,0:T(8,128)(2,1)S(1)}, u32[]{:S(2)}, u32[]{:S(2)}) collective-permute-start(bf16[96,768]{1,0:T(8,128)(2,1)S(1)} %get-tuple-element.240), channel_id=1, source_target_pairs={{0,16},{4,20},{8,24},{12,28},{16,0},{20,4},{24,8},{28,12},{1,17},{... | collective-permute-start | bytes 442376 | tf_op jit(solution)/shard_map/ppermute | solution.py:54
  (9 other events, 49.4 us)

commit v5 on v4

--- a/solution.py
+++ b/solution.py
@@ -24,17 +24,20 @@
     return lax.dot_general(a, b, dims, preferred_element_type=f32)
 
 
-def run(kernel, info, args, outs, scratch=(), after=(), limit=8, space=VMEM, to=VMEM):
+def run(kernel, info, args, outs, scratch=(), after=(), limit=8, space=VMEM, to=VMEM, far=()):
+    near = len(args)
+
     def body(*refs):
-        lead = 1 + len(args)
+        lead = 1 + near + len(far)
         rest = refs[lead + len(after) :]
         kernel(*refs[:lead], *rest[: len(outs)], *rest[len(outs) + 1 :])
         rest[len(outs)][...] = jnp.zeros((8, LANES), f32)
 
     args = [pltpu.with_memory_space_constraint(a, space.memory_space) for a in args]
+    args += [pltpu.with_memory_space_constraint(a, pltpu.HBM) for a in far]
     *results, mark = pl.pallas_call(
         body,
-        in_specs=[SMEM] + [space] * len(args) + [ANY] * len(after),
+        in_specs=[SMEM] + [space] * near + [HBM] * len(far) + [ANY] * len(after),
         out_specs=[to] * len(outs) + [VMEM],
         out_shape=[to.memory_space(shape, dtype) for shape, dtype in outs]
         + [pltpu.VMEM((8, LANES), f32)],
@@ -116,11 +119,37 @@
 def unfold(got, first, rows, target):
     half = rows // 2
     columns = target.shape[1]
-    target[:half, :] = got[first:, :columns]
-    target[half:, :] = got[first:, columns:]
-
-
-def second_split(info, vkept, okept, got, vkeep, okeep, send, flat, *, third, rows):
+    target[:half, :] = got[first : first + half, :columns]
+    target[half:, :] = got[first : first + half, columns:]
+
+
+def ride(taps, send):
+    rows, columns = taps.shape[0], send.shape[1]
+    value = taps[...].astype(bf16)
+    first = send.shape[0] - rows - rows // 2
+    send[first : first + rows, :] = value[:, :columns]
+    send[first + rows :, : columns // 2] = value[: rows // 2, columns:]
+    send[first + rows :, columns // 2 :] = value[rows // 2 :, columns:]
+
+
+def alight(taps, got, result):
+    rows, columns = taps.shape[0], got.shape[1]
+    first = got.shape[0] - rows - rows // 2
+    value = taps[...].astype(bf16).astype(f32)
+    half = rows // 2
+    result[:, :columns] = value[:, :columns] + got[first : first + rows, :].astype(f32)
+    result[:half, columns:] = value[:half, columns:] + got[
+        first + rows :, : columns // 2
+    ].astype(f32)
+    result[half:, columns:] = value[half:, columns:] + got[
+        first + rows :, columns // 2 :
+    ].astype(f32)
+
+
+def second_split(info, vkept, okept, got, *refs, third, rows):
+    *taps, vkeep, okeep, send, flat = refs
+    if taps:
+        ride(taps[0], send)
     total = vkept.shape[0]
     bit = (third + 1) % 3
     left = [b for b in range(3) if b != third]
@@ -132,7 +161,15 @@
     split_rows(info, bit, 0, total // 2, rows, put_into(okeep), fold, load)
 
 
-def third_split(info, vkept, okept, got, vkeep, okeep, send, flat, *, third, rows):
+def third_split(info, vkept, okept, got, *refs, third, rows):
+    if third == 1:
+        taps, vkeep, okeep, send, sums, flat = refs
+        alight(taps, got, sums)
+    elif third == 2:
+        sums, vkeep, okeep, send, flat = refs
+        ride(sums, send)
+    else:
+        vkeep, okeep, send, flat = refs
     total = vkept.shape[0]
     load = lambda at: add(vkept[at, :], got[at, :])
     split_rows(info, (third + 2) % 3, 0, total, rows, put_into(vkeep), put_into(send), load)
@@ -140,8 +177,13 @@
     okeep[...] = add(okept[...], flat[...])
 
 
-def last_split(info, vkept, okept, got, keep, send, *, rows):
+def last_split(info, vkept, okept, got, *refs, rows):
+    keep, send = refs[len(refs) // 4 :][:2]
     total, columns = vkept.shape
+    if len(refs) > 2:
+        alight(refs[0], got, refs[3])
+        keep[total // 2 :, :] = refs[3][...].astype(bf16)
+        send[total // 2 :, :] = refs[3][...].astype(bf16)
 
     def put(target):
         def to(at, value):
@@ -165,8 +207,9 @@
     return swap(value, *every_bit()[bit])
 
 
-def finish(keep, send, rows):
+def finish(keep, send, rows, riding):
     value = keep.astype(f32) + send_bit(send, 3).astype(f32)
+    value, behind = value[: value.shape[0] - riding], value[value.shape[0] - riding :]
     for bit in range(4, len(every_bit())):
         axis, place = every_bit()[bit]
         value = value.astype(bf16).reshape(-1, 2, rows, value.shape[1])
@@ -176,7 +219,7 @@
         )
         shape = (-1, value.shape[-1])
         value = keep.reshape(shape).astype(f32) + send_bit(send.reshape(shape), bit).astype(f32)
-    return value
+    return value, behind
 
 
 def sigmoid(v):
@@ -195,15 +238,15 @@
     )
 
 
-def prepare(info, *refs):
-    count = (len(refs) - 1) // 2
-    sem = refs[-1]
-    copies = [
-        pltpu.make_async_copy(refs[i], refs[count + i], sem.at[i]) for i in range(count)
-    ]
+def start_all(pairs, sem):
+    copies = [pltpu.make_async_copy(a, b, sem.at[i]) for i, (a, b) in enumerate(pairs)]
     for c in copies:
         c.start()
-    for c in copies:
+    return copies
+
+
+def prepare(info, ct, w_out, ct_to, w_to, sem):
+    for c in start_all([(w_out, w_to), (ct, ct_to)], sem):
         c.wait()
 
 
@@ -232,14 +275,17 @@
     halo[rows:, :] = after[...]
 
 
-def upstream(info, own, other, w_out, full, pull):
+def upstream(info, own, other, w_out, x, wv, wg, full, pull, x_to, wv_to, wg_to, sem):
     count, half = own.shape
+    copies = start_all([(x, x_to), (wv, wv_to), (wg, wg_to)], sem)
     mine, theirs = halves_at(info, half)
     full[:, pl.ds(mine, half)] = own[...]
     full[:, pl.ds(theirs, half)] = other[...]
     step = count // 2
     for c in range(0, count, step):
         pull[c : c + step, :] = dot(full[c : c + step, :], w_out[...], NT).astype(bf16)
+    for c in copies:
+        c.wait()
 
 
 def front(info, own, other, halo_own, halo_other, wv, wg, w_out, norm, rstd, hid, sig, slope, ends, edge):
@@ -455,7 +501,7 @@
 def taps_sums(info, dconv, hid, out, scratch, total, *, third):
     rows, channels = dconv.shape
     count = rows - 2 * NEAR
-    taps = out.shape[0]
+    taps = total.shape[0]
     half = (taps - 1) // 2
     groups = 16
     tiles = channels // LANES
@@ -486,7 +532,8 @@
             return 0
 
         lax.fori_loop(0, count // (8 * groups), body, 0)
-        out[:, local] = jnp.sum(total[...], axis=1)
+        out[:taps, local] = jnp.sum(total[...], axis=1)
+        out[taps:, local] = jnp.zeros((out.shape[0] - taps, LANES), f32)
         return 0
 
     lax.fori_loop(0, tiles, tile, 0)
@@ -603,25 +650,31 @@
         space=HBM,
     )
     before, after = lax.ppermute(last, "seq", up), lax.ppermute(first, "seq", down)
-    moved = [x, ct, w_value, w_gate, w_out]
-    xv, ctv, wv, wg, wo, mark = run(
+    ctv, wo, mark = run(
         prepare,
         info,
-        moved,
-        [(a.shape, bf16) for a in moved],
-        scratch=[pltpu.SemaphoreType.DMA((len(moved),))],
+        [ct, w_out],
+        [(ct.shape, bf16), (w_out.shape, bf16)],
+        scratch=[pltpu.SemaphoreType.DMA((2,))],
         after=[mark],
         space=HBM,
     )
-
-    rows, ext = count + 2 * NEAR, count + 2 * WIDE
-    full, pull, mark = run(
-        upstream, info, [ctv, ct_other, wo], [((count, width), bf16), ((count, channels), bf16)]
-    )
     halo, mark = run(
         pack, info, [before, after], [((2 * (WIDE + NEAR), channels), bf16)], after=[mark]
     )
     halo_other = swap(halo, "tensor")
+
+    rows, ext = count + 2 * NEAR, count + 2 * WIDE
+    full, pull, xv, wv, wg, mark = run(
+        upstream,
+        info,
+        [ctv, ct_other, wo],
+        [((count, width), bf16), ((count, channels), bf16)]
+        + [(a.shape, bf16) for a in (x, w_value, w_gate)],
+        scratch=[pltpu.SemaphoreType.DMA((3,))],
+        after=[mark],
+        far=[x, w_value, w_gate],
+    )
     norm, rstd, hid, sig, slope, ends, _ = run(
         front,
         info,
@@ -705,15 +758,17 @@
         kept.append((vkeep, okeep))
         got.append(send_bit(send, i))
 
-    def second(i, mark):
+    extra = (taps + 1) * 3 // 2
+
+    def second(i, mark, *riding):
         vkeep, okeep, send, mark = run(
             functools.partial(second_split, third=i, rows=block),
             info,
-            [*kept[i], got[i]],
+            [*kept[i], got[i], *riding],
             [
                 ((width // 4, 2 * third), bf16),
                 ((width // 8, third), bf16),
-                ((width // 4 + width // 16, 2 * third), bf16),
+                ((width // 4 + width // 16 + extra * len(riding), 2 * third), bf16),
             ],
             scratch=[pltpu.VMEM((width // 4, third), bf16)],
             after=[mark],
@@ -721,31 +776,35 @@
         kept[i], got[i] = (vkeep, okeep), send_bit(send, (i + 1) % 3)
         return mark
 
-    def third_step(i, mark):
-        vkeep, okeep, send, mark = run(
+    def third_step(i, mark, *riding):
+        off, on = (riding, ()) if i == 1 else ((), riding)
+        vkeep, okeep, send, *sums, mark = run(
             functools.partial(third_split, third=i, rows=block),
             info,
-            [*kept[i], got[i]],
+            [*kept[i], got[i], *riding],
             [
                 ((width // 8, 2 * third), bf16),
                 ((width // 8, third), bf16),
-                ((width // 8, 2 * third), bf16),
-            ],
+                ((width // 8 + extra * len(on), 2 * third), bf16),
+            ]
+            + [(r.shape, f32) for r in off],
             scratch=[pltpu.VMEM((width // 8, third), bf16)],
             after=[mark],
         )
         kept[i], got[i] = (vkeep, okeep), send_bit(send, (i + 2) % 3)
-        return mark
-
-    def last_step(i, mark):
+        return *sums, mark
+
+    def last_step(i, mark, *riding):
+        behind = (taps + 1) * len(riding)
         keep, send, mark = run(
             functools.partial(last_split, rows=block),
             info,
-            [*kept[i], got[i]],
-            [((width // 16, 3 * third), bf16)] * 2,
+            [*kept[i], got[i], *riding],
+            [((width // 16 + behind, 3 * third), bf16)] * 2,
+            scratch=[pltpu.VMEM(r.shape, f32) for r in riding],
             after=[mark],
         )
-        return finish(keep, send, block), mark
+        return *finish(keep, send, block, behind), mark
 
     def norm_part(own, mark):
         return run(
@@ -761,7 +820,7 @@
             functools.partial(taps_sums, third=i),
             info,
             [dconvs[i], hid],
-            [((taps, third), f32)],
+            [((taps + 1, third), f32)],
             scratch=[pltpu.VMEM((rows + 16, LANES), f32), pltpu.VMEM((taps, 8, LANES), f32)],
             after=[mark],
         )
@@ -777,22 +836,19 @@
             to=HBM,
         )
 
-    def taps_step(bit, value, mark):
-        return run(
-            add_taps, info, [value, send_bit(value, bit)], [(value.shape, f32)], after=[mark]
-        )
-
     parts = []
     for i in range(3):
         part, mark = taps_part(i, mark)
         parts.append(part)
-    kernel_grad = jnp.concatenate(parts, axis=1)
+    taps_own = jnp.concatenate(parts, axis=1)
+    *mine, mark = norm_part(True, mark)
+    mark = second(0, mark)
+    taps_sum, mark = run(
+        add_taps, info, [taps_own, send_bit(taps_own, 0)], [(taps_own.shape, f32)], after=[mark]
+    )
     *theirs, mark = norm_part(False, mark)
     theirs = [swap(t, "tensor") for t in theirs]
-    *mine, mark = norm_part(True, mark)
-    mark = second(0, mark)
-    kernel_grad, mark = taps_step(0, kernel_grad, mark)
-    mark = second(1, mark)
+    mark = second(1, mark, taps_sum)
     dnorm, stats3, mark = run(
         norm_sums,
         info,
@@ -801,22 +857,21 @@
         after=[mark],
     )
     stats3_other = swap(stats3, "tensor")
+    mark = second(2, mark)
     output, mark = final(output_rows, [x, out_mine, out_other], mark)
-    kernel_grad, mark = taps_step(1, kernel_grad, mark)
-    mark = second(2, mark)
     input_gradient, mark = final(
         input_rows, [ct, dnorm, norm, rstd, stats3, stats3_other], mark
     )
-    mark = third_step(0, mark)
-    kernel_grad, mark = taps_step(2, kernel_grad, mark)
-    for i in (1, 2):
-        mark = third_step(i, mark)
-    for bit in range(3, len(every)):
-        kernel_grad, mark = taps_step(bit, kernel_grad, mark)
-    totals = []
-    for i in range(3):
-        total, mark = last_step(i, mark)
-        totals.append(total)
+    (mark,) = third_step(0, mark)
+    taps_sum, mark = third_step(1, mark, taps_sum)
+    (mark,) = third_step(2, mark, taps_sum)
+    total0, _, mark = last_step(0, mark)
+    total1, _, mark = last_step(1, mark)
+    total2, kernel_grad, mark = last_step(2, mark, taps_sum)
+    totals = [total0, total1, total2]
+    for bit in range(4, len(every)):
+        kernel_grad = kernel_grad + send_bit(kernel_grad, bit)
+    kernel_grad = kernel_grad[:taps]
     value_grad, gate_grad = (
         jnp.concatenate([t[:, j * third : (j + 1) * third] for t in totals], axis=1)
         for j in (0, 1)

time: 151 us -> 140 us (0.927)
  waiting for transfers between devices: 37.6 us -> 29.4 us
  Pallas kernels: 80.1 us -> 76.6 us
    ppermute x28 -> x25, waiting for transfers between devices: 37.6 us -> 27 us  [swap(): return lax.ppermute(value, axis, [(i, i ^ 1 << bit) for i in range(size)])]
    pallas_call x37 -> x34, Pallas kernels: 80.1 us -> 76.6 us  [run(): pl.pallas_call(body, in_specs=[SMEM] + [space] * near + [HBM] * len(far)...]
    ppermute x1, waiting for transfers between devices: 0.01 us -> 2.39 us  [shards(): lax.ppermute(first, 'seq', down)]
    ppermute x28 -> x25, starting transfers between devices: 23.1 us -> 23.2 us  [swap(): return lax.ppermute(value, axis, [(i, i ^ 1 << bit) for i in range(size)])]
  transfers between devices with their start and end apart: 30 -> 27, of which waited for: 12 -> 11; matrix products, arithmetic and copies ran while one was open for 1% -> 0% of each run, Pallas kernels for 38% -> 40%
where the time goes in v5:
time: 140 us
  Pallas kernels  76.6 us (55%)
  starting transfers between devices  29.4 us (21%)
  waiting for transfers between devices  29.4 us (21%)
  other arithmetic  1.69 us (1%)
  between operations  1.69 us (1%)
    pallas_call x34, Pallas kernels, run(): pl.pallas_call(body, in_specs=[SMEM] + [space] * near + [HBM] * len(far)...  76.6 us
    ppermute x25, waiting for transfers between devices, swap(): return lax.ppermute(value, axis, [(i, i ^ 1 << bit) for i in range(size)])  27 us
    ppermute x25, starting transfers between devices, swap(): return lax.ppermute(value, axis, [(i, i ^ 1 << bit) for i in range(size)])  23.2 us
    ppermute x1, starting transfers between devices, shards(): lax.ppermute(last, 'seq', up)  4.85 us
  transfers between devices with their start and end apart: 27, of which 11 were waited for; matrix products, arithmetic and copies ran while one was open for 0% of the time, Pallas kernels for 40%

profile of v5, /device:TPU:0, one launch (start us, length us, event | category | flops | bytes accessed | tf_op | source)
XLA Modules:
  0.0 139.6 jit_solution(7519918448350717741)
XLA Ops:
  3.4 4.9 %collective-permute-start.1 = (bf16[48,768]{1,0:T(8,128)(2,1)S(1)}, bf16[48,768]{1,0:T(8,128)(2,1)S(1)}, u32[]{:S(2)}, u32[]{:S(2)}) collective-permute-start(bf16[48,768]{1,0:T(8,128)(2,1)S(1)} %get-tuple-element.123), channel_id=1, source_target_pairs={{0,4},{4,8},{8,12},{12,16},{16,20},{20,24},{24,28},{1,5},{5,9},{9,... | collective-permute-start | bytes 221192 | tf_op jit(solution)/shard_map/ppermute | solution.py:652
  9.6 2.5 %prepare.1 = (bf16[768,768]{1,0:T(8,128)(2,1)S(1)}, bf16[768,1536]{1,0:T(8,128)(2,1)S(1)}, f32[8,128]{1,0:T(8,128)S(1)}) custom-call(s32[8]{0:T(128)S(1)} %stack.27.refs_0_, bf16[768,768]{1,0:T(8,128)(2,1)} %bitcast.18, bf16[768,1536]{1,0:T(8,128)(2,1)} %refs_2_.2, f32[8,128]{1,0:T(8,128)S(1)} %get-tuple-element.120.refs_3_), custom_call_target="tpu_custom_call" | custom-call | flops 1024 | bytes 1024 | tf_op jit(solution)/shard_map/prepare/pallas_call | solution.py:38
  12.1 2.4 %collective-permute-done.2.refs_2_ = bf16[48,768]{1,0:T(8,128)(2,1)S(1)} collective-permute-done((bf16[48,768]{1,0:T(8,128)(2,1)S(1)}, bf16[48,768]{1,0:T(8,128)(2,1)S(1)}, u32[]{:S(2)}, u32[]{:S(2)}) %collective-permute-start.2) | collective-permute-done | bytes 73760 | tf_op jit(solution)/shard_map/ppermute | solution.py:652
  15.2 3.3 %upstream.1 = (bf16[768,1536]{1,0:T(8,128)(2,1)S(1)}, bf16[768,768]{1,0:T(8,128)(2,1)S(1)}, bf16[768,768]{1,0:T(8,128)(2,1)S(1)}, bf16[1536,768]{1,0:T(8,128)(2,...) custom-call(s32[8]{0:T(128)S(1)} %stack.27.refs_0_, bf16[768,768]{1,0:T(8,128)(2,1)S(1)} %get-tuple-element.121.refs_1_, ...), custom_call_target="tpu_custom_call" | custom-call | flops 1024 | bytes 1024 | tf_op jit(solution)/shard_map/upstream/pallas_call | solution.py:38
  18.5 7.8 %front.1 = (bf16[832,1536]{1,0:T(8,128)(2,1)S(1)}, f32[768,128]{1,0:T(8,128)S(1)}, bf16[832,768]{1,0:T(8,128)(2,1)S(1)}, bf16[768,768]{1,0:T(8,128)(2,1)S(1)}, b...) custom-call(s32[8]{0:T(128)S(1)} %stack.27.refs_0_, ...), custom_call_target="tpu_custom_call" | custom-call | flops 1024 | bytes 1024 | tf_op jit(solution)/shard_map/front/pallas_call | solution.py:38
  26.4 7.0 %depthwise.1 = (f32[800,768]{1,0:T(8,128)S(1)}, f32[800,128]{1,0:T(8,128)S(1)}, f32[8,128]{1,0:T(8,128)}) custom-call(s32[8]{0:T(128)S(1)} %stack.27.refs_0_, bf16[832,768]{1,0:T(8,128)(2,1)S(1)} %get-tuple-element.132.refs_1_.refs_2_, bf16[31,768]{1,0:T(8,128)(2,1)S(1)} %copy-done.2), custom_call_target="tpu_custom_call" | custom-call | flops 1024 | bytes 1024 | tf_op jit(solution)/shard_map/depthwise/pallas_call | solution.py:38
  35.3 5.2 %swish.1 = (bf16[768,768]{1,0:T(8,128)(2,1)S(1)}, f32[800,768]{1,0:T(8,128)S(1)}, f32[800,128]{1,0:T(8,128)S(1)}, f32[8,128]{1,0:T(8,128)}) custom-call(s32[8]{0:T(128)S(1)} %stack.27.refs_0_, f32[800,768]{1,0:T(8,128)S(1)} %get-tuple-element.133.refs_1_.refs_2_, bf16[768,768]{1,0:T(8,128)(2,1)S(1)} %get-tuple-element.134.refs_2_, ...), custom_call_target="tpu_custom_call" | custom-call | flops 1024 | bytes 1024 | tf_op jit(solution)/shard_map/swish/pallas_call | solution.py:38
  40.8 2.8 %out_terms.1 = (bf16[768,256]{1,0:T(8,128)(2,1)S(1)}, bf16[768,256]{1,0:T(8,128)(2,1)S(1)}, bf16[768,256]{1,0:T(8,128)(2,1)S(1)}, bf16[768,256]{1,0:T(8,128)(2,1...) custom-call(s32[8]{0:T(128)S(1)} %stack.27.refs_0_, ...), custom_call_target="tpu_custom_call" | custom-call | flops 1024 | bytes 1024 | tf_op jit(solution)/shard_map/out_terms/pallas_call | solution.py:38
  46.7 2.4 %collective-permute-start.10 = (bf16[768,256]{1,0:T(8,128)(2,1)S(1)}, bf16[768,256]{1,0:T(8,128)(2,1)S(1)}, u32[]{:S(2)}, u32[]{:S(2)}) collective-permute-start(bf16[768,256]{1,0:T(8,128)(2,1)S(1)} %get-tuple-element.154), channel_id=1, source_target_pairs={{0,4},{4,0},{8,12},{12,8},{16,20},{20,16},{24,28},{28,24},{1,5},{5... | collective-permute-start | bytes 1179656 | tf_op jit(solution)/shard_map/ppermute | solution.py:57
  49.1 4.8 %back.3 = (bf16[800,256]{1,0:T(8,128)(2,1)S(1)}, bf16[768,512]{1,0:T(8,128)(2,1)S(1)}, bf16[1536,512]{1,0:T(8,128)(2,1)S(1)}, f32[8,128]{1,0:T(8,128)S(1)}) custom-call(s32[8]{0:T(128)S(1)} %stack.27.refs_0_, f32[800,768]{1,0:T(8,128)S(1)} %get-tuple-element.138.refs_1_, f32[800,768]{1,0:T(8,128)S(1)} %get-tuple-element.133.refs_1_.refs_2_, ...), custom_call_target="tpu_custom_call" | custom-call | flops 1024 | bytes 1024 | tf_op jit(solution)/shard_map/back/pallas_call | solution.py:38
  59.4 5.0 %back.4 = (bf16[800,256]{1,0:T(8,128)(2,1)S(1)}, bf16[768,512]{1,0:T(8,128)(2,1)S(1)}, bf16[1536,512]{1,0:T(8,128)(2,1)S(1)}, f32[8,128]{1,0:T(8,128)S(1)}) custom-call(s32[8]{0:T(128)S(1)} %stack.27.refs_0_, f32[800,768]{1,0:T(8,128)S(1)} %get-tuple-element.138.refs_1_, f32[800,768]{1,0:T(8,128)S(1)} %get-tuple-element.133.refs_1_.refs_2_, ...), custom_call_target="tpu_custom_call" | custom-call | flops 1024 | bytes 1024 | tf_op jit(solution)/shard_map/back/pallas_call | solution.py:38
  66.9 4.8 %back.5 = (bf16[800,256]{1,0:T(8,128)(2,1)S(1)}, bf16[768,512]{1,0:T(8,128)(2,1)S(1)}, bf16[1536,512]{1,0:T(8,128)(2,1)S(1)}, f32[8,128]{1,0:T(8,128)S(1)}) custom-call(s32[8]{0:T(128)S(1)} %stack.27.refs_0_, f32[800,768]{1,0:T(8,128)S(1)} %get-tuple-element.138.refs_1_, f32[800,768]{1,0:T(8,128)S(1)} %get-tuple-element.133.refs_1_.refs_2_, ...), custom_call_target="tpu_custom_call" | custom-call | flops 1024 | bytes 1024 | tf_op jit(solution)/shard_map/back/pallas_call | solution.py:38
  72.9 2.5 %taps_sums.3 = (f32[32,256]{1,0:T(8,128)S(1)}, f32[8,128]{1,0:T(8,128)S(1)}) custom-call(s32[8]{0:T(128)S(1)} %stack.27.refs_0_, bf16[800,256]{1,0:T(8,128)(2,1)S(1)} %get-tuple-element.171.refs_1_, bf16[832,768]{1,0:T(8,128)(2,1)S(1)} %get-tuple-element.132.refs_1_.refs_2_, f32[8,128]{1,0:T(8,128)S(1)} %get-tuple-element.172.refs_3_), custom_call_target="tpu_custom_call" | custom-call | flops 1024 | bytes 1024 | tf_op jit(solution)/shard_map/taps_sums/pallas_call | solution.py:38
  75.5 2.5 %taps_sums.4 = (f32[32,256]{1,0:T(8,128)S(1)}, f32[8,128]{1,0:T(8,128)S(1)}) custom-call(s32[8]{0:T(128)S(1)} %stack.27.refs_0_, bf16[800,256]{1,0:T(8,128)(2,1)S(1)} %get-tuple-element.170.refs_1_, bf16[832,768]{1,0:T(8,128)(2,1)S(1)} %get-tuple-element.132.refs_1_.refs_2_, f32[8,128]{1,0:T(8,128)S(1)} %get-tuple-element.173.refs_3_), custom_call_target="tpu_custom_call" | custom-call | flops 1024 | bytes 1024 | tf_op jit(solution)/shard_map/taps_sums/pallas_call | solution.py:38
  78.0 2.5 %taps_sums.5 = (f32[32,256]{1,0:T(8,128)S(1)}, f32[8,128]{1,0:T(8,128)S(1)}) custom-call(s32[8]{0:T(128)S(1)} %stack.27.refs_0_, bf16[800,256]{1,0:T(8,128)(2,1)S(1)} %get-tuple-element.169.refs_1_, bf16[832,768]{1,0:T(8,128)(2,1)S(1)} %get-tuple-element.132.refs_1_.refs_2_, f32[8,128]{1,0:T(8,128)S(1)} %get-tuple-element.174.refs_3_), custom_call_target="tpu_custom_call" | custom-call | flops 1024 | bytes 1024 | tf_op jit(solution)/shard_map/taps_sums/pallas_call | solution.py:38
  82.1 2.6 %norm_half.2 = (f32[384,768]{1,0:T(8,128)S(1)}, f32[384,768]{1,0:T(8,128)S(1)}, f32[8,128]{1,0:T(8,128)S(1)}) custom-call(s32[8]{0:T(128)S(1)} %stack.27.refs_0_, bf16[768,512]{1,0:T(8,128)(2,1)S(1)} %get-tuple-element.166.refs_1_, bf16[768,512]{1,0:T(8,128)(2,1)S(1)} %get-tuple-element.167.refs_2_, bf16[768,512]{1,0:T(8,128)(2,1)S(1)} %get-tuple-element.168.refs_3_, ...), custom_call_target="tpu_custom_call" | custom-call | flops 1024 | bytes 1024 | tf_op jit(solution)/shard_map/norm_half/pallas_call | solution.py:38
  86.1 2.6 %norm_half.3 = (bf16[384,768]{1,0:T(8,128)(2,1)S(1)}, bf16[384,768]{1,0:T(8,128)(2,1)S(1)}, f32[8,128]{1,0:T(8,128)S(1)}) custom-call(s32[8]{0:T(128)S(1)} %stack.27.refs_0_, bf16[768,512]{1,0:T(8,128)(2,1)S(1)} %get-tuple-element.166.refs_1_, bf16[768,512]{1,0:T(8,128)(2,1)S(1)} %get-tuple-element.167.refs_2_, ...), custom_call_target="tpu_custom_call" | custom-call | flops 1024 | bytes 1024 | tf_op jit(solution)/shard_map/norm_half/pallas_call | solution.py:38
  94.4 2.6 %collective-permute-done.11.refs_3_ = bf16[960,512]{1,0:T(8,128)(2,1)S(1)} collective-permute-done((bf16[960,512]{1,0:T(8,128)(2,1)S(1)}, bf16[960,512]{1,0:T(8,128)(2,1)S(1)}, u32[]{:S(2)}, u32[]{:S(2)}) %collective-permute-start.11) | collective-permute-done | bytes 983072 | tf_op jit(solution)/shard_map/ppermute | solution.py:57
  101.1 2.2 %input_rows.1 = (bf16[768,768]{1,0:T(8,128)(2,1)}, f32[8,128]{1,0:T(8,128)S(1)}) custom-call(s32[8]{0:T(128)S(1)} %stack.27.refs_0_, bf16[768,768]{1,0:T(8,128)(2,1)S(1)} %bitcast.19, f32[768,768]{1,0:T(8,128)S(1)} %get-tuple-element.198.refs_2_, bf16[832,1536]{1,0:T(8,128)(2,1)S(1)} %get-tuple-element.142.refs_10_.refs_5_.refs_3_, ...), custom_call_target="tpu_custom_call" | custom-call | flops 1024 | bytes 1024 | tf_op jit(solution)/shard_map/input_rows/pallas_call | solution.py:38
  104.8 3.8 %collective-permute-done.21.refs_3_ = bf16[528,512]{1,0:T(8,128)(2,1)S(1)} collective-permute-done((bf16[528,512]{1,0:T(8,128)(2,1)S(1)}, bf16[528,512]{1,0:T(8,128)(2,1)S(1)}, u32[]{:S(2)}, u32[]{:S(2)}) %collective-permute-start.21) | collective-permute-done | bytes 540704 | tf_op jit(solution)/shard_map/ppermute | solution.py:57
  113.5 2.0 %collective-permute-start.22 = (bf16[96,768]{1,0:T(8,128)(2,1)S(1)}, bf16[96,768]{1,0:T(8,128)(2,1)S(1)}, u32[]{:S(2)}, u32[]{:S(2)}) collective-permute-start(bf16[96,768]{1,0:T(8,128)(2,1)S(1)} %get-tuple-element.221), channel_id=1, source_target_pairs={{0,16},{4,20},{8,24},{12,28},{16,0},{20,4},{24,8},{28,12},{1,17},{... | collective-permute-start | bytes 442376 | tf_op jit(solution)/shard_map/ppermute | solution.py:57
  121.8 8.2 %collective-permute-done.22 = bf16[96,768]{1,0:T(8,128)(2,1)S(1)} collective-permute-done((bf16[96,768]{1,0:T(8,128)(2,1)S(1)}, bf16[96,768]{1,0:T(8,128)(2,1)S(1)}, u32[]{:S(2)}, u32[]{:S(2)}) %collective-permute-start.22) | collective-permute-done | bytes 147488 | tf_op jit(solution)/shard_map/ppermute | solution.py:57
  130.1 3.1 %collective-permute-done.24 = bf16[96,768]{1,0:T(8,128)(2,1)S(1)} collective-permute-done((bf16[96,768]{1,0:T(8,128)(2,1)S(1)}, bf16[96,768]{1,0:T(8,128)(2,1)S(1)}, u32[]{:S(2)}, u32[]{:S(2)}) %collective-permute-start.24) | collective-permute-done | bytes 147488 | tf_op jit(solution)/shard_map/ppermute | solution.py:57
  133.2 4.0 %collective-permute-done.26 = bf16[128,768]{1,0:T(8,128)(2,1)S(1)} collective-permute-done((bf16[128,768]{1,0:T(8,128)(2,1)S(1)}, bf16[128,768]{1,0:T(8,128)(2,1)S(1)}, u32[]{:S(2)}, u32[]{:S(2)}) %collective-permute-start.26) | collective-permute-done | bytes 196640 | tf_op jit(solution)/shard_map/ppermute | solution.py:57
  (83 shorter events, 46.4 us)
Async XLA Ops:
  0.6 14.5 %collective-permute-start = (bf16[768,768]{1,0:T(8,128)(2,1)}, bf16[768,768]{1,0:T(8,128)(2,1)S(1)}, u32[]{:S(2)}, u32[]{:S(2)}) collective-permute-start(bf16[768,768]{1,0:T(8,128)(2,1)} %bitcast.16), channel_id=1, source_target_pairs={{0,2},{2,0},{1,3},{3,1},{4,6},{6,4},{5,7},{7,5},{8,10},{10,8},{9,1... | collective-permute-start | bytes 3538952 | tf_op jit(solution)/shard_map/ppermute | solution.py:57
  1.1 17.4 %collective-permute-start.3 = (bf16[768,768]{1,0:T(8,128)(2,1)}, bf16[768,768]{1,0:T(8,128)(2,1)S(1)}, u32[]{:S(2)}, u32[]{:S(2)}) collective-permute-start(bf16[768,768]{1,0:T(8,128)(2,1)} %bitcast.12), channel_id=1, source_target_pairs={{0,2},{2,0},{1,3},{3,1},{4,6},{6,4},{5,7},{7,5},{8,10},{10,8},{9,1... | collective-permute-start | bytes 3538952 | tf_op jit(solution)/shard_map/ppermute | solution.py:57
  3.4 8.7 %collective-permute-start.1 = (bf16[48,768]{1,0:T(8,128)(2,1)S(1)}, bf16[48,768]{1,0:T(8,128)(2,1)S(1)}, u32[]{:S(2)}, u32[]{:S(2)}) collective-permute-start(bf16[48,768]{1,0:T(8,128)(2,1)S(1)} %get-tuple-element.123), channel_id=1, source_target_pairs={{0,4},{4,8},{8,12},{12,16},{16,20},{20,24},{24,28},{1,5},{5,9},{9,... | collective-permute-start | bytes 221192 | tf_op jit(solution)/shard_map/ppermute | solution.py:652
  8.3 6.2 %collective-permute-start.2 = (bf16[48,768]{1,0:T(8,128)(2,1)S(1)}, bf16[48,768]{1,0:T(8,128)(2,1)S(1)}, u32[]{:S(2)}, u32[]{:S(2)}) collective-permute-start(bf16[48,768]{1,0:T(8,128)(2,1)S(1)} %get-tuple-element.124), channel_id=1, source_target_pairs={{4,0},{8,4},{12,8},{16,12},{20,16},{24,20},{28,24},{5,1},{9,5},{13... | collective-permute-start | bytes 221192 | tf_op jit(solution)/shard_map/ppermute | solution.py:652
  40.5 8.7 %collective-permute-start.6 = (f32[800,128]{1,0:T(8,128)S(1)}, f32[800,128]{1,0:T(8,128)S(1)}, u32[]{:S(2)}, u32[]{:S(2)}) collective-permute-start(f32[800,128]{1,0:T(8,128)S(1)} %get-tuple-element.139.refs_5_), channel_id=1, source_target_pairs={{0,2},{2,0},{1,3},{3,1},{4,6},{6,4},{5,7},{7,5},{8,10},{10,8},{9,1... | collective-permute-start | bytes 1228808 | tf_op jit(solution)/shard_map/ppermute | solution.py:57
  43.6 13.6 %collective-permute-start.8 = (bf16[768,256]{1,0:T(8,128)(2,1)S(1)}, bf16[768,256]{1,0:T(8,128)(2,1)S(1)}, u32[]{:S(2)}, u32[]{:S(2)}) collective-permute-start(bf16[768,256]{1,0:T(8,128)(2,1)S(1)} %get-tuple-element.151), channel_id=1, source_target_pairs={{0,8},{4,12},{8,0},{12,4},{16,24},{20,28},{24,16},{28,20},{1,9},{5... | collective-permute-start | bytes 1179656 | tf_op jit(solution)/shard_map/ppermute | solution.py:57
  45.2 12.0 %collective-permute-start.9 = (bf16[768,256]{1,0:T(8,128)(2,1)S(1)}, bf16[768,256]{1,0:T(8,128)(2,1)S(1)}, u32[]{:S(2)}, u32[]{:S(2)}) collective-permute-start(bf16[768,256]{1,0:T(8,128)(2,1)S(1)} %get-tuple-element.153), channel_id=1, source_target_pairs={{0,1},{1,0},{2,3},{3,2},{4,5},{5,4},{6,7},{7,6},{8,9},{9,8},{10,11... | collective-permute-start | bytes 1179656 | tf_op jit(solution)/shard_map/ppermute | solution.py:57
  46.7 11.3 %collective-permute-start.10 = (bf16[768,256]{1,0:T(8,128)(2,1)S(1)}, bf16[768,256]{1,0:T(8,128)(2,1)S(1)}, u32[]{:S(2)}, u32[]{:S(2)}) collective-permute-start(bf16[768,256]{1,0:T(8,128)(2,1)S(1)} %get-tuple-element.154), channel_id=1, source_target_pairs={{0,4},{4,0},{8,12},{12,8},{16,20},{20,16},{24,28},{28,24},{1,5},{5... | collective-permute-start | bytes 1179656 | tf_op jit(solution)/shard_map/ppermute | solution.py:57
  58.7 25.9 %collective-permute-start.13 = (bf16[960,512]{1,0:T(8,128)(2,1)S(1)}, bf16[960,512]{1,0:T(8,128)(2,1)S(1)}, u32[]{:S(2)}, u32[]{:S(2)}) collective-permute-start(bf16[960,512]{1,0:T(8,128)(2,1)S(1)} %get-tuple-element.183), channel_id=1, source_target_pairs={{0,1},{1,0},{2,3},{3,2},{4,5},{5,4},{6,7},{7,6},{8,9},{9,8},{10,11... | collective-permute-start | bytes 2949128 | tf_op jit(solution)/shard_map/ppermute | solution.py:57
  65.1 24.2 %collective-permute-start.16 = (bf16[960,512]{1,0:T(8,128)(2,1)S(1)}, bf16[960,512]{1,0:T(8,128)(2,1)S(1)}, u32[]{:S(2)}, u32[]{:S(2)}) collective-permute-start(bf16[960,512]{1,0:T(8,128)(2,1)S(1)} %get-tuple-element.191), channel_id=1, source_target_pairs={{0,4},{4,0},{8,12},{12,8},{16,20},{20,16},{24,28},{28,24},{1,5},{5... | collective-permute-start | bytes 2949128 | tf_op jit(solution)/shard_map/ppermute | solution.py:57
  66.9 32.5 %collective-permute-start.7 = (bf16[768,768]{1,0:T(8,128)(2,1)S(1)}, bf16[768,768]{1,0:T(8,128)(2,1)S(1)}, u32[]{:S(2)}, u32[]{:S(2)}) collective-permute-start(bf16[768,768]{1,0:T(8,128)(2,1)S(1)} %get-tuple-element.148), channel_id=1, source_target_pairs={{0,2},{2,0},{1,3},{3,1},{4,6},{6,4},{5,7},{7,5},{8,10},{10,8},{9,1... | collective-permute-start | bytes 3538952 | tf_op jit(solution)/shard_map/ppermute | solution.py:57
  72.4 24.6 %collective-permute-start.11 = (bf16[960,512]{1,0:T(8,128)(2,1)S(1)}, bf16[960,512]{1,0:T(8,128)(2,1)S(1)}, u32[]{:S(2)}, u32[]{:S(2)}) collective-permute-start(bf16[960,512]{1,0:T(8,128)(2,1)S(1)} %get-tuple-element.165), channel_id=1, source_target_pairs={{0,8},{4,12},{8,0},{12,4},{16,24},{20,28},{24,16},{28,20},{1,9},{5... | collective-permute-start | bytes 2949128 | tf_op jit(solution)/shard_map/ppermute | solution.py:57
  80.5 5.0 %collective-permute-start.12 = (f32[32,768]{1,0:T(8,128)S(1)}, f32[32,768]{1,0:T(8,128)S(1)}, u32[]{:S(2)}, u32[]{:S(2)}) collective-permute-start(f32[32,768]{1,0:T(8,128)S(1)} %constant_dynamic-update-slice_fusion.refs_1_), channel_id=1, source_target_pairs={{0,1},{1,0},{2,3},{3,2},{4,5},{5,4},{6,7},{7,6},{8,9},{9,8},{10,11... | collective-permute-start | bytes 294920 | tf_op jit(solution)/shard_map/ppermute | solution.py:57
  88.8 3.6 %collective-permute-start.15 = (bf16[384,768]{1,0:T(8,128)(2,1)S(1)}, bf16[384,768]{1,0:T(8,128)(2,1)S(1)}, u32[]{:S(2)}, u32[]{:S(2)}) collective-permute-start(bf16[384,768]{1,0:T(8,128)(2,1)S(1)} %get-tuple-element.188), channel_id=1, source_target_pairs={{0,2},{2,0},{1,3},{3,1},{4,6},{6,4},{5,7},{7,5},{8,10},{10,8},{9,1... | collective-permute-start | bytes 1769480 | tf_op jit(solution)/shard_map/ppermute | solution.py:57
  89.3 14.1 %collective-permute-start.18 = (bf16[480,512]{1,0:T(8,128)(2,1)S(1)}, bf16[480,512]{1,0:T(8,128)(2,1)S(1)}, u32[]{:S(2)}, u32[]{:S(2)}) collective-permute-start(bf16[480,512]{1,0:T(8,128)(2,1)S(1)} %get-tuple-element.205), channel_id=1, source_target_pairs={{0,4},{4,0},{8,12},{12,8},{16,20},{20,16},{24,28},{28,24},{1,5},{5... | collective-permute-start | bytes 1474568 | tf_op jit(solution)/shard_map/ppermute | solution.py:57
  90.7 17.9 %collective-permute-start.21 = (bf16[528,512]{1,0:T(8,128)(2,1)S(1)}, bf16[528,512]{1,0:T(8,128)(2,1)S(1)}, u32[]{:S(2)}, u32[]{:S(2)}) collective-permute-start(bf16[528,512]{1,0:T(8,128)(2,1)S(1)} %get-tuple-element.215), channel_id=1, source_target_pairs={{0,8},{4,12},{8,0},{12,4},{16,24},{20,28},{24,16},{28,20},{1,9},{5... | collective-permute-start | bytes 1622024 | tf_op jit(solution)/shard_map/ppermute | solution.py:57
  94.3 6.8 %collective-permute-start.17 = (f32[768,128]{1,0:T(8,128)S(1)}, f32[768,128]{1,0:T(8,128)S(1)}, u32[]{:S(2)}, u32[]{:S(2)}) collective-permute-start(f32[768,128]{1,0:T(8,128)S(1)} %get-tuple-element.200.refs_5_), channel_id=1, source_target_pairs={{0,2},{2,0},{1,3},{3,1},{4,6},{6,4},{5,7},{7,5},{8,10},{10,8},{9,1... | collective-permute-start | bytes 1179656 | tf_op jit(solution)/shard_map/ppermute | solution.py:57
  97.8 12.5 %collective-permute-start.20 = (bf16[480,512]{1,0:T(8,128)(2,1)S(1)}, bf16[480,512]{1,0:T(8,128)(2,1)S(1)}, u32[]{:S(2)}, u32[]{:S(2)}) collective-permute-start(bf16[480,512]{1,0:T(8,128)(2,1)S(1)} %get-tuple-element.212), channel_id=1, source_target_pairs={{0,1},{1,0},{2,3},{3,2},{4,5},{5,4},{6,7},{7,6},{8,9},{9,8},{10,11... | collective-permute-start | bytes 1474568 | tf_op jit(solution)/shard_map/ppermute | solution.py:57
  104.0 8.9 %collective-permute-start.19 = (bf16[192,512]{1,0:T(8,128)(2,1)S(1)}, bf16[192,512]{1,0:T(8,128)(2,1)S(1)}, u32[]{:S(2)}, u32[]{:S(2)}) collective-permute-start(bf16[192,512]{1,0:T(8,128)(2,1)S(1)} %get-tuple-element.209), channel_id=1, source_target_pairs={{0,8},{4,12},{8,0},{12,4},{16,24},{20,28},{24,16},{28,20},{1,9},{5... | collective-permute-start | bytes 589832 | tf_op jit(solution)/shard_map/ppermute | solution.py:57
  111.1 8.6 %collective-permute-start.25 = (bf16[240,512]{1,0:T(8,128)(2,1)S(1)}, bf16[240,512]{1,0:T(8,128)(2,1)S(1)}, u32[]{:S(2)}, u32[]{:S(2)}) collective-permute-start(bf16[240,512]{1,0:T(8,128)(2,1)S(1)} %get-tuple-element.230), channel_id=1, source_target_pairs={{0,4},{4,0},{8,12},{12,8},{16,20},{20,16},{24,28},{28,24},{1,5},{5... | collective-permute-start | bytes 737288 | tf_op jit(solution)/shard_map/ppermute | solution.py:57
  111.4 5.7 %collective-permute-start.23 = (bf16[192,512]{1,0:T(8,128)(2,1)S(1)}, bf16[192,512]{1,0:T(8,128)(2,1)S(1)}, u32[]{:S(2)}, u32[]{:S(2)}) collective-permute-start(bf16[192,512]{1,0:T(8,128)(2,1)S(1)} %get-tuple-element.224), channel_id=1, source_target_pairs={{0,1},{1,0},{2,3},{3,2},{4,5},{5,4},{6,7},{7,6},{8,9},{9,8},{10,11... | collective-permute-start | bytes 589832 | tf_op jit(solution)/shard_map/ppermute | solution.py:57
  113.5 16.5 %collective-permute-start.22 = (bf16[96,768]{1,0:T(8,128)(2,1)S(1)}, bf16[96,768]{1,0:T(8,128)(2,1)S(1)}, u32[]{:S(2)}, u32[]{:S(2)}) collective-permute-start(bf16[96,768]{1,0:T(8,128)(2,1)S(1)} %get-tuple-element.221), channel_id=1, source_target_pairs={{0,16},{4,20},{8,24},{12,28},{16,0},{20,4},{24,8},{28,12},{1,17},{... | collective-permute-start | bytes 442376 | tf_op jit(solution)/shard_map/ppermute | solution.py:57
  117.7 15.5 %collective-permute-start.24 = (bf16[96,768]{1,0:T(8,128)(2,1)S(1)}, bf16[96,768]{1,0:T(8,128)(2,1)S(1)}, u32[]{:S(2)}, u32[]{:S(2)}) collective-permute-start(bf16[96,768]{1,0:T(8,128)(2,1)S(1)} %get-tuple-element.227), channel_id=1, source_target_pairs={{0,16},{4,20},{8,24},{12,28},{16,0},{20,4},{24,8},{28,12},{1,17},{... | collective-permute-start | bytes 442376 | tf_op jit(solution)/shard_map/ppermute | solution.py:57
  120.8 16.5 %collective-permute-start.26 = (bf16[128,768]{1,0:T(8,128)(2,1)S(1)}, bf16[128,768]{1,0:T(8,128)(2,1)S(1)}, u32[]{:S(2)}, u32[]{:S(2)}) collective-permute-start(bf16[128,768]{1,0:T(8,128)(2,1)S(1)} %get-tuple-element.233), channel_id=1, source_target_pairs={{0,16},{4,20},{8,24},{12,28},{16,0},{20,4},{24,8},{28,12},{1,17},{... | collective-permute-start | bytes 589832 | tf_op jit(solution)/shard_map/ppermute | solution.py:57
  (6 other events, 22.0 us)

commit v6 on v5

--- a/solution.py
+++ b/solution.py
@@ -171,10 +171,24 @@
     else:
         vkeep, okeep, send, flat = refs
     total = vkept.shape[0]
+    bit, place = ((third + 2) % 3, 0) if third else (3, 1)
     load = lambda at: add(vkept[at, :], got[at, :])
-    split_rows(info, (third + 2) % 3, 0, total, rows, put_into(vkeep), put_into(send), load)
+    split_rows(info, bit, place, total, rows, put_into(vkeep), put_into(send), load)
     unfold(got, total, total // 2, flat)
-    okeep[...] = add(okept[...], flat[...])
+    if third:
+        okeep[...] = add(okept[...], flat[...])
+    else:
+        fold = put_folded(send, total // 2, total // 8)
+        load = lambda at: add(okept[at, :], flat[at, :])
+        split_rows(info, bit, 0, total // 2, rows, put_into(okeep), fold, load)
+
+
+def first_last_split(info, vkept, okept, got, keep, send, osum, flat, *, rows):
+    total = vkept.shape[0]
+    load = lambda at: add(vkept[at, :], got[at, :])
+    split_rows(info, 2, 0, total, rows, put_into(keep), put_into(send), load)
+    unfold(got, total, total // 2, flat)
+    osum[...] = okept[...].astype(f32) + flat[...].astype(f32)
 
 
 def last_split(info, vkept, okept, got, *refs, rows):
@@ -207,9 +221,7 @@
     return swap(value, *every_bit()[bit])
 
 
-def finish(keep, send, rows, riding):
-    value = keep.astype(f32) + send_bit(send, 3).astype(f32)
-    value, behind = value[: value.shape[0] - riding], value[value.shape[0] - riding :]
+def finish(value, rows):
     for bit in range(4, len(every_bit())):
         axis, place = every_bit()[bit]
         value = value.astype(bf16).reshape(-1, 2, rows, value.shape[1])
@@ -219,7 +231,7 @@
         )
         shape = (-1, value.shape[-1])
         value = keep.reshape(shape).astype(f32) + send_bit(send.reshape(shape), bit).astype(f32)
-    return value, behind
+    return value
 
 
 def sigmoid(v):
@@ -304,7 +316,7 @@
         norm[to, pl.ds(theirs, half)] = (b * inverse).astype(bf16)
         return inverse
 
-    chunk = 64
+    chunk = 128
 
     def body(i, _):
         at = pl.multiple_of(i * chunk, chunk)
@@ -428,7 +440,7 @@
 
     part(0, ends[:NEAR, :], NEAR)
     part(NEAR + count, ends[NEAR:, :], NEAR)
-    step = 32
+    step = 64
 
     def body(i, _):
         at = pl.multiple_of(i * step, step)
@@ -453,10 +465,8 @@
         split_rows(info, i, i, width, rows, keep, send, load)
 
 
-def back(info, dswish, conv, own, other, own2, other2, taps, sig, slope, norm, dconv, dvg, product, scratch, coef, *, third):
-    rows, channels = dswish.shape
-    count = sig.shape[0]
-    width = 2 * channels
+def slopes(info, own, other, own2, other2, coef, width):
+    rows = own.shape[0]
     mean, inverse = moments(own[...], other[...], width)
     half = LANES // 2
     shift = (own2[:, :1] + other2[:, :1]) / width
@@ -466,6 +476,17 @@
     coef[0] = jnp.broadcast_to(inverse, (rows, LANES))
     coef[1] = jnp.broadcast_to(tilt, (rows, LANES))
     coef[2] = jnp.broadcast_to(tilt * mean - inverse * shift, (rows, LANES))
+
+
+def back(info, dswish, conv, taps, sig, slope, norm, *refs, third):
+    rows, channels = dswish.shape
+    count = sig.shape[0]
+    width = 2 * channels
+    if third == 0:
+        *sums, dconv, dvg, product, coef, scratch = refs
+        slopes(info, *sums, coef, width)
+    else:
+        coef, dconv, dvg, product, scratch = refs
     tiles = channels // LANES // 3
     groups = 16
     skip = NEAR - (taps.shape[0] - 1) // 2
@@ -728,15 +749,19 @@
         )
 
     dconvs, dvgs, kept, got = [], [], [], []
+    sums = [stats, stats_other, stats2, stats2_other]
     for i in range(3):
-        dconv, dvg, product, mark = run(
+        dconv, dvg, product, *coef, mark = run(
             functools.partial(back, third=i),
             info,
-            [dswish, conv, stats, stats_other, stats2, stats2_other, kernel, sig, slope, norm],
-            [((rows, third), bf16), ((count, 2 * third), bf16), ((width, 2 * third), bf16)],
-            scratch=[pltpu.VMEM((rows + 16, LANES), f32), pltpu.VMEM((3, rows, LANES), f32)],
+            [dswish, conv, kernel, sig, slope, norm, *sums],
+            [((rows, third), bf16), ((count, 2 * third), bf16), ((width, 2 * third), bf16)]
+            + [((3, rows, LANES), f32)] * (i == 0),
+            scratch=[pltpu.VMEM((rows + 16, LANES), f32)],
             after=[mark],
         )
+        if i == 0:
+            sums = coef
         if i == 0:
             out_theirs, mark = out_part(False, mark)
             out_other = swap(out_theirs, "tensor")
@@ -784,18 +809,28 @@
             [*kept[i], got[i], *riding],
             [
                 ((width // 8, 2 * third), bf16),
-                ((width // 8, third), bf16),
-                ((width // 8 + extra * len(on), 2 * third), bf16),
+                ((width // 8 if i else width // 16, third), bf16),
+                ((width // 8 + (extra * len(on) if i else width // 32), 2 * third), bf16),
             ]
             + [(r.shape, f32) for r in off],
             scratch=[pltpu.VMEM((width // 8, third), bf16)],
             after=[mark],
         )
-        kept[i], got[i] = (vkeep, okeep), send_bit(send, (i + 2) % 3)
+        kept[i], got[i] = (vkeep, okeep), send_bit(send, (i + 2) % 3 if i else 3)
         return *sums, mark
 
     def last_step(i, mark, *riding):
         behind = (taps + 1) * len(riding)
+        if i == 0:
+            keep, send, osum, mark = run(
+                functools.partial(first_last_split, rows=block),
+                info,
+                [*kept[0], got[0]],
+                [((width // 16, 2 * third), bf16)] * 2 + [((width // 16, third), f32)],
+                scratch=[pltpu.VMEM((width // 16, third), bf16)],
+                after=[mark],
+            )
+            return keep.astype(f32) + send_bit(send, 2).astype(f32), osum, mark
         keep, send, mark = run(
             functools.partial(last_split, rows=block),
             info,
@@ -804,7 +839,8 @@
             scratch=[pltpu.VMEM(r.shape, f32) for r in riding],
             after=[mark],
         )
-        return *finish(keep, send, block, behind), mark
+        value = keep.astype(f32) + send_bit(send, 3).astype(f32)
+        return value[: width // 16], value[width // 16 :], mark
 
     def norm_part(own, mark):
         return run(
@@ -865,18 +901,20 @@
     (mark,) = third_step(0, mark)
     taps_sum, mark = third_step(1, mark, taps_sum)
     (mark,) = third_step(2, mark, taps_sum)
-    total0, _, mark = last_step(0, mark)
+    total0, out2, mark = last_step(0, mark)
     total1, _, mark = last_step(1, mark)
     total2, kernel_grad, mark = last_step(2, mark, taps_sum)
-    totals = [total0, total1, total2]
+    totals = [finish(t, block) for t in (total0, total1, total2)]
+    value_grad, gate_grad = (
+        jnp.concatenate([t[:, j * third : (j + 1) * third] for t in totals], axis=1)
+        for j in (0, 1)
+    )
+    out_grad = jnp.concatenate(
+        [totals[1][:, 2 * third :], totals[2][:, 2 * third :], finish(out2, block)], axis=1
+    ).T
     for bit in range(4, len(every)):
         kernel_grad = kernel_grad + send_bit(kernel_grad, bit)
     kernel_grad = kernel_grad[:taps]
-    value_grad, gate_grad = (
-        jnp.concatenate([t[:, j * third : (j + 1) * third] for t in totals], axis=1)
-        for j in (0, 1)
-    )
-    out_grad = jnp.concatenate([totals[(i + 1) % 3][:, 2 * third :] for i in range(3)], axis=1).T
     return (
         output[None],
         input_gradient[None],

time: 140 us -> 136 us (0.971)
  Pallas kernels: 76.6 us -> 73.6 us
    pallas_call x34, Pallas kernels: 76.6 us -> 73.6 us  [run(): pl.pallas_call(body, in_specs=[SMEM] + [space] * near + [HBM] * len(far)...]
  transfers between devices with their start and end apart: 27 -> 27, of which waited for: 11 -> 9; matrix products, arithmetic and copies ran while one was open for 0% -> 0% of each run, Pallas kernels for 40% -> 40%
where the time goes in v6:
time: 136 us
  Pallas kernels  73.6 us (54%)
  starting transfers between devices  30 us (22%)
  waiting for transfers between devices  28 us (21%)
  between operations  1.71 us (1%)
  other arithmetic  1.7 us (1%)
    pallas_call x34, Pallas kernels, run(): pl.pallas_call(body, in_specs=[SMEM] + [space] * near + [HBM] * len(far)...  73.6 us
    ppermute x25, waiting for transfers between devices, swap(): return lax.ppermute(value, axis, [(i, i ^ 1 << bit) for i in range(size)])  25.6 us
    ppermute x25, starting transfers between devices, swap(): return lax.ppermute(value, axis, [(i, i ^ 1 << bit) for i in range(size)])  23.9 us
    ppermute x1, starting transfers between devices, shards(): lax.ppermute(last, 'seq', up)  4.85 us
  transfers between devices with their start and end apart: 27, of which 9 were waited for; matrix products, arithmetic and copies ran while one was open for 0% of the time, Pallas kernels for 40%

profile of v6, /device:TPU:0, one launch (start us, length us, event | category | flops | bytes accessed | tf_op | source)
XLA Modules:
  0.0 135.8 jit_solution(9815968671492066983)
XLA Ops:
  3.4 4.9 %collective-permute-start.1 = (bf16[48,768]{1,0:T(8,128)(2,1)S(1)}, bf16[48,768]{1,0:T(8,128)(2,1)S(1)}, u32[]{:S(2)}, u32[]{:S(2)}) collective-permute-start(bf16[48,768]{1,0:T(8,128)(2,1)S(1)} %get-tuple-element.125), channel_id=1, source_target_pairs={{0,4},{4,8},{8,12},{12,16},{16,20},{20,24},{24,28},{1,5},{5,9},{9,... | collective-permute-start | bytes 221192 | tf_op jit(solution)/shard_map/ppermute | solution.py:673
  9.6 2.5 %prepare.1 = (bf16[768,768]{1,0:T(8,128)(2,1)S(1)}, bf16[768,1536]{1,0:T(8,128)(2,1)S(1)}, f32[8,128]{1,0:T(8,128)S(1)}) custom-call(s32[8]{0:T(128)S(1)} %stack.27.refs_0_, bf16[768,768]{1,0:T(8,128)(2,1)} %bitcast.18, bf16[768,1536]{1,0:T(8,128)(2,1)} %refs_2_.2, f32[8,128]{1,0:T(8,128)S(1)} %get-tuple-element.122.refs_3_), custom_call_target="tpu_custom_call" | custom-call | flops 1024 | bytes 1024 | tf_op jit(solution)/shard_map/prepare/pallas_call | solution.py:38
  12.1 2.4 %collective-permute-done.2.refs_2_ = bf16[48,768]{1,0:T(8,128)(2,1)S(1)} collective-permute-done((bf16[48,768]{1,0:T(8,128)(2,1)S(1)}, bf16[48,768]{1,0:T(8,128)(2,1)S(1)}, u32[]{:S(2)}, u32[]{:S(2)}) %collective-permute-start.2) | collective-permute-done | bytes 73760 | tf_op jit(solution)/shard_map/ppermute | solution.py:673
  15.2 3.4 %upstream.1 = (bf16[768,1536]{1,0:T(8,128)(2,1)S(1)}, bf16[768,768]{1,0:T(8,128)(2,1)S(1)}, bf16[768,768]{1,0:T(8,128)(2,1)S(1)}, bf16[1536,768]{1,0:T(8,128)(2,...) custom-call(s32[8]{0:T(128)S(1)} %stack.27.refs_0_, bf16[768,768]{1,0:T(8,128)(2,1)S(1)} %get-tuple-element.123.refs_1_, ...), custom_call_target="tpu_custom_call" | custom-call | flops 1024 | bytes 1024 | tf_op jit(solution)/shard_map/upstream/pallas_call | solution.py:38
  18.5 7.4 %front.1 = (bf16[832,1536]{1,0:T(8,128)(2,1)S(1)}, f32[768,128]{1,0:T(8,128)S(1)}, bf16[832,768]{1,0:T(8,128)(2,1)S(1)}, bf16[768,768]{1,0:T(8,128)(2,1)S(1)}, b...) custom-call(s32[8]{0:T(128)S(1)} %stack.27.refs_0_, ...), custom_call_target="tpu_custom_call" | custom-call | flops 1024 | bytes 1024 | tf_op jit(solution)/shard_map/front/pallas_call | solution.py:38
  26.0 7.1 %depthwise.1 = (f32[800,768]{1,0:T(8,128)S(1)}, f32[800,128]{1,0:T(8,128)S(1)}, f32[8,128]{1,0:T(8,128)}) custom-call(s32[8]{0:T(128)S(1)} %stack.27.refs_0_, bf16[832,768]{1,0:T(8,128)(2,1)S(1)} %get-tuple-element.134.refs_1_.refs_2_, bf16[31,768]{1,0:T(8,128)(2,1)S(1)} %copy-done.2), custom_call_target="tpu_custom_call" | custom-call | flops 1024 | bytes 1024 | tf_op jit(solution)/shard_map/depthwise/pallas_call | solution.py:38
  34.9 3.9 %swish.1 = (bf16[768,768]{1,0:T(8,128)(2,1)S(1)}, f32[800,768]{1,0:T(8,128)S(1)}, f32[800,128]{1,0:T(8,128)S(1)}, f32[8,128]{1,0:T(8,128)}) custom-call(s32[8]{0:T(128)S(1)} %stack.27.refs_0_, f32[800,768]{1,0:T(8,128)S(1)} %get-tuple-element.135.refs_1_.refs_2_, bf16[768,768]{1,0:T(8,128)(2,1)S(1)} %get-tuple-element.136.refs_2_, ...), custom_call_target="tpu_custom_call" | custom-call | flops 1024 | bytes 1024 | tf_op jit(solution)/shard_map/swish/pallas_call | solution.py:38
  39.1 2.7 %out_terms.1 = (bf16[768,256]{1,0:T(8,128)(2,1)S(1)}, bf16[768,256]{1,0:T(8,128)(2,1)S(1)}, bf16[768,256]{1,0:T(8,128)(2,1)S(1)}, bf16[768,256]{1,0:T(8,128)(2,1...) custom-call(s32[8]{0:T(128)S(1)} %stack.27.refs_0_, ...), custom_call_target="tpu_custom_call" | custom-call | flops 1024 | bytes 1024 | tf_op jit(solution)/shard_map/out_terms/pallas_call | solution.py:38
  45.0 2.4 %collective-permute-start.10 = (bf16[768,256]{1,0:T(8,128)(2,1)S(1)}, bf16[768,256]{1,0:T(8,128)(2,1)S(1)}, u32[]{:S(2)}, u32[]{:S(2)}) collective-permute-start(bf16[768,256]{1,0:T(8,128)(2,1)S(1)} %get-tuple-element.157), channel_id=1, source_target_pairs={{0,4},{4,0},{8,12},{12,8},{16,20},{20,16},{24,28},{28,24},{1,5},{5... | collective-permute-start | bytes 1179656 | tf_op jit(solution)/shard_map/ppermute | solution.py:57
  47.4 4.8 %back.3 = (bf16[800,256]{1,0:T(8,128)(2,1)S(1)}, bf16[768,512]{1,0:T(8,128)(2,1)S(1)}, bf16[1536,512]{1,0:T(8,128)(2,1)S(1)}, f32[3,800,128]{2,1,0:T(8,128)S(1)}, f32[8,128]{1,0:T(8,128)S(1)}) custom-call(s32[8]{0:T(128)S(1)} %stack.27.refs_0_, f32[800,768]{1,0:T(8,128)S(1)} %get-tuple-element.140.refs_1_, ...), custom_call_target="tpu_custom_call" | custom-call | flops 1024 | bytes 1024 | tf_op jit(solution)/shard_map/back/pallas_call | solution.py:38
  57.6 4.2 %back.4 = (bf16[800,256]{1,0:T(8,128)(2,1)S(1)}, bf16[768,512]{1,0:T(8,128)(2,1)S(1)}, bf16[1536,512]{1,0:T(8,128)(2,1)S(1)}, f32[8,128]{1,0:T(8,128)S(1)}) custom-call(s32[8]{0:T(128)S(1)} %stack.27.refs_0_, f32[800,768]{1,0:T(8,128)S(1)} %get-tuple-element.140.refs_1_, f32[800,768]{1,0:T(8,128)S(1)} %get-tuple-element.135.refs_1_.refs_2_, ...), custom_call_target="tpu_custom_call" | custom-call | flops 1024 | bytes 1024 | tf_op jit(solution)/shard_map/back/pallas_call | solution.py:38
  64.4 4.1 %back.5 = (bf16[800,256]{1,0:T(8,128)(2,1)S(1)}, bf16[768,512]{1,0:T(8,128)(2,1)S(1)}, bf16[1536,512]{1,0:T(8,128)(2,1)S(1)}, f32[8,128]{1,0:T(8,128)S(1)}) custom-call(s32[8]{0:T(128)S(1)} %stack.27.refs_0_, f32[800,768]{1,0:T(8,128)S(1)} %get-tuple-element.140.refs_1_, f32[800,768]{1,0:T(8,128)S(1)} %get-tuple-element.135.refs_1_.refs_2_, ...), custom_call_target="tpu_custom_call" | custom-call | flops 1024 | bytes 1024 | tf_op jit(solution)/shard_map/back/pallas_call | solution.py:38
  69.8 2.5 %taps_sums.3 = (f32[32,256]{1,0:T(8,128)S(1)}, f32[8,128]{1,0:T(8,128)S(1)}) custom-call(s32[8]{0:T(128)S(1)} %stack.27.refs_0_, bf16[800,256]{1,0:T(8,128)(2,1)S(1)} %get-tuple-element.174.refs_1_, bf16[832,768]{1,0:T(8,128)(2,1)S(1)} %get-tuple-element.134.refs_1_.refs_2_, f32[8,128]{1,0:T(8,128)S(1)} %get-tuple-element.175.refs_3_), custom_call_target="tpu_custom_call" | custom-call | flops 1024 | bytes 1024 | tf_op jit(solution)/shard_map/taps_sums/pallas_call | solution.py:38
  72.3 2.5 %taps_sums.4 = (f32[32,256]{1,0:T(8,128)S(1)}, f32[8,128]{1,0:T(8,128)S(1)}) custom-call(s32[8]{0:T(128)S(1)} %stack.27.refs_0_, bf16[800,256]{1,0:T(8,128)(2,1)S(1)} %get-tuple-element.173.refs_1_, bf16[832,768]{1,0:T(8,128)(2,1)S(1)} %get-tuple-element.134.refs_1_.refs_2_, f32[8,128]{1,0:T(8,128)S(1)} %get-tuple-element.176.refs_3_), custom_call_target="tpu_custom_call" | custom-call | flops 1024 | bytes 1024 | tf_op jit(solution)/shard_map/taps_sums/pallas_call | solution.py:38
  74.8 2.5 %taps_sums.5 = (f32[32,256]{1,0:T(8,128)S(1)}, f32[8,128]{1,0:T(8,128)S(1)}) custom-call(s32[8]{0:T(128)S(1)} %stack.27.refs_0_, bf16[800,256]{1,0:T(8,128)(2,1)S(1)} %get-tuple-element.172.refs_1_, bf16[832,768]{1,0:T(8,128)(2,1)S(1)} %get-tuple-element.134.refs_1_.refs_2_, f32[8,128]{1,0:T(8,128)S(1)} %get-tuple-element.177.refs_3_), custom_call_target="tpu_custom_call" | custom-call | flops 1024 | bytes 1024 | tf_op jit(solution)/shard_map/taps_sums/pallas_call | solution.py:38
  78.9 2.6 %norm_half.2 = (f32[384,768]{1,0:T(8,128)S(1)}, f32[384,768]{1,0:T(8,128)S(1)}, f32[8,128]{1,0:T(8,128)S(1)}) custom-call(s32[8]{0:T(128)S(1)} %stack.27.refs_0_, bf16[768,512]{1,0:T(8,128)(2,1)S(1)} %get-tuple-element.169.refs_1_, bf16[768,512]{1,0:T(8,128)(2,1)S(1)} %get-tuple-element.170.refs_2_, bf16[768,512]{1,0:T(8,128)(2,1)S(1)} %get-tuple-element.171.refs_3_, ...), custom_call_target="tpu_custom_call" | custom-call | flops 1024 | bytes 1024 | tf_op jit(solution)/shard_map/norm_half/pallas_call | solution.py:38
  82.9 2.6 %norm_half.3 = (bf16[384,768]{1,0:T(8,128)(2,1)S(1)}, bf16[384,768]{1,0:T(8,128)(2,1)S(1)}, f32[8,128]{1,0:T(8,128)S(1)}) custom-call(s32[8]{0:T(128)S(1)} %stack.27.refs_0_, bf16[768,512]{1,0:T(8,128)(2,1)S(1)} %get-tuple-element.169.refs_1_, bf16[768,512]{1,0:T(8,128)(2,1)S(1)} %get-tuple-element.170.refs_2_, ...), custom_call_target="tpu_custom_call" | custom-call | flops 1024 | bytes 1024 | tf_op jit(solution)/shard_map/norm_half/pallas_call | solution.py:38
  91.2 2.6 %collective-permute-done.11.refs_3_ = bf16[960,512]{1,0:T(8,128)(2,1)S(1)} collective-permute-done((bf16[960,512]{1,0:T(8,128)(2,1)S(1)}, bf16[960,512]{1,0:T(8,128)(2,1)S(1)}, u32[]{:S(2)}, u32[]{:S(2)}) %collective-permute-start.11) | collective-permute-done | bytes 983072 | tf_op jit(solution)/shard_map/ppermute | solution.py:57
  97.9 2.2 %input_rows.1 = (bf16[768,768]{1,0:T(8,128)(2,1)}, f32[8,128]{1,0:T(8,128)S(1)}) custom-call(s32[8]{0:T(128)S(1)} %stack.27.refs_0_, bf16[768,768]{1,0:T(8,128)(2,1)S(1)} %bitcast.19, f32[768,768]{1,0:T(8,128)S(1)} %get-tuple-element.201.refs_2_, bf16[832,1536]{1,0:T(8,128)(2,1)S(1)} %get-tuple-element.143.refs_6_.refs_5_.refs_3_, ...), custom_call_target="tpu_custom_call" | custom-call | flops 1024 | bytes 1024 | tf_op jit(solution)/shard_map/input_rows/pallas_call | solution.py:38
  102.7 4.8 %collective-permute-done.21.refs_3_ = bf16[528,512]{1,0:T(8,128)(2,1)S(1)} collective-permute-done((bf16[528,512]{1,0:T(8,128)(2,1)S(1)}, bf16[528,512]{1,0:T(8,128)(2,1)S(1)}, u32[]{:S(2)}, u32[]{:S(2)}) %collective-permute-start.21) | collective-permute-done | bytes 540704 | tf_op jit(solution)/shard_map/ppermute | solution.py:57
  109.7 2.2 %collective-permute-start.23 = (bf16[192,512]{1,0:T(8,128)(2,1)S(1)}, bf16[192,512]{1,0:T(8,128)(2,1)S(1)}, u32[]{:S(2)}, u32[]{:S(2)}) collective-permute-start(bf16[192,512]{1,0:T(8,128)(2,1)S(1)} %get-tuple-element.227), channel_id=1, source_target_pairs={{0,1},{1,0},{2,3},{3,2},{4,5},{5,4},{6,7},{7,6},{8,9},{9,8},{10,11... | collective-permute-start | bytes 589832 | tf_op jit(solution)/shard_map/ppermute | solution.py:57
  111.9 2.1 %collective-permute-done.19.refs_3_ = bf16[240,512]{1,0:T(8,128)(2,1)S(1)} collective-permute-done((bf16[240,512]{1,0:T(8,128)(2,1)S(1)}, bf16[240,512]{1,0:T(8,128)(2,1)S(1)}, u32[]{:S(2)}, u32[]{:S(2)}) %collective-permute-start.19) | collective-permute-done | bytes 245792 | tf_op jit(solution)/shard_map/ppermute | solution.py:57
  121.2 9.1 %collective-permute-done.24 = bf16[96,768]{1,0:T(8,128)(2,1)S(1)} collective-permute-done((bf16[96,768]{1,0:T(8,128)(2,1)S(1)}, bf16[96,768]{1,0:T(8,128)(2,1)S(1)}, u32[]{:S(2)}, u32[]{:S(2)}) %collective-permute-start.24) | collective-permute-done | bytes 147488 | tf_op jit(solution)/shard_map/ppermute | solution.py:57
  130.4 3.1 %collective-permute-done.26 = bf16[128,768]{1,0:T(8,128)(2,1)S(1)} collective-permute-done((bf16[128,768]{1,0:T(8,128)(2,1)S(1)}, bf16[128,768]{1,0:T(8,128)(2,1)S(1)}, u32[]{:S(2)}, u32[]{:S(2)}) %collective-permute-start.26) | collective-permute-done | bytes 196640 | tf_op jit(solution)/shard_map/ppermute | solution.py:57
  (83 shorter events, 45.5 us)
Async XLA Ops:
  0.6 14.5 %collective-permute-start = (bf16[768,768]{1,0:T(8,128)(2,1)}, bf16[768,768]{1,0:T(8,128)(2,1)S(1)}, u32[]{:S(2)}, u32[]{:S(2)}) collective-permute-start(bf16[768,768]{1,0:T(8,128)(2,1)} %bitcast.16), channel_id=1, source_target_pairs={{0,2},{2,0},{1,3},{3,1},{4,6},{6,4},{5,7},{7,5},{8,10},{10,8},{9,1... | collective-permute-start | bytes 3538952 | tf_op jit(solution)/shard_map/ppermute | solution.py:57
  1.1 17.4 %collective-permute-start.3 = (bf16[768,768]{1,0:T(8,128)(2,1)}, bf16[768,768]{1,0:T(8,128)(2,1)S(1)}, u32[]{:S(2)}, u32[]{:S(2)}) collective-permute-start(bf16[768,768]{1,0:T(8,128)(2,1)} %bitcast.12), channel_id=1, source_target_pairs={{0,2},{2,0},{1,3},{3,1},{4,6},{6,4},{5,7},{7,5},{8,10},{10,8},{9,1... | collective-permute-start | bytes 3538952 | tf_op jit(solution)/shard_map/ppermute | solution.py:57
  3.4 8.7 %collective-permute-start.1 = (bf16[48,768]{1,0:T(8,128)(2,1)S(1)}, bf16[48,768]{1,0:T(8,128)(2,1)S(1)}, u32[]{:S(2)}, u32[]{:S(2)}) collective-permute-start(bf16[48,768]{1,0:T(8,128)(2,1)S(1)} %get-tuple-element.125), channel_id=1, source_target_pairs={{0,4},{4,8},{8,12},{12,16},{16,20},{20,24},{24,28},{1,5},{5,9},{9,... | collective-permute-start | bytes 221192 | tf_op jit(solution)/shard_map/ppermute | solution.py:673
  8.3 6.2 %collective-permute-start.2 = (bf16[48,768]{1,0:T(8,128)(2,1)S(1)}, bf16[48,768]{1,0:T(8,128)(2,1)S(1)}, u32[]{:S(2)}, u32[]{:S(2)}) collective-permute-start(bf16[48,768]{1,0:T(8,128)(2,1)S(1)} %get-tuple-element.126), channel_id=1, source_target_pairs={{4,0},{8,4},{12,8},{16,12},{20,16},{24,20},{28,24},{5,1},{9,5},{13... | collective-permute-start | bytes 221192 | tf_op jit(solution)/shard_map/ppermute | solution.py:673
  38.8 8.7 %collective-permute-start.6 = (f32[800,128]{1,0:T(8,128)S(1)}, f32[800,128]{1,0:T(8,128)S(1)}, u32[]{:S(2)}, u32[]{:S(2)}) collective-permute-start(f32[800,128]{1,0:T(8,128)S(1)} %get-tuple-element.144.refs_9_), channel_id=1, source_target_pairs={{0,2},{2,0},{1,3},{3,1},{4,6},{6,4},{5,7},{7,5},{8,10},{10,8},{9,1... | collective-permute-start | bytes 1228808 | tf_op jit(solution)/shard_map/ppermute | solution.py:57
  41.9 13.7 %collective-permute-start.8 = (bf16[768,256]{1,0:T(8,128)(2,1)S(1)}, bf16[768,256]{1,0:T(8,128)(2,1)S(1)}, u32[]{:S(2)}, u32[]{:S(2)}) collective-permute-start(bf16[768,256]{1,0:T(8,128)(2,1)S(1)} %get-tuple-element.154), channel_id=1, source_target_pairs={{0,8},{4,12},{8,0},{12,4},{16,24},{20,28},{24,16},{28,20},{1,9},{5... | collective-permute-start | bytes 1179656 | tf_op jit(solution)/shard_map/ppermute | solution.py:57
  43.5 12.0 %collective-permute-start.9 = (bf16[768,256]{1,0:T(8,128)(2,1)S(1)}, bf16[768,256]{1,0:T(8,128)(2,1)S(1)}, u32[]{:S(2)}, u32[]{:S(2)}) collective-permute-start(bf16[768,256]{1,0:T(8,128)(2,1)S(1)} %get-tuple-element.156), channel_id=1, source_target_pairs={{0,1},{1,0},{2,3},{3,2},{4,5},{5,4},{6,7},{7,6},{8,9},{9,8},{10,11... | collective-permute-start | bytes 1179656 | tf_op jit(solution)/shard_map/ppermute | solution.py:57
  45.0 11.3 %collective-permute-start.10 = (bf16[768,256]{1,0:T(8,128)(2,1)S(1)}, bf16[768,256]{1,0:T(8,128)(2,1)S(1)}, u32[]{:S(2)}, u32[]{:S(2)}) collective-permute-start(bf16[768,256]{1,0:T(8,128)(2,1)S(1)} %get-tuple-element.157), channel_id=1, source_target_pairs={{0,4},{4,0},{8,12},{12,8},{16,20},{20,16},{24,28},{28,24},{1,5},{5... | collective-permute-start | bytes 1179656 | tf_op jit(solution)/shard_map/ppermute | solution.py:57
  57.0 24.5 %collective-permute-start.13 = (bf16[960,512]{1,0:T(8,128)(2,1)S(1)}, bf16[960,512]{1,0:T(8,128)(2,1)S(1)}, u32[]{:S(2)}, u32[]{:S(2)}) collective-permute-start(bf16[960,512]{1,0:T(8,128)(2,1)S(1)} %get-tuple-element.186), channel_id=1, source_target_pairs={{0,1},{1,0},{2,3},{3,2},{4,5},{5,4},{6,7},{7,6},{8,9},{9,8},{10,11... | collective-permute-start | bytes 2949128 | tf_op jit(solution)/shard_map/ppermute | solution.py:57
  62.6 23.5 %collective-permute-start.16 = (bf16[960,512]{1,0:T(8,128)(2,1)S(1)}, bf16[960,512]{1,0:T(8,128)(2,1)S(1)}, u32[]{:S(2)}, u32[]{:S(2)}) collective-permute-start(bf16[960,512]{1,0:T(8,128)(2,1)S(1)} %get-tuple-element.194), channel_id=1, source_target_pairs={{0,4},{4,0},{8,12},{12,8},{16,20},{20,16},{24,28},{28,24},{1,5},{5... | collective-permute-start | bytes 2949128 | tf_op jit(solution)/shard_map/ppermute | solution.py:57
  64.4 31.8 %collective-permute-start.7 = (bf16[768,768]{1,0:T(8,128)(2,1)S(1)}, bf16[768,768]{1,0:T(8,128)(2,1)S(1)}, u32[]{:S(2)}, u32[]{:S(2)}) collective-permute-start(bf16[768,768]{1,0:T(8,128)(2,1)S(1)} %get-tuple-element.150), channel_id=1, source_target_pairs={{0,2},{2,0},{1,3},{3,1},{4,6},{6,4},{5,7},{7,5},{8,10},{10,8},{9,1... | collective-permute-start | bytes 3538952 | tf_op jit(solution)/shard_map/ppermute | solution.py:57
  69.2 24.6 %collective-permute-start.11 = (bf16[960,512]{1,0:T(8,128)(2,1)S(1)}, bf16[960,512]{1,0:T(8,128)(2,1)S(1)}, u32[]{:S(2)}, u32[]{:S(2)}) collective-permute-start(bf16[960,512]{1,0:T(8,128)(2,1)S(1)} %get-tuple-element.168), channel_id=1, source_target_pairs={{0,8},{4,12},{8,0},{12,4},{16,24},{20,28},{24,16},{28,20},{1,9},{5... | collective-permute-start | bytes 2949128 | tf_op jit(solution)/shard_map/ppermute | solution.py:57
  77.3 5.0 %collective-permute-start.12 = (f32[32,768]{1,0:T(8,128)S(1)}, f32[32,768]{1,0:T(8,128)S(1)}, u32[]{:S(2)}, u32[]{:S(2)}) collective-permute-start(f32[32,768]{1,0:T(8,128)S(1)} %constant_dynamic-update-slice_fusion.refs_1_), channel_id=1, source_target_pairs={{0,1},{1,0},{2,3},{3,2},{4,5},{5,4},{6,7},{7,6},{8,9},{9,8},{10,11... | collective-permute-start | bytes 294920 | tf_op jit(solution)/shard_map/ppermute | solution.py:57
  85.6 3.6 %collective-permute-start.15 = (bf16[384,768]{1,0:T(8,128)(2,1)S(1)}, bf16[384,768]{1,0:T(8,128)(2,1)S(1)}, u32[]{:S(2)}, u32[]{:S(2)}) collective-permute-start(bf16[384,768]{1,0:T(8,128)(2,1)S(1)} %get-tuple-element.191), channel_id=1, source_target_pairs={{0,2},{2,0},{1,3},{3,1},{4,6},{6,4},{5,7},{7,5},{8,10},{10,8},{9,1... | collective-permute-start | bytes 1769480 | tf_op jit(solution)/shard_map/ppermute | solution.py:57
  86.1 14.1 %collective-permute-start.18 = (bf16[480,512]{1,0:T(8,128)(2,1)S(1)}, bf16[480,512]{1,0:T(8,128)(2,1)S(1)}, u32[]{:S(2)}, u32[]{:S(2)}) collective-permute-start(bf16[480,512]{1,0:T(8,128)(2,1)S(1)} %get-tuple-element.208), channel_id=1, source_target_pairs={{0,4},{4,0},{8,12},{12,8},{16,20},{20,16},{24,28},{28,24},{1,5},{5... | collective-permute-start | bytes 1474568 | tf_op jit(solution)/shard_map/ppermute | solution.py:57
  87.9 19.5 %collective-permute-start.21 = (bf16[528,512]{1,0:T(8,128)(2,1)S(1)}, bf16[528,512]{1,0:T(8,128)(2,1)S(1)}, u32[]{:S(2)}, u32[]{:S(2)}) collective-permute-start(bf16[528,512]{1,0:T(8,128)(2,1)S(1)} %get-tuple-element.218), channel_id=1, source_target_pairs={{0,8},{4,12},{8,0},{12,4},{16,24},{20,28},{24,16},{28,20},{1,9},{5... | collective-permute-start | bytes 1622024 | tf_op jit(solution)/shard_map/ppermute | solution.py:57
  91.2 6.8 %collective-permute-start.17 = (f32[768,128]{1,0:T(8,128)S(1)}, f32[768,128]{1,0:T(8,128)S(1)}, u32[]{:S(2)}, u32[]{:S(2)}) collective-permute-start(f32[768,128]{1,0:T(8,128)S(1)} %get-tuple-element.203.refs_5_), channel_id=1, source_target_pairs={{0,2},{2,0},{1,3},{3,1},{4,6},{6,4},{5,7},{7,5},{8,10},{10,8},{9,1... | collective-permute-start | bytes 1179656 | tf_op jit(solution)/shard_map/ppermute | solution.py:57
  94.7 13.5 %collective-permute-start.20 = (bf16[480,512]{1,0:T(8,128)(2,1)S(1)}, bf16[480,512]{1,0:T(8,128)(2,1)S(1)}, u32[]{:S(2)}, u32[]{:S(2)}) collective-permute-start(bf16[480,512]{1,0:T(8,128)(2,1)S(1)} %get-tuple-element.215), channel_id=1, source_target_pairs={{0,1},{1,0},{2,3},{3,2},{4,5},{5,4},{6,7},{7,6},{8,9},{9,8},{10,11... | collective-permute-start | bytes 1474568 | tf_op jit(solution)/shard_map/ppermute | solution.py:57
  100.9 13.2 %collective-permute-start.19 = (bf16[240,512]{1,0:T(8,128)(2,1)S(1)}, bf16[240,512]{1,0:T(8,128)(2,1)S(1)}, u32[]{:S(2)}, u32[]{:S(2)}) collective-permute-start(bf16[240,512]{1,0:T(8,128)(2,1)S(1)} %get-tuple-element.212), channel_id=1, source_target_pairs={{0,16},{4,20},{8,24},{12,28},{16,0},{20,4},{24,8},{28,12},{1,17},{... | collective-permute-start | bytes 737288 | tf_op jit(solution)/shard_map/ppermute | solution.py:57
  108.8 9.6 %collective-permute-start.25 = (bf16[240,512]{1,0:T(8,128)(2,1)S(1)}, bf16[240,512]{1,0:T(8,128)(2,1)S(1)}, u32[]{:S(2)}, u32[]{:S(2)}) collective-permute-start(bf16[240,512]{1,0:T(8,128)(2,1)S(1)} %get-tuple-element.233), channel_id=1, source_target_pairs={{0,4},{4,0},{8,12},{12,8},{16,20},{20,16},{24,28},{28,24},{1,5},{5... | collective-permute-start | bytes 737288 | tf_op jit(solution)/shard_map/ppermute | solution.py:57
  109.7 6.7 %collective-permute-start.23 = (bf16[192,512]{1,0:T(8,128)(2,1)S(1)}, bf16[192,512]{1,0:T(8,128)(2,1)S(1)}, u32[]{:S(2)}, u32[]{:S(2)}) collective-permute-start(bf16[192,512]{1,0:T(8,128)(2,1)S(1)} %get-tuple-element.227), channel_id=1, source_target_pairs={{0,1},{1,0},{2,3},{3,2},{4,5},{5,4},{6,7},{7,6},{8,9},{9,8},{10,11... | collective-permute-start | bytes 589832 | tf_op jit(solution)/shard_map/ppermute | solution.py:57
  114.7 6.5 %collective-permute-start.22 = (bf16[96,512]{1,0:T(8,128)(2,1)S(1)}, bf16[96,512]{1,0:T(8,128)(2,1)S(1)}, u32[]{:S(2)}, u32[]{:S(2)}) collective-permute-start(bf16[96,512]{1,0:T(8,128)(2,1)S(1)} %get-tuple-element.224), channel_id=1, source_target_pairs={{0,8},{4,12},{8,0},{12,4},{16,24},{20,28},{24,16},{28,20},{1,9},{5... | collective-permute-start | bytes 294920 | tf_op jit(solution)/shard_map/ppermute | solution.py:57
  117.0 13.3 %collective-permute-start.24 = (bf16[96,768]{1,0:T(8,128)(2,1)S(1)}, bf16[96,768]{1,0:T(8,128)(2,1)S(1)}, u32[]{:S(2)}, u32[]{:S(2)}) collective-permute-start(bf16[96,768]{1,0:T(8,128)(2,1)S(1)} %get-tuple-element.230), channel_id=1, source_target_pairs={{0,16},{4,20},{8,24},{12,28},{16,0},{20,4},{24,8},{28,12},{1,17},{... | collective-permute-start | bytes 442376 | tf_op jit(solution)/shard_map/ppermute | solution.py:57
  119.6 14.0 %collective-permute-start.26 = (bf16[128,768]{1,0:T(8,128)(2,1)S(1)}, bf16[128,768]{1,0:T(8,128)(2,1)S(1)}, u32[]{:S(2)}, u32[]{:S(2)}) collective-permute-start(bf16[128,768]{1,0:T(8,128)(2,1)S(1)} %get-tuple-element.236), channel_id=1, source_target_pairs={{0,16},{4,20},{8,24},{12,28},{16,0},{20,4},{24,8},{28,12},{1,17},{... | collective-permute-start | bytes 589832 | tf_op jit(solution)/shard_map/ppermute | solution.py:57
  (6 other events, 22.0 us)

commit v7 on v6

--- a/solution.py
+++ b/solution.py
@@ -300,7 +300,16 @@
         c.wait()
 
 
-def front(info, own, other, halo_own, halo_other, wv, wg, w_out, norm, rstd, hid, sig, slope, ends, edge):
+def upstream_ends(info, halo_own, halo_other, w_out, ends, edge):
+    half = halo_own.shape[1]
+    mine, theirs = halves_at(info, half)
+    for a, at in ((halo_own, mine), (halo_other, theirs)):
+        edge[:NEAR, pl.ds(at, half)] = a[WIDE : WIDE + NEAR, :]
+        edge[NEAR:, pl.ds(at, half)] = a[2 * WIDE + NEAR :, :]
+    ends[...] = dot(edge[...], w_out[...], NT)
+
+
+def front(info, own, other, halo_own, halo_other, wv, wg, norm, rstd, hid, sig, slope):
     count, half = own.shape
     channels = wv.shape[1]
     mine, theirs = halves_at(info, half)
@@ -331,11 +340,6 @@
     lax.fori_loop(0, count // chunk, body, 0, unroll=2)
     for to, at in ((0, 0), (WIDE + count, WIDE + NEAR)):
         normalize(pl.ds(to, WIDE), halo_own[at : at + WIDE, :], halo_other[at : at + WIDE, :])
-    for a, at in ((halo_own, mine), (halo_other, theirs)):
-        edge[:NEAR, pl.ds(at, half)] = a[WIDE : WIDE + NEAR, :]
-        edge[NEAR:, pl.ds(at, half)] = a[2 * WIDE + NEAR :, :]
-    ends[...] = dot(edge[...], w_out[...], NT)
-
     tile = channels // 3
     rows = count + 2 * WIDE
     step = rows // 2
@@ -696,24 +700,22 @@
         after=[mark],
         far=[x, w_value, w_gate],
     )
-    norm, rstd, hid, sig, slope, ends, _ = run(
+    norm, rstd, hid, sig, slope, _ = run(
         front,
         info,
-        [xv, x_other, halo, halo_other, wv, wg, wo],
+        [xv, x_other, halo, halo_other, wv, wg],
         [
             ((ext, width), bf16),
             ((count, LANES), f32),
             ((ext, channels), bf16),
             ((count, channels), bf16),
             ((count, channels), bf16),
-            ((2 * NEAR, channels), f32),
         ],
-        scratch=[pltpu.VMEM((2 * NEAR, width), bf16)],
         after=[mark],
     )
     row_sums = ((rows, LANES), f32)
     column = pltpu.VMEM((rows, LANES), f32)
-    conv, stats, _ = run(
+    conv, stats, mark = run(
         depthwise,
         info,
         [hid, kernel],
@@ -721,6 +723,14 @@
         scratch=[pltpu.VMEM((ext + 16, LANES), f32), column, column],
     )
     stats_other = swap(stats, "tensor")
+    ends, mark = run(
+        upstream_ends,
+        info,
+        [halo, halo_other, wo],
+        [((2 * NEAR, channels), f32)],
+        scratch=[pltpu.VMEM((2 * NEAR, width), bf16)],
+        after=[mark],
+    )
     swished, dswish, stats2, _ = run(
         swish,
         info,

time: 136 us -> 135 us (level)
    pallas_call x34 -> x35, Pallas kernels: 73.6 us -> 74 us  [run(): pl.pallas_call(body, in_specs=[SMEM] + [space] * near + [HBM] * len(far)...]
  transfers between devices with their start and end apart: 27 -> 27, of which waited for: 9 -> 8; matrix products, arithmetic and copies ran while one was open for 0% -> 0% of each run, Pallas kernels for 40% -> 42%
where the time goes in v7:
time: 135 us
  Pallas kernels  74 us (55%)
  starting transfers between devices  29.7 us (22%)
  waiting for transfers between devices  27.1 us (20%)
  between operations  1.73 us (1%)
  other arithmetic  1.69 us (1%)
    pallas_call x35, Pallas kernels, run(): pl.pallas_call(body, in_specs=[SMEM] + [space] * near + [HBM] * len(far)...  74 us
    ppermute x25, waiting for transfers between devices, swap(): return lax.ppermute(value, axis, [(i, i ^ 1 << bit) for i in range(size)])  24.7 us
    ppermute x25, starting transfers between devices, swap(): return lax.ppermute(value, axis, [(i, i ^ 1 << bit) for i in range(size)])  23.6 us
    ppermute x1, starting transfers between devices, shards(): lax.ppermute(last, 'seq', up)  4.85 us
  transfers between devices with their start and end apart: 27, of which 8 were waited for; matrix products, arithmetic and copies ran while one was open for 0% of the time, Pallas kernels for 42%

profile of v7, /device:TPU:0, one launch (start us, length us, event | category | flops | bytes accessed | tf_op | source)
XLA Modules:
  0.0 135.1 jit_solution(2347665749704220341)
XLA Ops:
  3.4 4.9 %collective-permute-start.1 = (bf16[48,768]{1,0:T(8,128)(2,1)S(1)}, bf16[48,768]{1,0:T(8,128)(2,1)S(1)}, u32[]{:S(2)}, u32[]{:S(2)}) collective-permute-start(bf16[48,768]{1,0:T(8,128)(2,1)S(1)} %get-tuple-element.126), channel_id=1, source_target_pairs={{0,4},{4,8},{8,12},{12,16},{16,20},{20,24},{24,28},{1,5},{5,9},{9,... | collective-permute-start | bytes 221192 | tf_op jit(solution)/shard_map/ppermute | solution.py:677
  9.6 2.5 %prepare.1 = (bf16[768,768]{1,0:T(8,128)(2,1)S(1)}, bf16[768,1536]{1,0:T(8,128)(2,1)S(1)}, f32[8,128]{1,0:T(8,128)S(1)}) custom-call(s32[8]{0:T(128)S(1)} %stack.27.refs_0_, bf16[768,768]{1,0:T(8,128)(2,1)} %bitcast.18, bf16[768,1536]{1,0:T(8,128)(2,1)} %refs_2_.2, f32[8,128]{1,0:T(8,128)S(1)} %get-tuple-element.123.refs_3_), custom_call_target="tpu_custom_call" | custom-call | flops 1024 | bytes 1024 | tf_op jit(solution)/shard_map/prepare/pallas_call | solution.py:38
  12.1 2.4 %collective-permute-done.2.refs_2_ = bf16[48,768]{1,0:T(8,128)(2,1)S(1)} collective-permute-done((bf16[48,768]{1,0:T(8,128)(2,1)S(1)}, bf16[48,768]{1,0:T(8,128)(2,1)S(1)}, u32[]{:S(2)}, u32[]{:S(2)}) %collective-permute-start.2) | collective-permute-done | bytes 73760 | tf_op jit(solution)/shard_map/ppermute | solution.py:677
  15.2 3.4 %upstream.1 = (bf16[768,1536]{1,0:T(8,128)(2,1)S(1)}, bf16[768,768]{1,0:T(8,128)(2,1)S(1)}, bf16[768,768]{1,0:T(8,128)(2,1)S(1)}, bf16[1536,768]{1,0:T(8,128)(2,...) custom-call(s32[8]{0:T(128)S(1)} %stack.27.refs_0_, bf16[768,768]{1,0:T(8,128)(2,1)S(1)} %get-tuple-element.124.refs_1_, ...), custom_call_target="tpu_custom_call" | custom-call | flops 1024 | bytes 1024 | tf_op jit(solution)/shard_map/upstream/pallas_call | solution.py:38
  18.5 6.5 %front.1 = (bf16[832,1536]{1,0:T(8,128)(2,1)S(1)}, f32[768,128]{1,0:T(8,128)S(1)}, bf16[832,768]{1,0:T(8,128)(2,1)S(1)}, bf16[768,768]{1,0:T(8,128)(2,1)S(1)}, b...) custom-call(s32[8]{0:T(128)S(1)} %stack.27.refs_0_, bf16[768,768]{1,0:T(8,128)(2,1)S(1)} %get-tuple-element.130.refs_1_, ...), custom_call_target="tpu_custom_call" | custom-call | flops 1024 | bytes 1024 | tf_op jit(solution)/shard_map/front/pallas_call | solution.py:38
  25.1 6.7 %depthwise.1 = (f32[800,768]{1,0:T(8,128)S(1)}, f32[800,128]{1,0:T(8,128)S(1)}, f32[8,128]{1,0:T(8,128)S(1)}) custom-call(s32[8]{0:T(128)S(1)} %stack.27.refs_0_, bf16[832,768]{1,0:T(8,128)(2,1)S(1)} %get-tuple-element.135.refs_1_.refs_2_, bf16[31,768]{1,0:T(8,128)(2,1)S(1)} %copy-done.2), custom_call_target="tpu_custom_call" | custom-call | flops 1024 | bytes 1024 | tf_op jit(solution)/shard_map/depthwise/pallas_call | solution.py:38
  34.1 3.9 %swish.1 = (bf16[768,768]{1,0:T(8,128)(2,1)S(1)}, f32[800,768]{1,0:T(8,128)S(1)}, f32[800,128]{1,0:T(8,128)S(1)}, f32[8,128]{1,0:T(8,128)}) custom-call(s32[8]{0:T(128)S(1)} %stack.27.refs_0_, f32[800,768]{1,0:T(8,128)S(1)} %get-tuple-element.136.refs_1_.refs_2_, bf16[768,768]{1,0:T(8,128)(2,1)S(1)} %get-tuple-element.137.refs_2_, ...), custom_call_target="tpu_custom_call" | custom-call | flops 1024 | bytes 1024 | tf_op jit(solution)/shard_map/swish/pallas_call | solution.py:38
  38.0 2.7 %out_terms.1 = (bf16[768,256]{1,0:T(8,128)(2,1)S(1)}, bf16[768,256]{1,0:T(8,128)(2,1)S(1)}, bf16[768,256]{1,0:T(8,128)(2,1)S(1)}, bf16[768,256]{1,0:T(8,128)(2,1...) custom-call(s32[8]{0:T(128)S(1)} %stack.27.refs_0_, ...), custom_call_target="tpu_custom_call" | custom-call | flops 1024 | bytes 1024 | tf_op jit(solution)/shard_map/out_terms/pallas_call | solution.py:38
  43.8 2.4 %collective-permute-start.10 = (bf16[768,256]{1,0:T(8,128)(2,1)S(1)}, bf16[768,256]{1,0:T(8,128)(2,1)S(1)}, u32[]{:S(2)}, u32[]{:S(2)}) collective-permute-start(bf16[768,256]{1,0:T(8,128)(2,1)S(1)} %get-tuple-element.159), channel_id=1, source_target_pairs={{0,4},{4,0},{8,12},{12,8},{16,20},{20,16},{24,28},{28,24},{1,5},{5... | collective-permute-start | bytes 1179656 | tf_op jit(solution)/shard_map/ppermute | solution.py:57
  46.2 4.8 %back.3 = (bf16[800,256]{1,0:T(8,128)(2,1)S(1)}, bf16[768,512]{1,0:T(8,128)(2,1)S(1)}, bf16[1536,512]{1,0:T(8,128)(2,1)S(1)}, f32[3,800,128]{2,1,0:T(8,128)S(1)}, f32[8,128]{1,0:T(8,128)S(1)}) custom-call(s32[8]{0:T(128)S(1)} %stack.27.refs_0_, f32[800,768]{1,0:T(8,128)S(1)} %get-tuple-element.142.refs_1_, ...), custom_call_target="tpu_custom_call" | custom-call | flops 1024 | bytes 1024 | tf_op jit(solution)/shard_map/back/pallas_call | solution.py:38
  56.8 4.2 %back.4 = (bf16[800,256]{1,0:T(8,128)(2,1)S(1)}, bf16[768,512]{1,0:T(8,128)(2,1)S(1)}, bf16[1536,512]{1,0:T(8,128)(2,1)S(1)}, f32[8,128]{1,0:T(8,128)S(1)}) custom-call(s32[8]{0:T(128)S(1)} %stack.27.refs_0_, f32[800,768]{1,0:T(8,128)S(1)} %get-tuple-element.142.refs_1_, f32[800,768]{1,0:T(8,128)S(1)} %get-tuple-element.136.refs_1_.refs_2_, ...), custom_call_target="tpu_custom_call" | custom-call | flops 1024 | bytes 1024 | tf_op jit(solution)/shard_map/back/pallas_call | solution.py:38
  63.6 4.1 %back.5 = (bf16[800,256]{1,0:T(8,128)(2,1)S(1)}, bf16[768,512]{1,0:T(8,128)(2,1)S(1)}, bf16[1536,512]{1,0:T(8,128)(2,1)S(1)}, f32[8,128]{1,0:T(8,128)S(1)}) custom-call(s32[8]{0:T(128)S(1)} %stack.27.refs_0_, f32[800,768]{1,0:T(8,128)S(1)} %get-tuple-element.142.refs_1_, f32[800,768]{1,0:T(8,128)S(1)} %get-tuple-element.136.refs_1_.refs_2_, ...), custom_call_target="tpu_custom_call" | custom-call | flops 1024 | bytes 1024 | tf_op jit(solution)/shard_map/back/pallas_call | solution.py:38
  68.9 2.5 %taps_sums.3 = (f32[32,256]{1,0:T(8,128)S(1)}, f32[8,128]{1,0:T(8,128)S(1)}) custom-call(s32[8]{0:T(128)S(1)} %stack.27.refs_0_, bf16[800,256]{1,0:T(8,128)(2,1)S(1)} %get-tuple-element.176.refs_1_, bf16[832,768]{1,0:T(8,128)(2,1)S(1)} %get-tuple-element.135.refs_1_.refs_2_, f32[8,128]{1,0:T(8,128)S(1)} %get-tuple-element.177.refs_3_), custom_call_target="tpu_custom_call" | custom-call | flops 1024 | bytes 1024 | tf_op jit(solution)/shard_map/taps_sums/pallas_call | solution.py:38
  71.5 2.5 %taps_sums.4 = (f32[32,256]{1,0:T(8,128)S(1)}, f32[8,128]{1,0:T(8,128)S(1)}) custom-call(s32[8]{0:T(128)S(1)} %stack.27.refs_0_, bf16[800,256]{1,0:T(8,128)(2,1)S(1)} %get-tuple-element.175.refs_1_, bf16[832,768]{1,0:T(8,128)(2,1)S(1)} %get-tuple-element.135.refs_1_.refs_2_, f32[8,128]{1,0:T(8,128)S(1)} %get-tuple-element.178.refs_3_), custom_call_target="tpu_custom_call" | custom-call | flops 1024 | bytes 1024 | tf_op jit(solution)/shard_map/taps_sums/pallas_call | solution.py:38
  74.0 2.5 %taps_sums.5 = (f32[32,256]{1,0:T(8,128)S(1)}, f32[8,128]{1,0:T(8,128)S(1)}) custom-call(s32[8]{0:T(128)S(1)} %stack.27.refs_0_, bf16[800,256]{1,0:T(8,128)(2,1)S(1)} %get-tuple-element.174.refs_1_, bf16[832,768]{1,0:T(8,128)(2,1)S(1)} %get-tuple-element.135.refs_1_.refs_2_, f32[8,128]{1,0:T(8,128)S(1)} %get-tuple-element.179.refs_3_), custom_call_target="tpu_custom_call" | custom-call | flops 1024 | bytes 1024 | tf_op jit(solution)/shard_map/taps_sums/pallas_call | solution.py:38
  78.1 2.6 %norm_half.2 = (f32[384,768]{1,0:T(8,128)S(1)}, f32[384,768]{1,0:T(8,128)S(1)}, f32[8,128]{1,0:T(8,128)S(1)}) custom-call(s32[8]{0:T(128)S(1)} %stack.27.refs_0_, bf16[768,512]{1,0:T(8,128)(2,1)S(1)} %get-tuple-element.171.refs_1_, bf16[768,512]{1,0:T(8,128)(2,1)S(1)} %get-tuple-element.172.refs_2_, bf16[768,512]{1,0:T(8,128)(2,1)S(1)} %get-tuple-element.173.refs_3_, ...), custom_call_target="tpu_custom_call" | custom-call | flops 1024 | bytes 1024 | tf_op jit(solution)/shard_map/norm_half/pallas_call | solution.py:38
  82.1 2.6 %norm_half.3 = (bf16[384,768]{1,0:T(8,128)(2,1)S(1)}, bf16[384,768]{1,0:T(8,128)(2,1)S(1)}, f32[8,128]{1,0:T(8,128)S(1)}) custom-call(s32[8]{0:T(128)S(1)} %stack.27.refs_0_, bf16[768,512]{1,0:T(8,128)(2,1)S(1)} %get-tuple-element.171.refs_1_, bf16[768,512]{1,0:T(8,128)(2,1)S(1)} %get-tuple-element.172.refs_2_, ...), custom_call_target="tpu_custom_call" | custom-call | flops 1024 | bytes 1024 | tf_op jit(solution)/shard_map/norm_half/pallas_call | solution.py:38
  90.4 2.7 %collective-permute-done.11.refs_3_ = bf16[960,512]{1,0:T(8,128)(2,1)S(1)} collective-permute-done((bf16[960,512]{1,0:T(8,128)(2,1)S(1)}, bf16[960,512]{1,0:T(8,128)(2,1)S(1)}, u32[]{:S(2)}, u32[]{:S(2)}) %collective-permute-start.11) | collective-permute-done | bytes 983072 | tf_op jit(solution)/shard_map/ppermute | solution.py:57
  97.1 2.2 %input_rows.1 = (bf16[768,768]{1,0:T(8,128)(2,1)}, f32[8,128]{1,0:T(8,128)S(1)}) custom-call(s32[8]{0:T(128)S(1)} %stack.27.refs_0_, bf16[768,768]{1,0:T(8,128)(2,1)S(1)} %bitcast.19, f32[768,768]{1,0:T(8,128)S(1)} %get-tuple-element.203.refs_2_, bf16[832,1536]{1,0:T(8,128)(2,1)S(1)} %get-tuple-element.145.refs_6_.refs_5_.refs_3_, ...), custom_call_target="tpu_custom_call" | custom-call | flops 1024 | bytes 1024 | tf_op jit(solution)/shard_map/input_rows/pallas_call | solution.py:38
  101.8 4.8 %collective-permute-done.21.refs_3_ = bf16[528,512]{1,0:T(8,128)(2,1)S(1)} collective-permute-done((bf16[528,512]{1,0:T(8,128)(2,1)S(1)}, bf16[528,512]{1,0:T(8,128)(2,1)S(1)}, u32[]{:S(2)}, u32[]{:S(2)}) %collective-permute-start.21) | collective-permute-done | bytes 540704 | tf_op jit(solution)/shard_map/ppermute | solution.py:57
  108.6 2.6 %collective-permute-start.23 = (bf16[192,512]{1,0:T(8,128)(2,1)S(1)}, bf16[192,512]{1,0:T(8,128)(2,1)S(1)}, u32[]{:S(2)}, u32[]{:S(2)}) collective-permute-start(bf16[192,512]{1,0:T(8,128)(2,1)S(1)} %get-tuple-element.229), channel_id=1, source_target_pairs={{0,1},{1,0},{2,3},{3,2},{4,5},{5,4},{6,7},{7,6},{8,9},{9,8},{10,11... | collective-permute-start | bytes 589832 | tf_op jit(solution)/shard_map/ppermute | solution.py:57
  111.1 2.1 %collective-permute-done.19.refs_3_ = bf16[240,512]{1,0:T(8,128)(2,1)S(1)} collective-permute-done((bf16[240,512]{1,0:T(8,128)(2,1)S(1)}, bf16[240,512]{1,0:T(8,128)(2,1)S(1)}, u32[]{:S(2)}, u32[]{:S(2)}) %collective-permute-start.19) | collective-permute-done | bytes 245792 | tf_op jit(solution)/shard_map/ppermute | solution.py:57
  120.4 9.1 %collective-permute-done.24 = bf16[96,768]{1,0:T(8,128)(2,1)S(1)} collective-permute-done((bf16[96,768]{1,0:T(8,128)(2,1)S(1)}, bf16[96,768]{1,0:T(8,128)(2,1)S(1)}, u32[]{:S(2)}, u32[]{:S(2)}) %collective-permute-start.24) | collective-permute-done | bytes 147488 | tf_op jit(solution)/shard_map/ppermute | solution.py:57
  129.6 3.2 %collective-permute-done.26 = bf16[128,768]{1,0:T(8,128)(2,1)S(1)} collective-permute-done((bf16[128,768]{1,0:T(8,128)(2,1)S(1)}, bf16[128,768]{1,0:T(8,128)(2,1)S(1)}, u32[]{:S(2)}, u32[]{:S(2)}) %collective-permute-start.26) | collective-permute-done | bytes 196640 | tf_op jit(solution)/shard_map/ppermute | solution.py:57
  (84 shorter events, 45.6 us)
Async XLA Ops:
  0.6 14.5 %collective-permute-start = (bf16[768,768]{1,0:T(8,128)(2,1)}, bf16[768,768]{1,0:T(8,128)(2,1)S(1)}, u32[]{:S(2)}, u32[]{:S(2)}) collective-permute-start(bf16[768,768]{1,0:T(8,128)(2,1)} %bitcast.16), channel_id=1, source_target_pairs={{0,2},{2,0},{1,3},{3,1},{4,6},{6,4},{5,7},{7,5},{8,10},{10,8},{9,1... | collective-permute-start | bytes 3538952 | tf_op jit(solution)/shard_map/ppermute | solution.py:57
  1.1 17.4 %collective-permute-start.3 = (bf16[768,768]{1,0:T(8,128)(2,1)}, bf16[768,768]{1,0:T(8,128)(2,1)S(1)}, u32[]{:S(2)}, u32[]{:S(2)}) collective-permute-start(bf16[768,768]{1,0:T(8,128)(2,1)} %bitcast.12), channel_id=1, source_target_pairs={{0,2},{2,0},{1,3},{3,1},{4,6},{6,4},{5,7},{7,5},{8,10},{10,8},{9,1... | collective-permute-start | bytes 3538952 | tf_op jit(solution)/shard_map/ppermute | solution.py:57
  3.4 8.7 %collective-permute-start.1 = (bf16[48,768]{1,0:T(8,128)(2,1)S(1)}, bf16[48,768]{1,0:T(8,128)(2,1)S(1)}, u32[]{:S(2)}, u32[]{:S(2)}) collective-permute-start(bf16[48,768]{1,0:T(8,128)(2,1)S(1)} %get-tuple-element.126), channel_id=1, source_target_pairs={{0,4},{4,8},{8,12},{12,16},{16,20},{20,24},{24,28},{1,5},{5,9},{9,... | collective-permute-start | bytes 221192 | tf_op jit(solution)/shard_map/ppermute | solution.py:677
  8.3 6.2 %collective-permute-start.2 = (bf16[48,768]{1,0:T(8,128)(2,1)S(1)}, bf16[48,768]{1,0:T(8,128)(2,1)S(1)}, u32[]{:S(2)}, u32[]{:S(2)}) collective-permute-start(bf16[48,768]{1,0:T(8,128)(2,1)S(1)} %get-tuple-element.127), channel_id=1, source_target_pairs={{4,0},{8,4},{12,8},{16,12},{20,16},{24,20},{28,24},{5,1},{9,5},{13... | collective-permute-start | bytes 221192 | tf_op jit(solution)/shard_map/ppermute | solution.py:677
  37.9 8.3 %collective-permute-start.6 = (f32[800,128]{1,0:T(8,128)S(1)}, f32[800,128]{1,0:T(8,128)S(1)}, u32[]{:S(2)}, u32[]{:S(2)}) collective-permute-start(f32[800,128]{1,0:T(8,128)S(1)} %get-tuple-element.146.refs_9_), channel_id=1, source_target_pairs={{0,2},{2,0},{1,3},{3,1},{4,6},{6,4},{5,7},{7,5},{8,10},{10,8},{9,1... | collective-permute-start | bytes 1228808 | tf_op jit(solution)/shard_map/ppermute | solution.py:57
  40.7 13.7 %collective-permute-start.8 = (bf16[768,256]{1,0:T(8,128)(2,1)S(1)}, bf16[768,256]{1,0:T(8,128)(2,1)S(1)}, u32[]{:S(2)}, u32[]{:S(2)}) collective-permute-start(bf16[768,256]{1,0:T(8,128)(2,1)S(1)} %get-tuple-element.156), channel_id=1, source_target_pairs={{0,8},{4,12},{8,0},{12,4},{16,24},{20,28},{24,16},{28,20},{1,9},{5... | collective-permute-start | bytes 1179656 | tf_op jit(solution)/shard_map/ppermute | solution.py:57
  42.3 12.0 %collective-permute-start.9 = (bf16[768,256]{1,0:T(8,128)(2,1)S(1)}, bf16[768,256]{1,0:T(8,128)(2,1)S(1)}, u32[]{:S(2)}, u32[]{:S(2)}) collective-permute-start(bf16[768,256]{1,0:T(8,128)(2,1)S(1)} %get-tuple-element.158), channel_id=1, source_target_pairs={{0,1},{1,0},{2,3},{3,2},{4,5},{5,4},{6,7},{7,6},{8,9},{9,8},{10,11... | collective-permute-start | bytes 1179656 | tf_op jit(solution)/shard_map/ppermute | solution.py:57
  43.8 11.6 %collective-permute-start.10 = (bf16[768,256]{1,0:T(8,128)(2,1)S(1)}, bf16[768,256]{1,0:T(8,128)(2,1)S(1)}, u32[]{:S(2)}, u32[]{:S(2)}) collective-permute-start(bf16[768,256]{1,0:T(8,128)(2,1)S(1)} %get-tuple-element.159), channel_id=1, source_target_pairs={{0,4},{4,0},{8,12},{12,8},{16,20},{20,16},{24,28},{28,24},{1,5},{5... | collective-permute-start | bytes 1179656 | tf_op jit(solution)/shard_map/ppermute | solution.py:57
  56.2 24.5 %collective-permute-start.13 = (bf16[960,512]{1,0:T(8,128)(2,1)S(1)}, bf16[960,512]{1,0:T(8,128)(2,1)S(1)}, u32[]{:S(2)}, u32[]{:S(2)}) collective-permute-start(bf16[960,512]{1,0:T(8,128)(2,1)S(1)} %get-tuple-element.188), channel_id=1, source_target_pairs={{0,1},{1,0},{2,3},{3,2},{4,5},{5,4},{6,7},{7,6},{8,9},{9,8},{10,11... | collective-permute-start | bytes 2949128 | tf_op jit(solution)/shard_map/ppermute | solution.py:57
  61.8 23.5 %collective-permute-start.16 = (bf16[960,512]{1,0:T(8,128)(2,1)S(1)}, bf16[960,512]{1,0:T(8,128)(2,1)S(1)}, u32[]{:S(2)}, u32[]{:S(2)}) collective-permute-start(bf16[960,512]{1,0:T(8,128)(2,1)S(1)} %get-tuple-element.196), channel_id=1, source_target_pairs={{0,4},{4,0},{8,12},{12,8},{16,20},{20,16},{24,28},{28,24},{1,5},{5... | collective-permute-start | bytes 2949128 | tf_op jit(solution)/shard_map/ppermute | solution.py:57
  63.6 31.8 %collective-permute-start.7 = (bf16[768,768]{1,0:T(8,128)(2,1)S(1)}, bf16[768,768]{1,0:T(8,128)(2,1)S(1)}, u32[]{:S(2)}, u32[]{:S(2)}) collective-permute-start(bf16[768,768]{1,0:T(8,128)(2,1)S(1)} %get-tuple-element.152), channel_id=1, source_target_pairs={{0,2},{2,0},{1,3},{3,1},{4,6},{6,4},{5,7},{7,5},{8,10},{10,8},{9,1... | collective-permute-start | bytes 3538952 | tf_op jit(solution)/shard_map/ppermute | solution.py:57
  68.4 24.6 %collective-permute-start.11 = (bf16[960,512]{1,0:T(8,128)(2,1)S(1)}, bf16[960,512]{1,0:T(8,128)(2,1)S(1)}, u32[]{:S(2)}, u32[]{:S(2)}) collective-permute-start(bf16[960,512]{1,0:T(8,128)(2,1)S(1)} %get-tuple-element.170), channel_id=1, source_target_pairs={{0,8},{4,12},{8,0},{12,4},{16,24},{20,28},{24,16},{28,20},{1,9},{5... | collective-permute-start | bytes 2949128 | tf_op jit(solution)/shard_map/ppermute | solution.py:57
  76.5 5.0 %collective-permute-start.12 = (f32[32,768]{1,0:T(8,128)S(1)}, f32[32,768]{1,0:T(8,128)S(1)}, u32[]{:S(2)}, u32[]{:S(2)}) collective-permute-start(f32[32,768]{1,0:T(8,128)S(1)} %constant_dynamic-update-slice_fusion.refs_1_), channel_id=1, source_target_pairs={{0,1},{1,0},{2,3},{3,2},{4,5},{5,4},{6,7},{7,6},{8,9},{9,8},{10,11... | collective-permute-start | bytes 294920 | tf_op jit(solution)/shard_map/ppermute | solution.py:57
  84.7 3.6 %collective-permute-start.15 = (bf16[384,768]{1,0:T(8,128)(2,1)S(1)}, bf16[384,768]{1,0:T(8,128)(2,1)S(1)}, u32[]{:S(2)}, u32[]{:S(2)}) collective-permute-start(bf16[384,768]{1,0:T(8,128)(2,1)S(1)} %get-tuple-element.193), channel_id=1, source_target_pairs={{0,2},{2,0},{1,3},{3,1},{4,6},{6,4},{5,7},{7,5},{8,10},{10,8},{9,1... | collective-permute-start | bytes 1769480 | tf_op jit(solution)/shard_map/ppermute | solution.py:57
  85.2 14.1 %collective-permute-start.18 = (bf16[480,512]{1,0:T(8,128)(2,1)S(1)}, bf16[480,512]{1,0:T(8,128)(2,1)S(1)}, u32[]{:S(2)}, u32[]{:S(2)}) collective-permute-start(bf16[480,512]{1,0:T(8,128)(2,1)S(1)} %get-tuple-element.210), channel_id=1, source_target_pairs={{0,4},{4,0},{8,12},{12,8},{16,20},{20,16},{24,28},{28,24},{1,5},{5... | collective-permute-start | bytes 1474568 | tf_op jit(solution)/shard_map/ppermute | solution.py:57
  87.5 19.2 %collective-permute-start.21 = (bf16[528,512]{1,0:T(8,128)(2,1)S(1)}, bf16[528,512]{1,0:T(8,128)(2,1)S(1)}, u32[]{:S(2)}, u32[]{:S(2)}) collective-permute-start(bf16[528,512]{1,0:T(8,128)(2,1)S(1)} %get-tuple-element.220), channel_id=1, source_target_pairs={{0,8},{4,12},{8,0},{12,4},{16,24},{20,28},{24,16},{28,20},{1,9},{5... | collective-permute-start | bytes 1622024 | tf_op jit(solution)/shard_map/ppermute | solution.py:57
  90.3 6.8 %collective-permute-start.17 = (f32[768,128]{1,0:T(8,128)S(1)}, f32[768,128]{1,0:T(8,128)S(1)}, u32[]{:S(2)}, u32[]{:S(2)}) collective-permute-start(f32[768,128]{1,0:T(8,128)S(1)} %get-tuple-element.205.refs_5_), channel_id=1, source_target_pairs={{0,2},{2,0},{1,3},{3,1},{4,6},{6,4},{5,7},{7,5},{8,10},{10,8},{9,1... | collective-permute-start | bytes 1179656 | tf_op jit(solution)/shard_map/ppermute | solution.py:57
  93.8 13.5 %collective-permute-start.20 = (bf16[480,512]{1,0:T(8,128)(2,1)S(1)}, bf16[480,512]{1,0:T(8,128)(2,1)S(1)}, u32[]{:S(2)}, u32[]{:S(2)}) collective-permute-start(bf16[480,512]{1,0:T(8,128)(2,1)S(1)} %get-tuple-element.217), channel_id=1, source_target_pairs={{0,1},{1,0},{2,3},{3,2},{4,5},{5,4},{6,7},{7,6},{8,9},{9,8},{10,11... | collective-permute-start | bytes 1474568 | tf_op jit(solution)/shard_map/ppermute | solution.py:57
  100.0 13.2 %collective-permute-start.19 = (bf16[240,512]{1,0:T(8,128)(2,1)S(1)}, bf16[240,512]{1,0:T(8,128)(2,1)S(1)}, u32[]{:S(2)}, u32[]{:S(2)}) collective-permute-start(bf16[240,512]{1,0:T(8,128)(2,1)S(1)} %get-tuple-element.214), channel_id=1, source_target_pairs={{0,16},{4,20},{8,24},{12,28},{16,0},{20,4},{24,8},{28,12},{1,17},{... | collective-permute-start | bytes 737288 | tf_op jit(solution)/shard_map/ppermute | solution.py:57
  108.0 9.6 %collective-permute-start.25 = (bf16[240,512]{1,0:T(8,128)(2,1)S(1)}, bf16[240,512]{1,0:T(8,128)(2,1)S(1)}, u32[]{:S(2)}, u32[]{:S(2)}) collective-permute-start(bf16[240,512]{1,0:T(8,128)(2,1)S(1)} %get-tuple-element.235), channel_id=1, source_target_pairs={{0,4},{4,0},{8,12},{12,8},{16,20},{20,16},{24,28},{28,24},{1,5},{5... | collective-permute-start | bytes 737288 | tf_op jit(solution)/shard_map/ppermute | solution.py:57
  108.6 7.1 %collective-permute-start.23 = (bf16[192,512]{1,0:T(8,128)(2,1)S(1)}, bf16[192,512]{1,0:T(8,128)(2,1)S(1)}, u32[]{:S(2)}, u32[]{:S(2)}) collective-permute-start(bf16[192,512]{1,0:T(8,128)(2,1)S(1)} %get-tuple-element.229), channel_id=1, source_target_pairs={{0,1},{1,0},{2,3},{3,2},{4,5},{5,4},{6,7},{7,6},{8,9},{9,8},{10,11... | collective-permute-start | bytes 589832 | tf_op jit(solution)/shard_map/ppermute | solution.py:57
  113.9 6.5 %collective-permute-start.22 = (bf16[96,512]{1,0:T(8,128)(2,1)S(1)}, bf16[96,512]{1,0:T(8,128)(2,1)S(1)}, u32[]{:S(2)}, u32[]{:S(2)}) collective-permute-start(bf16[96,512]{1,0:T(8,128)(2,1)S(1)} %get-tuple-element.226), channel_id=1, source_target_pairs={{0,8},{4,12},{8,0},{12,4},{16,24},{20,28},{24,16},{28,20},{1,9},{5... | collective-permute-start | bytes 294920 | tf_op jit(solution)/shard_map/ppermute | solution.py:57
  116.3 13.3 %collective-permute-start.24 = (bf16[96,768]{1,0:T(8,128)(2,1)S(1)}, bf16[96,768]{1,0:T(8,128)(2,1)S(1)}, u32[]{:S(2)}, u32[]{:S(2)}) collective-permute-start(bf16[96,768]{1,0:T(8,128)(2,1)S(1)} %get-tuple-element.232), channel_id=1, source_target_pairs={{0,16},{4,20},{8,24},{12,28},{16,0},{20,4},{24,8},{28,12},{1,17},{... | collective-permute-start | bytes 442376 | tf_op jit(solution)/shard_map/ppermute | solution.py:57
  118.7 14.0 %collective-permute-start.26 = (bf16[128,768]{1,0:T(8,128)(2,1)S(1)}, bf16[128,768]{1,0:T(8,128)(2,1)S(1)}, u32[]{:S(2)}, u32[]{:S(2)}) collective-permute-start(bf16[128,768]{1,0:T(8,128)(2,1)S(1)} %get-tuple-element.238), channel_id=1, source_target_pairs={{0,16},{4,20},{8,24},{12,28},{16,0},{20,4},{24,8},{28,12},{1,17},{... | collective-permute-start | bytes 589832 | tf_op jit(solution)/shard_map/ppermute | solution.py:57
  (6 other events, 21.9 us)

commit v8 on v7

--- a/solution.py
+++ b/solution.py
@@ -425,7 +425,7 @@
     mean = (first[:, :1] + second[:, :1]) / width
     half = LANES // 2
     square = (first[:, half : half + 1] + second[:, half : half + 1]) / width
-    return mean, lax.rsqrt(square - mean * mean + epsilon)
+    return mean, lax.rsqrt(jnp.maximum(square - mean * mean, 0.0) + epsilon)
 
 
 def swish(info, conv, pull, ends, own, other, swished, dswish, stats):

time: 135 us -> 135 us (level)
  no operation moved by 1% of the time
where the time goes in v8:
time: 135 us
  Pallas kernels  74 us (55%)
  starting transfers between devices  29.7 us (22%)
  waiting for transfers between devices  27.1 us (20%)
  between operations  1.73 us (1%)
  other arithmetic  1.69 us (1%)
    pallas_call x35, Pallas kernels, run(): pl.pallas_call(body, in_specs=[SMEM] + [space] * near + [HBM] * len(far)...  74 us
    ppermute x25, waiting for transfers between devices, swap(): return lax.ppermute(value, axis, [(i, i ^ 1 << bit) for i in range(size)])  24.7 us
    ppermute x25, starting transfers between devices, swap(): return lax.ppermute(value, axis, [(i, i ^ 1 << bit) for i in range(size)])  23.6 us
    ppermute x1, starting transfers between devices, shards(): lax.ppermute(last, 'seq', up)  4.85 us
  transfers between devices with their start and end apart: 27, of which 8 were waited for; matrix products, arithmetic and copies ran while one was open for 0% of the time, Pallas kernels for 42%

profile of v8, /device:TPU:0, one launch (start us, length us, event | category | flops | bytes accessed | tf_op | source)
XLA Modules:
  0.0 135.1 jit_solution(2349820961211916714)
XLA Ops:
  3.4 4.9 %collective-permute-start.1 = (bf16[48,768]{1,0:T(8,128)(2,1)S(1)}, bf16[48,768]{1,0:T(8,128)(2,1)S(1)}, u32[]{:S(2)}, u32[]{:S(2)}) collective-permute-start(bf16[48,768]{1,0:T(8,128)(2,1)S(1)} %get-tuple-element.126), channel_id=1, source_target_pairs={{0,4},{4,8},{8,12},{12,16},{16,20},{20,24},{24,28},{1,5},{5,9},{9,... | collective-permute-start | bytes 221192 | tf_op jit(solution)/shard_map/ppermute | solution.py:677
  9.6 2.5 %prepare.1 = (bf16[768,768]{1,0:T(8,128)(2,1)S(1)}, bf16[768,1536]{1,0:T(8,128)(2,1)S(1)}, f32[8,128]{1,0:T(8,128)S(1)}) custom-call(s32[8]{0:T(128)S(1)} %stack.27.refs_0_, bf16[768,768]{1,0:T(8,128)(2,1)} %bitcast.18, bf16[768,1536]{1,0:T(8,128)(2,1)} %refs_2_.2, f32[8,128]{1,0:T(8,128)S(1)} %get-tuple-element.123.refs_3_), custom_call_target="tpu_custom_call" | custom-call | flops 1024 | bytes 1024 | tf_op jit(solution)/shard_map/prepare/pallas_call | solution.py:38
  12.1 2.4 %collective-permute-done.2.refs_2_ = bf16[48,768]{1,0:T(8,128)(2,1)S(1)} collective-permute-done((bf16[48,768]{1,0:T(8,128)(2,1)S(1)}, bf16[48,768]{1,0:T(8,128)(2,1)S(1)}, u32[]{:S(2)}, u32[]{:S(2)}) %collective-permute-start.2) | collective-permute-done | bytes 73760 | tf_op jit(solution)/shard_map/ppermute | solution.py:677
  15.2 3.4 %upstream.1 = (bf16[768,1536]{1,0:T(8,128)(2,1)S(1)}, bf16[768,768]{1,0:T(8,128)(2,1)S(1)}, bf16[768,768]{1,0:T(8,128)(2,1)S(1)}, bf16[1536,768]{1,0:T(8,128)(2,...) custom-call(s32[8]{0:T(128)S(1)} %stack.27.refs_0_, bf16[768,768]{1,0:T(8,128)(2,1)S(1)} %get-tuple-element.124.refs_1_, ...), custom_call_target="tpu_custom_call" | custom-call | flops 1024 | bytes 1024 | tf_op jit(solution)/shard_map/upstream/pallas_call | solution.py:38
  18.5 6.5 %front.1 = (bf16[832,1536]{1,0:T(8,128)(2,1)S(1)}, f32[768,128]{1,0:T(8,128)S(1)}, bf16[832,768]{1,0:T(8,128)(2,1)S(1)}, bf16[768,768]{1,0:T(8,128)(2,1)S(1)}, b...) custom-call(s32[8]{0:T(128)S(1)} %stack.27.refs_0_, bf16[768,768]{1,0:T(8,128)(2,1)S(1)} %get-tuple-element.130.refs_1_, ...), custom_call_target="tpu_custom_call" | custom-call | flops 1024 | bytes 1024 | tf_op jit(solution)/shard_map/front/pallas_call | solution.py:38
  25.1 6.7 %depthwise.1 = (f32[800,768]{1,0:T(8,128)S(1)}, f32[800,128]{1,0:T(8,128)S(1)}, f32[8,128]{1,0:T(8,128)S(1)}) custom-call(s32[8]{0:T(128)S(1)} %stack.27.refs_0_, bf16[832,768]{1,0:T(8,128)(2,1)S(1)} %get-tuple-element.135.refs_1_.refs_2_, bf16[31,768]{1,0:T(8,128)(2,1)S(1)} %copy-done.2), custom_call_target="tpu_custom_call" | custom-call | flops 1024 | bytes 1024 | tf_op jit(solution)/shard_map/depthwise/pallas_call | solution.py:38
  34.1 3.9 %swish.1 = (bf16[768,768]{1,0:T(8,128)(2,1)S(1)}, f32[800,768]{1,0:T(8,128)S(1)}, f32[800,128]{1,0:T(8,128)S(1)}, f32[8,128]{1,0:T(8,128)}) custom-call(s32[8]{0:T(128)S(1)} %stack.27.refs_0_, f32[800,768]{1,0:T(8,128)S(1)} %get-tuple-element.136.refs_1_.refs_2_, bf16[768,768]{1,0:T(8,128)(2,1)S(1)} %get-tuple-element.137.refs_2_, ...), custom_call_target="tpu_custom_call" | custom-call | flops 1024 | bytes 1024 | tf_op jit(solution)/shard_map/swish/pallas_call | solution.py:38
  38.0 2.7 %out_terms.1 = (bf16[768,256]{1,0:T(8,128)(2,1)S(1)}, bf16[768,256]{1,0:T(8,128)(2,1)S(1)}, bf16[768,256]{1,0:T(8,128)(2,1)S(1)}, bf16[768,256]{1,0:T(8,128)(2,1...) custom-call(s32[8]{0:T(128)S(1)} %stack.27.refs_0_, ...), custom_call_target="tpu_custom_call" | custom-call | flops 1024 | bytes 1024 | tf_op jit(solution)/shard_map/out_terms/pallas_call | solution.py:38
  43.8 2.4 %collective-permute-start.10 = (bf16[768,256]{1,0:T(8,128)(2,1)S(1)}, bf16[768,256]{1,0:T(8,128)(2,1)S(1)}, u32[]{:S(2)}, u32[]{:S(2)}) collective-permute-start(bf16[768,256]{1,0:T(8,128)(2,1)S(1)} %get-tuple-element.159), channel_id=1, source_target_pairs={{0,4},{4,0},{8,12},{12,8},{16,20},{20,16},{24,28},{28,24},{1,5},{5... | collective-permute-start | bytes 1179656 | tf_op jit(solution)/shard_map/ppermute | solution.py:57
  46.3 4.8 %back.3 = (bf16[800,256]{1,0:T(8,128)(2,1)S(1)}, bf16[768,512]{1,0:T(8,128)(2,1)S(1)}, bf16[1536,512]{1,0:T(8,128)(2,1)S(1)}, f32[3,800,128]{2,1,0:T(8,128)S(1)}, f32[8,128]{1,0:T(8,128)S(1)}) custom-call(s32[8]{0:T(128)S(1)} %stack.27.refs_0_, f32[800,768]{1,0:T(8,128)S(1)} %get-tuple-element.142.refs_1_, ...), custom_call_target="tpu_custom_call" | custom-call | flops 1024 | bytes 1024 | tf_op jit(solution)/shard_map/back/pallas_call | solution.py:38
  56.8 4.2 %back.4 = (bf16[800,256]{1,0:T(8,128)(2,1)S(1)}, bf16[768,512]{1,0:T(8,128)(2,1)S(1)}, bf16[1536,512]{1,0:T(8,128)(2,1)S(1)}, f32[8,128]{1,0:T(8,128)S(1)}) custom-call(s32[8]{0:T(128)S(1)} %stack.27.refs_0_, f32[800,768]{1,0:T(8,128)S(1)} %get-tuple-element.142.refs_1_, f32[800,768]{1,0:T(8,128)S(1)} %get-tuple-element.136.refs_1_.refs_2_, ...), custom_call_target="tpu_custom_call" | custom-call | flops 1024 | bytes 1024 | tf_op jit(solution)/shard_map/back/pallas_call | solution.py:38
  63.6 4.1 %back.5 = (bf16[800,256]{1,0:T(8,128)(2,1)S(1)}, bf16[768,512]{1,0:T(8,128)(2,1)S(1)}, bf16[1536,512]{1,0:T(8,128)(2,1)S(1)}, f32[8,128]{1,0:T(8,128)S(1)}) custom-call(s32[8]{0:T(128)S(1)} %stack.27.refs_0_, f32[800,768]{1,0:T(8,128)S(1)} %get-tuple-element.142.refs_1_, f32[800,768]{1,0:T(8,128)S(1)} %get-tuple-element.136.refs_1_.refs_2_, ...), custom_call_target="tpu_custom_call" | custom-call | flops 1024 | bytes 1024 | tf_op jit(solution)/shard_map/back/pallas_call | solution.py:38
  68.9 2.5 %taps_sums.3 = (f32[32,256]{1,0:T(8,128)S(1)}, f32[8,128]{1,0:T(8,128)S(1)}) custom-call(s32[8]{0:T(128)S(1)} %stack.27.refs_0_, bf16[800,256]{1,0:T(8,128)(2,1)S(1)} %get-tuple-element.176.refs_1_, bf16[832,768]{1,0:T(8,128)(2,1)S(1)} %get-tuple-element.135.refs_1_.refs_2_, f32[8,128]{1,0:T(8,128)S(1)} %get-tuple-element.177.refs_3_), custom_call_target="tpu_custom_call" | custom-call | flops 1024 | bytes 1024 | tf_op jit(solution)/shard_map/taps_sums/pallas_call | solution.py:38
  71.5 2.5 %taps_sums.4 = (f32[32,256]{1,0:T(8,128)S(1)}, f32[8,128]{1,0:T(8,128)S(1)}) custom-call(s32[8]{0:T(128)S(1)} %stack.27.refs_0_, bf16[800,256]{1,0:T(8,128)(2,1)S(1)} %get-tuple-element.175.refs_1_, bf16[832,768]{1,0:T(8,128)(2,1)S(1)} %get-tuple-element.135.refs_1_.refs_2_, f32[8,128]{1,0:T(8,128)S(1)} %get-tuple-element.178.refs_3_), custom_call_target="tpu_custom_call" | custom-call | flops 1024 | bytes 1024 | tf_op jit(solution)/shard_map/taps_sums/pallas_call | solution.py:38
  74.0 2.5 %taps_sums.5 = (f32[32,256]{1,0:T(8,128)S(1)}, f32[8,128]{1,0:T(8,128)S(1)}) custom-call(s32[8]{0:T(128)S(1)} %stack.27.refs_0_, bf16[800,256]{1,0:T(8,128)(2,1)S(1)} %get-tuple-element.174.refs_1_, bf16[832,768]{1,0:T(8,128)(2,1)S(1)} %get-tuple-element.135.refs_1_.refs_2_, f32[8,128]{1,0:T(8,128)S(1)} %get-tuple-element.179.refs_3_), custom_call_target="tpu_custom_call" | custom-call | flops 1024 | bytes 1024 | tf_op jit(solution)/shard_map/taps_sums/pallas_call | solution.py:38
  78.1 2.6 %norm_half.2 = (f32[384,768]{1,0:T(8,128)S(1)}, f32[384,768]{1,0:T(8,128)S(1)}, f32[8,128]{1,0:T(8,128)S(1)}) custom-call(s32[8]{0:T(128)S(1)} %stack.27.refs_0_, bf16[768,512]{1,0:T(8,128)(2,1)S(1)} %get-tuple-element.171.refs_1_, bf16[768,512]{1,0:T(8,128)(2,1)S(1)} %get-tuple-element.172.refs_2_, bf16[768,512]{1,0:T(8,128)(2,1)S(1)} %get-tuple-element.173.refs_3_, ...), custom_call_target="tpu_custom_call" | custom-call | flops 1024 | bytes 1024 | tf_op jit(solution)/shard_map/norm_half/pallas_call | solution.py:38
  82.1 2.6 %norm_half.3 = (bf16[384,768]{1,0:T(8,128)(2,1)S(1)}, bf16[384,768]{1,0:T(8,128)(2,1)S(1)}, f32[8,128]{1,0:T(8,128)S(1)}) custom-call(s32[8]{0:T(128)S(1)} %stack.27.refs_0_, bf16[768,512]{1,0:T(8,128)(2,1)S(1)} %get-tuple-element.171.refs_1_, bf16[768,512]{1,0:T(8,128)(2,1)S(1)} %get-tuple-element.172.refs_2_, ...), custom_call_target="tpu_custom_call" | custom-call | flops 1024 | bytes 1024 | tf_op jit(solution)/shard_map/norm_half/pallas_call | solution.py:38
  90.4 2.7 %collective-permute-done.11.refs_3_ = bf16[960,512]{1,0:T(8,128)(2,1)S(1)} collective-permute-done((bf16[960,512]{1,0:T(8,128)(2,1)S(1)}, bf16[960,512]{1,0:T(8,128)(2,1)S(1)}, u32[]{:S(2)}, u32[]{:S(2)}) %collective-permute-start.11) | collective-permute-done | bytes 983072 | tf_op jit(solution)/shard_map/ppermute | solution.py:57
  97.1 2.2 %input_rows.1 = (bf16[768,768]{1,0:T(8,128)(2,1)}, f32[8,128]{1,0:T(8,128)S(1)}) custom-call(s32[8]{0:T(128)S(1)} %stack.27.refs_0_, bf16[768,768]{1,0:T(8,128)(2,1)S(1)} %bitcast.19, f32[768,768]{1,0:T(8,128)S(1)} %get-tuple-element.203.refs_2_, bf16[832,1536]{1,0:T(8,128)(2,1)S(1)} %get-tuple-element.145.refs_6_.refs_5_.refs_3_, ...), custom_call_target="tpu_custom_call" | custom-call | flops 1024 | bytes 1024 | tf_op jit(solution)/shard_map/input_rows/pallas_call | solution.py:38
  101.8 4.8 %collective-permute-done.21.refs_3_ = bf16[528,512]{1,0:T(8,128)(2,1)S(1)} collective-permute-done((bf16[528,512]{1,0:T(8,128)(2,1)S(1)}, bf16[528,512]{1,0:T(8,128)(2,1)S(1)}, u32[]{:S(2)}, u32[]{:S(2)}) %collective-permute-start.21) | collective-permute-done | bytes 540704 | tf_op jit(solution)/shard_map/ppermute | solution.py:57
  108.6 2.6 %collective-permute-start.23 = (bf16[192,512]{1,0:T(8,128)(2,1)S(1)}, bf16[192,512]{1,0:T(8,128)(2,1)S(1)}, u32[]{:S(2)}, u32[]{:S(2)}) collective-permute-start(bf16[192,512]{1,0:T(8,128)(2,1)S(1)} %get-tuple-element.229), channel_id=1, source_target_pairs={{0,1},{1,0},{2,3},{3,2},{4,5},{5,4},{6,7},{7,6},{8,9},{9,8},{10,11... | collective-permute-start | bytes 589832 | tf_op jit(solution)/shard_map/ppermute | solution.py:57
  111.1 2.1 %collective-permute-done.19.refs_3_ = bf16[240,512]{1,0:T(8,128)(2,1)S(1)} collective-permute-done((bf16[240,512]{1,0:T(8,128)(2,1)S(1)}, bf16[240,512]{1,0:T(8,128)(2,1)S(1)}, u32[]{:S(2)}, u32[]{:S(2)}) %collective-permute-start.19) | collective-permute-done | bytes 245792 | tf_op jit(solution)/shard_map/ppermute | solution.py:57
  120.4 9.1 %collective-permute-done.24 = bf16[96,768]{1,0:T(8,128)(2,1)S(1)} collective-permute-done((bf16[96,768]{1,0:T(8,128)(2,1)S(1)}, bf16[96,768]{1,0:T(8,128)(2,1)S(1)}, u32[]{:S(2)}, u32[]{:S(2)}) %collective-permute-start.24) | collective-permute-done | bytes 147488 | tf_op jit(solution)/shard_map/ppermute | solution.py:57
  129.6 3.2 %collective-permute-done.26 = bf16[128,768]{1,0:T(8,128)(2,1)S(1)} collective-permute-done((bf16[128,768]{1,0:T(8,128)(2,1)S(1)}, bf16[128,768]{1,0:T(8,128)(2,1)S(1)}, u32[]{:S(2)}, u32[]{:S(2)}) %collective-permute-start.26) | collective-permute-done | bytes 196640 | tf_op jit(solution)/shard_map/ppermute | solution.py:57
  (84 shorter events, 45.6 us)
Async XLA Ops:
  0.6 14.5 %collective-permute-start = (bf16[768,768]{1,0:T(8,128)(2,1)}, bf16[768,768]{1,0:T(8,128)(2,1)S(1)}, u32[]{:S(2)}, u32[]{:S(2)}) collective-permute-start(bf16[768,768]{1,0:T(8,128)(2,1)} %bitcast.16), channel_id=1, source_target_pairs={{0,2},{2,0},{1,3},{3,1},{4,6},{6,4},{5,7},{7,5},{8,10},{10,8},{9,1... | collective-permute-start | bytes 3538952 | tf_op jit(solution)/shard_map/ppermute | solution.py:57
  1.1 17.4 %collective-permute-start.3 = (bf16[768,768]{1,0:T(8,128)(2,1)}, bf16[768,768]{1,0:T(8,128)(2,1)S(1)}, u32[]{:S(2)}, u32[]{:S(2)}) collective-permute-start(bf16[768,768]{1,0:T(8,128)(2,1)} %bitcast.12), channel_id=1, source_target_pairs={{0,2},{2,0},{1,3},{3,1},{4,6},{6,4},{5,7},{7,5},{8,10},{10,8},{9,1... | collective-permute-start | bytes 3538952 | tf_op jit(solution)/shard_map/ppermute | solution.py:57
  3.4 8.7 %collective-permute-start.1 = (bf16[48,768]{1,0:T(8,128)(2,1)S(1)}, bf16[48,768]{1,0:T(8,128)(2,1)S(1)}, u32[]{:S(2)}, u32[]{:S(2)}) collective-permute-start(bf16[48,768]{1,0:T(8,128)(2,1)S(1)} %get-tuple-element.126), channel_id=1, source_target_pairs={{0,4},{4,8},{8,12},{12,16},{16,20},{20,24},{24,28},{1,5},{5,9},{9,... | collective-permute-start | bytes 221192 | tf_op jit(solution)/shard_map/ppermute | solution.py:677
  8.3 6.2 %collective-permute-start.2 = (bf16[48,768]{1,0:T(8,128)(2,1)S(1)}, bf16[48,768]{1,0:T(8,128)(2,1)S(1)}, u32[]{:S(2)}, u32[]{:S(2)}) collective-permute-start(bf16[48,768]{1,0:T(8,128)(2,1)S(1)} %get-tuple-element.127), channel_id=1, source_target_pairs={{4,0},{8,4},{12,8},{16,12},{20,16},{24,20},{28,24},{5,1},{9,5},{13... | collective-permute-start | bytes 221192 | tf_op jit(solution)/shard_map/ppermute | solution.py:677
  37.9 8.3 %collective-permute-start.6 = (f32[800,128]{1,0:T(8,128)S(1)}, f32[800,128]{1,0:T(8,128)S(1)}, u32[]{:S(2)}, u32[]{:S(2)}) collective-permute-start(f32[800,128]{1,0:T(8,128)S(1)} %get-tuple-element.146.refs_9_), channel_id=1, source_target_pairs={{0,2},{2,0},{1,3},{3,1},{4,6},{6,4},{5,7},{7,5},{8,10},{10,8},{9,1... | collective-permute-start | bytes 1228808 | tf_op jit(solution)/shard_map/ppermute | solution.py:57
  40.7 13.6 %collective-permute-start.8 = (bf16[768,256]{1,0:T(8,128)(2,1)S(1)}, bf16[768,256]{1,0:T(8,128)(2,1)S(1)}, u32[]{:S(2)}, u32[]{:S(2)}) collective-permute-start(bf16[768,256]{1,0:T(8,128)(2,1)S(1)} %get-tuple-element.156), channel_id=1, source_target_pairs={{0,8},{4,12},{8,0},{12,4},{16,24},{20,28},{24,16},{28,20},{1,9},{5... | collective-permute-start | bytes 1179656 | tf_op jit(solution)/shard_map/ppermute | solution.py:57
  42.3 12.0 %collective-permute-start.9 = (bf16[768,256]{1,0:T(8,128)(2,1)S(1)}, bf16[768,256]{1,0:T(8,128)(2,1)S(1)}, u32[]{:S(2)}, u32[]{:S(2)}) collective-permute-start(bf16[768,256]{1,0:T(8,128)(2,1)S(1)} %get-tuple-element.158), channel_id=1, source_target_pairs={{0,1},{1,0},{2,3},{3,2},{4,5},{5,4},{6,7},{7,6},{8,9},{9,8},{10,11... | collective-permute-start | bytes 1179656 | tf_op jit(solution)/shard_map/ppermute | solution.py:57
  43.8 11.6 %collective-permute-start.10 = (bf16[768,256]{1,0:T(8,128)(2,1)S(1)}, bf16[768,256]{1,0:T(8,128)(2,1)S(1)}, u32[]{:S(2)}, u32[]{:S(2)}) collective-permute-start(bf16[768,256]{1,0:T(8,128)(2,1)S(1)} %get-tuple-element.159), channel_id=1, source_target_pairs={{0,4},{4,0},{8,12},{12,8},{16,20},{20,16},{24,28},{28,24},{1,5},{5... | collective-permute-start | bytes 1179656 | tf_op jit(solution)/shard_map/ppermute | solution.py:57
  56.2 24.5 %collective-permute-start.13 = (bf16[960,512]{1,0:T(8,128)(2,1)S(1)}, bf16[960,512]{1,0:T(8,128)(2,1)S(1)}, u32[]{:S(2)}, u32[]{:S(2)}) collective-permute-start(bf16[960,512]{1,0:T(8,128)(2,1)S(1)} %get-tuple-element.188), channel_id=1, source_target_pairs={{0,1},{1,0},{2,3},{3,2},{4,5},{5,4},{6,7},{7,6},{8,9},{9,8},{10,11... | collective-permute-start | bytes 2949128 | tf_op jit(solution)/shard_map/ppermute | solution.py:57
  61.8 23.5 %collective-permute-start.16 = (bf16[960,512]{1,0:T(8,128)(2,1)S(1)}, bf16[960,512]{1,0:T(8,128)(2,1)S(1)}, u32[]{:S(2)}, u32[]{:S(2)}) collective-permute-start(bf16[960,512]{1,0:T(8,128)(2,1)S(1)} %get-tuple-element.196), channel_id=1, source_target_pairs={{0,4},{4,0},{8,12},{12,8},{16,20},{20,16},{24,28},{28,24},{1,5},{5... | collective-permute-start | bytes 2949128 | tf_op jit(solution)/shard_map/ppermute | solution.py:57
  63.6 31.8 %collective-permute-start.7 = (bf16[768,768]{1,0:T(8,128)(2,1)S(1)}, bf16[768,768]{1,0:T(8,128)(2,1)S(1)}, u32[]{:S(2)}, u32[]{:S(2)}) collective-permute-start(bf16[768,768]{1,0:T(8,128)(2,1)S(1)} %get-tuple-element.152), channel_id=1, source_target_pairs={{0,2},{2,0},{1,3},{3,1},{4,6},{6,4},{5,7},{7,5},{8,10},{10,8},{9,1... | collective-permute-start | bytes 3538952 | tf_op jit(solution)/shard_map/ppermute | solution.py:57
  68.4 24.6 %collective-permute-start.11 = (bf16[960,512]{1,0:T(8,128)(2,1)S(1)}, bf16[960,512]{1,0:T(8,128)(2,1)S(1)}, u32[]{:S(2)}, u32[]{:S(2)}) collective-permute-start(bf16[960,512]{1,0:T(8,128)(2,1)S(1)} %get-tuple-element.170), channel_id=1, source_target_pairs={{0,8},{4,12},{8,0},{12,4},{16,24},{20,28},{24,16},{28,20},{1,9},{5... | collective-permute-start | bytes 2949128 | tf_op jit(solution)/shard_map/ppermute | solution.py:57
  76.5 5.0 %collective-permute-start.12 = (f32[32,768]{1,0:T(8,128)S(1)}, f32[32,768]{1,0:T(8,128)S(1)}, u32[]{:S(2)}, u32[]{:S(2)}) collective-permute-start(f32[32,768]{1,0:T(8,128)S(1)} %constant_dynamic-update-slice_fusion.refs_1_), channel_id=1, source_target_pairs={{0,1},{1,0},{2,3},{3,2},{4,5},{5,4},{6,7},{7,6},{8,9},{9,8},{10,11... | collective-permute-start | bytes 294920 | tf_op jit(solution)/shard_map/ppermute | solution.py:57
  84.7 3.6 %collective-permute-start.15 = (bf16[384,768]{1,0:T(8,128)(2,1)S(1)}, bf16[384,768]{1,0:T(8,128)(2,1)S(1)}, u32[]{:S(2)}, u32[]{:S(2)}) collective-permute-start(bf16[384,768]{1,0:T(8,128)(2,1)S(1)} %get-tuple-element.193), channel_id=1, source_target_pairs={{0,2},{2,0},{1,3},{3,1},{4,6},{6,4},{5,7},{7,5},{8,10},{10,8},{9,1... | collective-permute-start | bytes 1769480 | tf_op jit(solution)/shard_map/ppermute | solution.py:57
  85.2 14.1 %collective-permute-start.18 = (bf16[480,512]{1,0:T(8,128)(2,1)S(1)}, bf16[480,512]{1,0:T(8,128)(2,1)S(1)}, u32[]{:S(2)}, u32[]{:S(2)}) collective-permute-start(bf16[480,512]{1,0:T(8,128)(2,1)S(1)} %get-tuple-element.210), channel_id=1, source_target_pairs={{0,4},{4,0},{8,12},{12,8},{16,20},{20,16},{24,28},{28,24},{1,5},{5... | collective-permute-start | bytes 1474568 | tf_op jit(solution)/shard_map/ppermute | solution.py:57
  87.5 19.2 %collective-permute-start.21 = (bf16[528,512]{1,0:T(8,128)(2,1)S(1)}, bf16[528,512]{1,0:T(8,128)(2,1)S(1)}, u32[]{:S(2)}, u32[]{:S(2)}) collective-permute-start(bf16[528,512]{1,0:T(8,128)(2,1)S(1)} %get-tuple-element.220), channel_id=1, source_target_pairs={{0,8},{4,12},{8,0},{12,4},{16,24},{20,28},{24,16},{28,20},{1,9},{5... | collective-permute-start | bytes 1622024 | tf_op jit(solution)/shard_map/ppermute | solution.py:57
  90.3 6.8 %collective-permute-start.17 = (f32[768,128]{1,0:T(8,128)S(1)}, f32[768,128]{1,0:T(8,128)S(1)}, u32[]{:S(2)}, u32[]{:S(2)}) collective-permute-start(f32[768,128]{1,0:T(8,128)S(1)} %get-tuple-element.205.refs_5_), channel_id=1, source_target_pairs={{0,2},{2,0},{1,3},{3,1},{4,6},{6,4},{5,7},{7,5},{8,10},{10,8},{9,1... | collective-permute-start | bytes 1179656 | tf_op jit(solution)/shard_map/ppermute | solution.py:57
  93.9 13.5 %collective-permute-start.20 = (bf16[480,512]{1,0:T(8,128)(2,1)S(1)}, bf16[480,512]{1,0:T(8,128)(2,1)S(1)}, u32[]{:S(2)}, u32[]{:S(2)}) collective-permute-start(bf16[480,512]{1,0:T(8,128)(2,1)S(1)} %get-tuple-element.217), channel_id=1, source_target_pairs={{0,1},{1,0},{2,3},{3,2},{4,5},{5,4},{6,7},{7,6},{8,9},{9,8},{10,11... | collective-permute-start | bytes 1474568 | tf_op jit(solution)/shard_map/ppermute | solution.py:57
  100.0 13.2 %collective-permute-start.19 = (bf16[240,512]{1,0:T(8,128)(2,1)S(1)}, bf16[240,512]{1,0:T(8,128)(2,1)S(1)}, u32[]{:S(2)}, u32[]{:S(2)}) collective-permute-start(bf16[240,512]{1,0:T(8,128)(2,1)S(1)} %get-tuple-element.214), channel_id=1, source_target_pairs={{0,16},{4,20},{8,24},{12,28},{16,0},{20,4},{24,8},{28,12},{1,17},{... | collective-permute-start | bytes 737288 | tf_op jit(solution)/shard_map/ppermute | solution.py:57
  108.0 9.6 %collective-permute-start.25 = (bf16[240,512]{1,0:T(8,128)(2,1)S(1)}, bf16[240,512]{1,0:T(8,128)(2,1)S(1)}, u32[]{:S(2)}, u32[]{:S(2)}) collective-permute-start(bf16[240,512]{1,0:T(8,128)(2,1)S(1)} %get-tuple-element.235), channel_id=1, source_target_pairs={{0,4},{4,0},{8,12},{12,8},{16,20},{20,16},{24,28},{28,24},{1,5},{5... | collective-permute-start | bytes 737288 | tf_op jit(solution)/shard_map/ppermute | solution.py:57
  108.6 7.1 %collective-permute-start.23 = (bf16[192,512]{1,0:T(8,128)(2,1)S(1)}, bf16[192,512]{1,0:T(8,128)(2,1)S(1)}, u32[]{:S(2)}, u32[]{:S(2)}) collective-permute-start(bf16[192,512]{1,0:T(8,128)(2,1)S(1)} %get-tuple-element.229), channel_id=1, source_target_pairs={{0,1},{1,0},{2,3},{3,2},{4,5},{5,4},{6,7},{7,6},{8,9},{9,8},{10,11... | collective-permute-start | bytes 589832 | tf_op jit(solution)/shard_map/ppermute | solution.py:57
  113.9 6.5 %collective-permute-start.22 = (bf16[96,512]{1,0:T(8,128)(2,1)S(1)}, bf16[96,512]{1,0:T(8,128)(2,1)S(1)}, u32[]{:S(2)}, u32[]{:S(2)}) collective-permute-start(bf16[96,512]{1,0:T(8,128)(2,1)S(1)} %get-tuple-element.226), channel_id=1, source_target_pairs={{0,8},{4,12},{8,0},{12,4},{16,24},{20,28},{24,16},{28,20},{1,9},{5... | collective-permute-start | bytes 294920 | tf_op jit(solution)/shard_map/ppermute | solution.py:57
  116.3 13.3 %collective-permute-start.24 = (bf16[96,768]{1,0:T(8,128)(2,1)S(1)}, bf16[96,768]{1,0:T(8,128)(2,1)S(1)}, u32[]{:S(2)}, u32[]{:S(2)}) collective-permute-start(bf16[96,768]{1,0:T(8,128)(2,1)S(1)} %get-tuple-element.232), channel_id=1, source_target_pairs={{0,16},{4,20},{8,24},{12,28},{16,0},{20,4},{24,8},{28,12},{1,17},{... | collective-permute-start | bytes 442376 | tf_op jit(solution)/shard_map/ppermute | solution.py:57
  118.7 14.0 %collective-permute-start.26 = (bf16[128,768]{1,0:T(8,128)(2,1)S(1)}, bf16[128,768]{1,0:T(8,128)(2,1)S(1)}, u32[]{:S(2)}, u32[]{:S(2)}) collective-permute-start(bf16[128,768]{1,0:T(8,128)(2,1)S(1)} %get-tuple-element.238), channel_id=1, source_target_pairs={{0,16},{4,20},{8,24},{12,28},{16,0},{20,4},{24,8},{28,12},{1,17},{... | collective-permute-start | bytes 589832 | tf_op jit(solution)/shard_map/ppermute | solution.py:57
  (6 other events, 21.9 us)
